TPU v7x, 32 devices: a whole 2x2x4 slice. The times are simulated.
32 devices in a mesh: tm: 8 (over y, x, core), tile: 4 (over z).
Axes of the slice: x: 2, y: 2, z: 4, core: 2. Of those that a mesh axis runs over, the one named last changes fastest.
Arguments:
- queries: bfloat16 [4096, 1536], P(('tm', 'tile')), may hold values from -16 to 16
- keys: bfloat16 [4096, 1536], P(('tm', 'tile')), may hold values from -16 to 16
- values: bfloat16 [4096, 1536], P(('tm', 'tile')), may hold values from -6 to 6
- grad_out: bfloat16 [4096, 1536], P(('tm', 'tile')), may hold values from -6 to 6
- span_of_group: int32 [8], replicated, may hold values from 0 to 7, each once
- noise_level: int32 [8], replicated, may hold values from 0 to 999
- next_live: int32 [32], replicated, may hold values 0 or 1
- level_bias: float32 [1000, 12], replicated, may hold values from -2 to 2
Outputs:
- attended: bfloat16 [4096, 1536], P(('tm', 'tile'))
- grad_queries: bfloat16 [4096, 1536], P(('tm', 'tile'))
- grad_keys: bfloat16 [4096, 1536], P(('tm', 'tile'))
- grad_values: bfloat16 [4096, 1536], P(('tm', 'tile'))
Inputs may be any that keep to these rules, and one draw needn't show every extreme that they name: span_of_group is a permutation of 0 to 7.
All inputs are finite; a program needn't handle non-finite values.
Results may differ from a plain program's by a relative error of at most 0.019.
Values may be sent and summed in bfloat16 or wider, within the bound.
No kernel may reach another device: no remote copies, remote signals or barrier semaphores. Data moves between devices by JAX's collectives and lax.ppermute only.
A program may use at most 256 MiB of HBM per device.

v0:
```python
import functools
import math

import jax
import jax.numpy as jnp
from jax import lax
from jax.experimental import pallas as pl
from jax.experimental.pallas import tpu as pltpu
from jax.sharding import PartitionSpec as P

VMEM = pltpu.VMEM
SMEM = pltpu.SMEM
BF16 = jnp.bfloat16
F32 = jnp.float32
NT = (((1,), (1,)), ((), ()))
LOG2E = 1.4426950408889634
DEAD = -1e30


def params(mib):
    return pltpu.CompilerParams(vmem_limit_bytes=mib * 1024 * 1024)


def whole(space):
    return pl.BlockSpec(memory_space=space)


def shard_count(heads, groups):
    count = 1
    while heads % (2 * count) == 0 and groups % (2 * count) == 0:
        count *= 2
    return count


def fold(op, x):
    return op(x.reshape(x.shape[0] // 8, 8, x.shape[1]), axis=0)


def pack_kernel(z, pos_ref, *refs):
    sources, refs = refs[:4], refs[4:]
    outs, (pair, early, held, sems) = refs[: z.shards], refs[z.shards :]
    half, cols = z.tok // 2, z.own_heads * z.width
    copies = []
    for i, src in enumerate(sources):
        for j in range(2):
            rows = pl.ds(j * half, half)
            copy = pltpu.make_async_copy(src.at[rows], held.at[i, rows], sems.at[i, j])
            copy.start()
            copies.append(copy)
    for i in range(4):
        copies[2 * i].wait()
        copies[2 * i + 1].wait()
        for hop in range(z.shards):
            lanes = pl.ds(pl.multiple_of((pos_ref[0] ^ hop) * cols, 128), cols)
            part = held[i, :, lanes]
            outs[hop][i] = part
            if hop == 0 and i < 2:
                pair[i] = part
            if hop == z.shards - 1 and i < 2:
                early[i] = part


def pack(z, pos, arrays):
    cols = z.own_heads * z.width
    sources = [pltpu.with_memory_space_constraint(x, pltpu.HBM) for x in arrays]
    shape = jax.ShapeDtypeStruct
    results = pl.pallas_call(
        functools.partial(pack_kernel, z),
        out_shape=[shape((4, z.tok, cols), BF16)] * z.shards
        + [shape((2, z.tok, cols), BF16)] * 2,
        in_specs=[whole(SMEM)] + [whole(pltpu.HBM)] * 4,
        out_specs=[whole(VMEM)] * (z.shards + 2),
        scratch_shapes=[
            VMEM((4, z.tok, cols * z.shards), BF16),
            pltpu.SemaphoreType.DMA((4, 2)),
        ],
        compiler_params=params(8),
        name="pack",
    )(pos, *sources)
    return results[:-2], results[-2], results[-1]


def bias_kernel(z, meta_ref, table_ref, after_ref, bias):
    level_ids = lax.broadcasted_iota(jnp.int32, table_ref.shape, 1)
    for span in range(z.groups):
        column = jnp.sum(
            jnp.where(level_ids == z.level(meta_ref, span), table_ref[...], 0.0),
            axis=1,
            keepdims=True,
        )
        bias[span] = jnp.broadcast_to(column * LOG2E, bias.shape[1:])


def bias_rows(z, meta, table, other):
    return pl.pallas_call(
        functools.partial(bias_kernel, z),
        out_shape=jax.ShapeDtypeStruct((z.groups, table.shape[0], z.tok), F32),
        in_specs=[whole(SMEM), whole(VMEM), whole(pl.ANY)],
        out_specs=whole(VMEM),
        compiler_params=params(8),
        name="bias",
    )(meta, table, other)


def tile_kernel(full_ref, out):
    for i in range(2):
        out[i] = full_ref[i]


def tile_of(full):
    return pl.pallas_call(
        tile_kernel,
        out_shape=jax.ShapeDtypeStruct((2,) + full.shape[1:], BF16),
        in_specs=[whole(VMEM)],
        out_specs=whole(VMEM),
        compiler_params=params(8),
        name="tile",
    )(full)


def stack_kernel(count, *refs):
    for i in range(count):
        for j in range(2):
            refs[-1][i, j] = refs[i][j]


def stack(parts, *others):
    one = parts[0].shape
    return pl.pallas_call(
        functools.partial(stack_kernel, len(parts)),
        out_shape=jax.ShapeDtypeStruct((len(parts), 2) + one[1:], BF16),
        in_specs=[whole(VMEM)] * len(parts) + [whole(pl.ANY)] * len(others),
        out_specs=whole(VMEM),
        compiler_params=params(8),
        name="stack",
    )(*parts, *others)


def after_kernel(*refs):
    pass


def after(x, *others):
    return pl.pallas_call(
        after_kernel,
        out_shape=jax.ShapeDtypeStruct(x.shape, x.dtype),
        in_specs=[whole(pl.ANY)] * (1 + len(others)),
        out_specs=whole(pl.ANY),
        input_output_aliases={0: 0},
        compiler_params=params(1),
        name="after",
    )(x, *others)


class Sizes:
    def __init__(self, shards, replicas, tiles, own_heads, width, tok):
        self.shards, self.replicas, self.tiles = shards, replicas, tiles
        self.own_heads, self.width, self.tok = own_heads, width, tok
        self.groups = shards * replicas
        self.batch = own_heads if self.groups <= 8 else 1
        self.inv_root = 1.0 / math.sqrt(width)

    def group_of(self, meta_ref, turn, hop):
        return (meta_ref[0] ^ hop) * self.replicas + lax.rem(meta_ref[1] + turn, self.replicas)

    def span(self, meta_ref, turn, hop):
        return meta_ref[3 + self.group_of(meta_ref, turn, hop)]

    def level(self, meta_ref, span):
        return meta_ref[3 + self.groups + span]

    def live(self, meta_ref, hop):
        tile = self.group_of(meta_ref, 0, hop) * self.tiles + meta_ref[2]
        return meta_ref[3 + 2 * self.groups + tile]

    def slots(self, meta_ref):
        for turn in range(self.replicas):
            for hop in range(self.shards):
                yield turn, hop, self.span(meta_ref, turn, hop)

    def lanes(self, h):
        return pl.ds(h * self.width, self.width)

    def first_head(self, meta_ref):
        base = 0 if self.batch == self.own_heads else pl.program_id(0) * self.batch
        return meta_ref[0] * self.own_heads + base

    def steps(self, count):
        return lax.div(count + 1, 2)

    def call(self, kernel, name, limit, operands, outs, scratch):
        split = self.batch != self.own_heads

        def spec(shape, kind):
            if kind == "scalar":
                return whole(SMEM)
            if not split:
                return whole(VMEM)
            block, axis = list(shape), {"heads": 0, "lanes": len(shape) - 1}.get(kind)
            if axis is None:
                return pl.BlockSpec(tuple(block), lambda h: (0,) * len(block))
            block[axis] = block[axis] // self.own_heads * self.batch
            return pl.BlockSpec(
                tuple(block), lambda h: tuple(h if d == axis else 0 for d in range(len(block)))
            )

        return pl.pallas_call(
            functools.partial(kernel, self),
            grid=(self.own_heads // self.batch,) if split else (),
            in_specs=[spec(x.shape, kind) for x, kind in operands],
            out_specs=[spec(x.shape, kind) for x, kind in outs],
            out_shape=[x for x, kind in outs],
            scratch_shapes=scratch,
            compiler_params=params(limit),
            name=name,
        )(*(x for x, kind in operands))


def by_slot(z, refs):
    found = []
    for turn in range(len(refs) // 3):
        first, middle, last = refs[3 * turn : 3 * turn + 3]
        found += [first] + [middle.at[i] for i in range(z.shards - 2)] + [last]
    return found


def order_tiles(z, meta_ref, tiles, kv, kt, vt):
    for turn, hop, span in z.slots(meta_ref):
        ref = tiles[turn * z.shards + hop]
        rows = pl.ds(pl.multiple_of(span * z.tok, z.tok), z.tok)
        half = pl.ds(pl.multiple_of(lax.rem(span, 2) * z.tok, z.tok), z.tok)
        for h in range(z.batch):
            k, v = ref[0, :, z.lanes(h)], ref[1, :, z.lanes(h)]
            kv[h, rows, : z.width] = k
            kv[h, rows, z.width :] = v
            kt[h, lax.div(span, 2), :, half] = k.T
            vt[h, lax.div(span, 2), :, half] = v.T


def softmax_sums(z, first, count, bias, kv, both, score, dprob):
    heads, tok = range(z.batch), z.tok
    scale = z.inv_root * LOG2E

    def step(c, carry):
        rows = pl.ds(pl.multiple_of(c * 2 * tok, 2 * tok), 2 * tok)
        new = []
        for h in heads:
            sd = jnp.dot(kv[h, rows, :], both[h][...], preferred_element_type=F32)
            parts = []
            for j in range(2):
                span = 2 * c + j
                shift = bias[span, pl.ds(first + h, 1), :] + jnp.where(span < count, 0.0, DEAD)
                parts.append(sd[j * tok : (j + 1) * tok, :tok] * scale + shift)
            s, dp = jnp.concatenate(parts, axis=0), sd[:, tok:]
            score[h][c] = s
            dprob[h][c] = dp
            old, total, mixed = carry[3 * h : 3 * h + 3]
            peak = jnp.maximum(old, fold(jnp.max, s))
            e = jnp.exp2(s.reshape(-1, 8, tok) - peak[None])
            fade = jnp.exp2(old - peak)
            new += [
                peak,
                total * fade + jnp.sum(e, axis=0),
                mixed * fade + jnp.sum(e * dp.reshape(-1, 8, tok), axis=0),
            ]
        return tuple(new)

    start = (jnp.full((8, tok), -3e38, F32), jnp.zeros((8, tok), F32), jnp.zeros((8, tok), F32))
    sums = lax.fori_loop(0, z.steps(count), step, start * z.batch)
    peaks = [jnp.max(x, axis=0, keepdims=True) for x in sums[::3]]
    fades = [jnp.exp2(x - peak) for x, peak in zip(sums[::3], peaks)]
    totals, mixed = (
        [jnp.sum(x * fade, axis=0, keepdims=True) for x, fade in zip(sums[i::3], fades)]
        for i in (1, 2)
    )
    return peaks, totals, mixed


def gradients(z, count, log_total, delta, score, dprob, both, kt, vt, acc, ot, dqt):
    def grad_step(c, carry):
        rows = pl.ds(pl.multiple_of(c * 2 * z.tok, 2 * z.tok), 2 * z.tok)
        for h in range(z.batch):
            w = jnp.exp2(score[h][c] - log_total[h])
            ds = (w * (dprob[h][c] - delta[h])).astype(BF16)
            w = w.astype(BF16)
            acc[h, rows, :] += jnp.dot(
                jnp.concatenate([ds, w], axis=1), both[h][...], preferred_element_type=F32
            )
            ot[h][...] += jnp.dot(vt[h, c], w, preferred_element_type=F32)
            dqt[h][...] += jnp.dot(kt[h, c], ds, preferred_element_type=F32)
        return carry

    lax.fori_loop(0, z.steps(count), grad_step, 0)


def write_sums(z, meta_ref, acc, sums):
    for turn, hop, span in z.slots(meta_ref):
        goal = sums[turn * z.shards + hop]
        rows = pl.ds(pl.multiple_of(span * z.tok, z.tok), z.tok)
        for h in range(z.batch):
            goal[0, :, z.lanes(h)] = (acc[h, rows, : z.width] * z.inv_root).astype(BF16)
            goal[1, :, z.lanes(h)] = acc[h, rows, z.width :].astype(BF16)


def own_kernel(z, meta_ref, bias, *refs):
    full, refs = refs[: z.shards], refs[z.shards :]
    count = 3 * (z.replicas - 1)
    others, (kt, vt, both, turned, score, dprob, stats, kv) = refs[:count], refs[count:]
    first = z.first_head(meta_ref)
    order_tiles(z, meta_ref, list(full) + by_slot(z, others), kv, kt, vt)
    for hop in range(z.shards):
        for h in range(z.batch):
            for i in range(2):
                for j in range(2):
                    block = full[hop][2 + i, :, z.lanes(h)]
                    block = block if i == j else jnp.zeros_like(block)
                    both[h, hop, pl.ds(i * z.tok, z.tok), z.lanes(j)] = block
                    turned[h, hop, pl.ds(i * z.width, z.width), pl.ds(j * z.tok, z.tok)] = block.T
        count = z.span(meta_ref, 0, hop) + 1
        heads = range(z.batch)
        sums = softmax_sums(
            z,
            first,
            count,
            bias,
            kv,
            [turned.at[h, hop] for h in heads],
            [score.at[h, hop] for h in heads],
            [dprob.at[h, hop] for h in heads],
        )
        for h in heads:
            for i in range(3):
                stats[h, hop, i : i + 1, :] = sums[i][h]


def ahead_kernel(z, meta_ref, bias, both, turned, stats, *refs):
    tiles, refs = by_slot(z, refs[: 3 * z.replicas]), refs[3 * z.replicas :]
    (final, ot, dqt), sums, refs = refs[:3], refs[3 : 3 + z.groups], refs[3 + z.groups :]
    kv, kt, vt, score, dprob, acc = refs
    first = z.first_head(meta_ref)
    heads = range(z.batch)
    order_tiles(z, meta_ref, tiles, kv, kt, vt)
    acc[...] = jnp.zeros_like(acc)
    ot[...] = jnp.zeros_like(ot)
    dqt[...] = jnp.zeros_like(dqt)
    for hop in range(z.shards):
        count = z.span(meta_ref, 0, hop) + 1
        live = z.live(meta_ref, hop)
        near = [[stats[h, hop, i : i + 1, :] for h in heads] for i in range(3)]

        @pl.when(live != 1)
        def _():
            for h in heads:
                final[h, hop, 0:1, :] = near[0][h] + jnp.log2(near[1][h])
                final[h, hop, 1:2, :] = near[2][h] / near[1][h]

        @pl.when(live == 1)
        def _():
            views = (
                [score.at[h] for h in heads],
                [dprob.at[h] for h in heads],
                [both.at[h, hop] for h in heads],
            )
            far = softmax_sums(z, first, count, bias, kv, [turned.at[h, hop] for h in heads], views[0], views[1])
            log_total, delta = [], []
            for h in heads:
                peak = jnp.maximum(near[0][h], far[0][h])
                a, b = jnp.exp2(near[0][h] - peak), jnp.exp2(far[0][h] - peak)
                total = near[1][h] * a + far[1][h] * b
                log_total.append(peak + jnp.log2(total))
                delta.append((near[2][h] * a + far[2][h] * b) / total)
                final[h, hop, 0:1, :] = log_total[h]
                final[h, hop, 1:2, :] = delta[h]
            gradients(
                z,
                count,
                log_total,
                delta,
                *views,
                kt,
                vt,
                acc,
                [ot.at[h, hop] for h in heads],
                [dqt.at[h, hop] for h in heads],
            )

    write_sums(z, meta_ref, acc, sums)


def rows_kernel(z, meta_ref, kt, vt, both, score, dprob, final, ot_in, dqt_in, *refs):
    refs = refs[1:]
    rows_out, sums, refs = refs[: z.shards], refs[z.shards : z.shards + z.groups], refs[-3:]
    acc, ot, dqt = refs
    heads = range(z.batch)
    acc[...] = jnp.zeros_like(acc)
    for hop in range(z.shards):
        count = z.span(meta_ref, 0, hop) + 1
        for h in heads:
            ot[h] = ot_in[h, hop]
            dqt[h] = dqt_in[h, hop]
        gradients(
            z,
            count,
            [final[h, hop, 0:1, :] for h in heads],
            [final[h, hop, 1:2, :] for h in heads],
            [score.at[h, hop] for h in heads],
            [dprob.at[h, hop] for h in heads],
            [both.at[h, hop] for h in heads],
            kt,
            vt,
            acc,
            [ot.at[h] for h in heads],
            [dqt.at[h] for h in heads],
        )
        for h in heads:
            rows_out[hop][0, :, z.lanes(h)] = ot[h].astype(BF16).T
            rows_out[hop][1, :, z.lanes(h)] = (dqt[h] * z.inv_root).astype(BF16).T
    write_sums(z, meta_ref, acc, sums)


def add_up(terms, at=()):
    total = terms[0][at].astype(F32)
    for term in terms[1:]:
        total = total + term[at].astype(F32)
    return total.astype(BF16)


def join(lists):
    count = len(lists[0])

    def kernel(*refs):
        for i in range(len(lists)):
            for which in range(2):
                refs[-1][i, which] = add_up(refs[i * count : (i + 1) * count], which)

    operands = [x for parts in lists for x in parts]
    return pl.pallas_call(
        kernel,
        out_shape=jax.ShapeDtypeStruct((len(lists),) + operands[0].shape, BF16),
        in_specs=[whole(VMEM)] * len(operands),
        out_specs=whole(VMEM),
        compiler_params=params(8),
        name="join",
    )(*operands)


def merge(lists, joined, last):
    count = len(lists[0])

    def kernel(*refs):
        refs, outs = refs[: -1 - len(lists)], refs[-1 - len(lists) :]
        arrived, refs = refs[0], refs[1:]
        for which in range(2):
            for i in range(len(lists)):
                terms = list(refs[i * count : (i + 1) * count]) + [arrived.at[i]]
                outs[i][which] = add_up(terms, which)
            outs[-1][which] = add_up(refs[len(lists) * count :], which)

    operands = [joined] + [x for parts in lists for x in parts] + last
    return pl.pallas_call(
        kernel,
        out_shape=[jax.ShapeDtypeStruct(last[0].shape, BF16)] * (len(lists) + 1),
        in_specs=[whole(VMEM)] * len(operands),
        out_specs=[whole(VMEM)] * (len(lists) + 1),
        compiler_params=params(8),
        name="merge",
    )(*operands)


def unpack(pos, lists):
    shards = len(lists)
    tok, cols = lists[0][0].shape[1:]

    def kernel(pos_ref, *refs):
        ins, outs = list(refs[:-2]), refs[-2:]
        for hop in range(shards):
            terms, ins = ins[: len(lists[hop])], ins[len(lists[hop]) :]
            lanes = pl.ds(pl.multiple_of((pos_ref[0] ^ hop) * cols, 128), cols)
            for i in range(2):
                outs[i][:, lanes] = add_up(terms, i)

    operands = [x for parts in lists for x in parts]
    return pl.pallas_call(
        kernel,
        out_shape=[jax.ShapeDtypeStruct((tok, cols * shards), BF16)] * 2,
        in_specs=[whole(SMEM)] + [whole(VMEM)] * len(operands),
        out_specs=[whole(VMEM)] * 2,
        compiler_params=params(8),
        name="unpack",
    )(pos, *operands)


def per_device(queries, keys, values, grad_out, span_of_group, noise_level, next_live, level_bias):
    tok, model = queries.shape
    heads = level_bias.shape[1]
    width = model // heads
    groups = lax.axis_size("tm")
    tiles = lax.axis_size("tile")
    shards = shard_count(heads, groups)
    replicas = groups // shards
    own = heads // shards
    cols = own * width
    z = Sizes(shards, replicas, tiles, own, width, tok)
    me = lax.axis_index("tm")
    pos = jnp.stack([me // replicas, me % replicas, lax.axis_index("tile")]).astype(jnp.int32)
    meta = jnp.concatenate([pos, span_of_group, noise_level, next_live])
    shape = jax.ShapeDtypeStruct

    def to_shard(x, hop, lift):
        if hop == 0 and lift == 0:
            return x
        pairs = []
        for t in range(groups):
            goal = ((t // replicas) ^ hop) * replicas + t % replicas
            for s in range(tiles):
                pairs.append((t * tiles + s, goal * tiles + (s + lift) % tiles))
        return lax.ppermute(x, ("tm", "tile"), pairs)

    def to_replica(x, turn):
        pairs = [(t, t // replicas * replicas + (t - turn) % replicas) for t in range(groups)]
        return lax.ppermute(x, "tm", pairs)

    def with_others(parts):
        return [
            [parts[hop]]
            + [
                to_replica(parts[turn * shards + hop], replicas - turn)
                for turn in range(1, replicas)
            ]
            for hop in hops
        ]

    def swapped(tiles):
        return [to_replica(x, turn) for turn in range(1, replicas) for x in tiles]

    hops = list(range(shards))
    last = shards - 1
    packed, pair, early = pack(z, pos, (keys, values, queries, grad_out))
    full = [to_shard(packed[hop], hop, 0) for hop in hops]
    bias = bias_rows(z, meta, level_bias.T, full[1])
    far_first, far_last = to_shard(pair, 0, -1), to_shard(early, 0, -1)
    direct = stack(full[1:last], far_first, far_last, bias)
    near = [pair, direct, tile_of(full[last])]
    far = [far_first, to_shard(direct, 0, -1), to_shard(far_last, last, 0)]

    scalars = [(meta, "scalar")]
    one = shape((2, tok, cols), BF16)
    half = groups // 2
    square = shape((own, half, width, 2 * tok), BF16)
    block = shape((own, shards, half, 2 * tok, tok), F32)
    stat = shape((own, shards, 8, tok), F32)
    part = shape((own, shards, width, tok), F32)
    batch = z.batch
    kt, vt, both, turned, score, dprob, stats = z.call(
        own_kernel,
        "own",
        8 if batch == own else 48,
        scalars
        + [(bias, "all")]
        + [(x, "lanes") for x in full + swapped(near)],
        [
            (square, "heads"),
            (square, "heads"),
            (shape((own, shards, 2 * tok, 2 * width), BF16), "heads"),
            (shape((own, shards, 2 * width, 2 * tok), BF16), "heads"),
            (block, "heads"),
            (block, "heads"),
            (stat, "heads"),
        ],
        [
            VMEM((batch, groups * tok, 2 * width), BF16),
        ],
    )
    far = [after(x, stats) for x in far]
    far += swapped(far)
    results = z.call(
        ahead_kernel,
        "ahead",
        16 if batch == own else 48,
        scalars
        + [(bias, "all"), (both, "heads"), (turned, "heads"), (stats, "heads")]
        + [(x, "lanes") for x in far],
        [(stat, "heads"), (part, "heads"), (part, "heads")]
        + [(one, "lanes")] * groups,
        [
            VMEM((batch, groups * tok, 2 * width), BF16),
            VMEM((batch, half, width, 2 * tok), BF16),
            VMEM((batch, half, width, 2 * tok), BF16),
            VMEM((batch, half, 2 * tok, tok), F32),
            VMEM((batch, half, 2 * tok, tok), F32),
            VMEM((batch, groups * tok, 2 * width), F32),
        ],
    )
    final, ot, dqt = results[:3]
    far_parts = with_others(results[3:])
    far_sums = join(far_parts[1:])
    far_home = to_shard(far_sums, 0, 1)
    results = z.call(
        rows_kernel,
        "rows",
        8 if batch == own else 48,
        scalars
        + [(x, "heads") for x in (kt, vt, both, score, dprob, final, ot, dqt)]
        + [(far_sums, "lanes")],
        [(one, "lanes")] * (shards + groups),
        [
            VMEM((batch, groups * tok, 2 * width), F32),
            VMEM((batch, width, tok), F32),
            VMEM((batch, width, tok), F32),
        ],
    )
    rows_home = [to_shard(results[hop], hop, 0) for hop in hops]
    near_parts = with_others(results[shards:])
    *sums, far_last = merge(near_parts[1:], far_home, far_parts[0])
    sums_home = [to_shard(x, hop, 0) for hop, x in zip(hops[1:], sums)]
    last_home = to_shard(far_last, 0, 1)
    attended, grad_queries = unpack(pos, [[x] for x in rows_home])
    grad_keys, grad_values = unpack(
        pos, [near_parts[0] + [last_home]] + [[x] for x in sums_home]
    )
    return attended, grad_queries, grad_keys, grad_values


def solution(mesh):
    sharded = P(("tm", "tile"), None)
    return jax.shard_map(
        per_device,
        mesh=mesh,
        in_specs=(sharded,) * 4 + (P(),) * 4,
        out_specs=(sharded,) * 4,
        check_vma=False,
    )
```

profile of v0, /device:TPU:0, one launch (start us, length us, event | category | flops | bytes accessed | tf_op | source)
XLA Modules:
  0.0 82.1 jit_solution(4949836581970178634)
XLA Ops:
  0.7 2.1 %pack.1 = (bf16[4,128,384]{2,1,0:T(8,128)(2,1)S(1)}, bf16[4,128,384]{2,1,0:T(8,128)(2,1)S(1)}, bf16[4,128,384]{2,1,0:T(8,128)(2,1)S(1)}, bf16[4,128,384]{2,1,0:T...) custom-call(s32[3]{0:T(128)S(1)} %pad_add_fusion.pos_ref, ...), custom_call_target="tpu_custom_call" | custom-call | tf_op jit(solution)/shard_map/pack/pallas_call | solution.py:67
  2.8 3.0 %collective-permute-start = (bf16[4,128,384]{2,1,0:T(8,128)(2,1)S(1)}, bf16[4,128,384]{2,1,0:T(8,128)(2,1)S(1)}, u32[]{:S(2)}, u32[]{:S(2)}) collective-permute-start(bf16[4,128,384]{2,1,0:T(8,128)(2,1)S(1)} %get-tuple-element.48), channel_id=1, source_target_pairs={{0,8},{1,9},{2,10},{3,11},{4,12},{5,13},{6,14},{7,15},{8,0},{9,1},... | collective-permute-start | bytes 1179656 | tf_op jit(solution)/shard_map/ppermute | solution.py:517
  5.8 1.5 %collective-permute-start.1 = (bf16[4,128,384]{2,1,0:T(8,128)(2,1)S(1)}, bf16[4,128,384]{2,1,0:T(8,128)(2,1)S(1)}, u32[]{:S(2)}, u32[]{:S(2)}) collective-permute-start(bf16[4,128,384]{2,1,0:T(8,128)(2,1)S(1)} %get-tuple-element.50), channel_id=1, source_target_pairs={{0,16},{1,17},{2,18},{3,19},{4,20},{5,21},{6,22},{7,23},{8,24},{9,... | collective-permute-start | bytes 1179656 | tf_op jit(solution)/shard_map/ppermute | solution.py:517
  7.4 3.6 %collective-permute-start.5 = (bf16[2,128,384]{2,1,0:T(8,128)(2,1)S(1)}, bf16[2,128,384]{2,1,0:T(8,128)(2,1)S(1)}, u32[]{:S(2)}, u32[]{:S(2)}) collective-permute-start(bf16[2,128,384]{2,1,0:T(8,128)(2,1)S(1)} %get-tuple-element.53), channel_id=1, source_target_pairs={{0,3},{1,0},{2,1},{3,2},{4,7},{5,4},{6,5},{7,6},{8,11},{9,8},{10,9... | collective-permute-start | bytes 589832 | tf_op jit(solution)/shard_map/ppermute | solution.py:517
  12.7 3.1 %collective-permute-done.after_ref.refs_0_.refs_1_ = bf16[4,128,384]{2,1,0:T(8,128)(2,1)S(1)} collective-permute-done((bf16[4,128,384]{2,1,0:T(8,128)(2,1)S(1)}, bf16[4,128,384]{2,1,0:T(8,128)(2,1)S(1)}, u32[]{:S(2)}, u32[]{:S(2)}) %collective-permute-start) | collective-permute-done | bytes 393248 | tf_op jit(solution)/shard_map/ppermute | solution.py:517
  17.3 1.5 %collective-permute-done.4.refs_2_.refs_0_ = bf16[2,128,384]{2,1,0:T(8,128)(2,1)S(1)} collective-permute-done((bf16[2,128,384]{2,1,0:T(8,128)(2,1)S(1)}, bf16[2,128,384]{2,1,0:T(8,128)(2,1)S(1)}, u32[]{:S(2)}, u32[]{:S(2)}) %collective-permute-start.4) | collective-permute-done | bytes 196640 | tf_op jit(solution)/shard_map/ppermute | solution.py:517
  18.8 6.1 %collective-permute-done.1.refs_1_.refs_2_ = bf16[4,128,384]{2,1,0:T(8,128)(2,1)S(1)} collective-permute-done((bf16[4,128,384]{2,1,0:T(8,128)(2,1)S(1)}, bf16[4,128,384]{2,1,0:T(8,128)(2,1)S(1)}, u32[]{:S(2)}, u32[]{:S(2)}) %collective-permute-start.1) | collective-permute-done | bytes 393248 | tf_op jit(solution)/shard_map/ppermute | solution.py:517
  25.0 3.7 %collective-permute-start.8 = (bf16[2,2,128,384]{3,2,1,0:T(8,128)(2,1)S(1)}, bf16[2,2,128,384]{3,2,1,0:T(8,128)(2,1)S(1)}, u32[]{:S(2)}, u32[]{:S(2)}) collective-permute-start(bf16[2,2,128,384]{3,2,1,0:T(8,128)(2,1)S(1)} %stack.17), channel_id=1, source_target_pairs={{0,3},{1,0},{2,1},{3,2},{4,7},{5,4},{6,5},{7,6},{8,11},{9,8},{10,9... | collective-permute-start | bytes 1179656 | tf_op jit(solution)/shard_map/ppermute | solution.py:517
  29.2 1.5 %collective-permute-start.9 = (bf16[2,128,384]{2,1,0:T(8,128)(2,1)S(1)}, bf16[2,128,384]{2,1,0:T(8,128)(2,1)S(1)}, u32[]{:S(2)}, u32[]{:S(2)}) collective-permute-start(bf16[2,128,384]{2,1,0:T(8,128)(2,1)S(1)} %collective-permute-done.5.refs_3_), channel_id=1, source_target_pairs={{0,24},{1,25},{2,26},{3,27},{4,28},{5,29},{6,30},{7,31},{8,16},{9,... | collective-permute-start | bytes 589832 | tf_op jit(solution)/shard_map/ppermute | solution.py:517
  30.7 5.6 %own.1 = (bf16[3,4,128,256]{3,2,1,0:T(8,128)(2,1)S(1)}, bf16[3,4,128,256]{3,2,1,0:T(8,128)(2,1)S(1)}, bf16[3,4,256,256]{3,2,1,0:T(8,128)(2,1)S(1)}, bf16[3,4,256...) custom-call(s32[51]{0:T(128)S(1)} %concatenate.4.meta_ref, ...), custom_call_target="tpu_custom_call" | custom-call | tf_op jit(solution)/shard_map/own/pallas_call | solution.py:207
  36.3 1.3 %collective-permute-done.8.refs_0_ = bf16[2,2,128,384]{3,2,1,0:T(8,128)(2,1)S(1)} collective-permute-done((bf16[2,2,128,384]{3,2,1,0:T(8,128)(2,1)S(1)}, bf16[2,2,128,384]{3,2,1,0:T(8,128)(2,1)S(1)}, u32[]{:S(2)}, u32[]{:S(2)}) %collective-permute-start.8) | collective-permute-done | bytes 393248 | tf_op jit(solution)/shard_map/ppermute | solution.py:517
  38.2 1.4 %collective-permute-done.10.refs_3_ = bf16[2,128,384]{2,1,0:T(8,128)(2,1)S(1)} collective-permute-done((bf16[2,128,384]{2,1,0:T(8,128)(2,1)S(1)}, bf16[2,128,384]{2,1,0:T(8,128)(2,1)S(1)}, u32[]{:S(2)}, u32[]{:S(2)}) %collective-permute-start.10) | collective-permute-done | bytes 196640 | tf_op jit(solution)/shard_map/ppermute | solution.py:521
  39.9 9.4 %ahead.1 = (f32[3,4,8,128]{3,2,1,0:T(8,128)S(1)}, f32[3,4,128,128]{3,2,1,0:T(8,128)S(1)}, f32[3,4,128,128]{3,2,1,0:T(8,128)S(1)}, bf16[2,128,384]{2,1,0:T(8,128)...) custom-call(s32[51]{0:T(128)S(1)} %concatenate.4.meta_ref, ...), custom_call_target="tpu_custom_call" | custom-call | tf_op jit(solution)/shard_map/ahead/pallas_call | solution.py:207
  51.8 5.7 %rows.1 = (bf16[2,128,384]{2,1,0:T(8,128)(2,1)S(1)}, bf16[2,128,384]{2,1,0:T(8,128)(2,1)S(1)}, bf16[2,128,384]{2,1,0:T(8,128)(2,1)S(1)}, bf16[2,128,384]{2,1,0:T...) custom-call(s32[51]{0:T(128)S(1)} %concatenate.4.meta_ref, ...), custom_call_target="tpu_custom_call" | custom-call | tf_op jit(solution)/shard_map/rows/pallas_call | solution.py:207
  59.0 1.5 %collective-permute-start.17 = (bf16[2,128,384]{2,1,0:T(8,128)(2,1)S(1)}, bf16[2,128,384]{2,1,0:T(8,128)(2,1)S(1)}, u32[]{:S(2)}, u32[]{:S(2)}) collective-permute-start(bf16[2,128,384]{2,1,0:T(8,128)(2,1)S(1)} %get-tuple-element.72), channel_id=1, source_target_pairs={{0,16},{1,17},{2,18},{3,19},{4,20},{5,21},{6,22},{7,23},{8,24},{9,... | collective-permute-start | bytes 589832 | tf_op jit(solution)/shard_map/ppermute | solution.py:517
  60.6 1.1 %collective-permute-start.18 = (bf16[2,128,384]{2,1,0:T(8,128)(2,1)S(1)}, bf16[2,128,384]{2,1,0:T(8,128)(2,1)S(1)}, u32[]{:S(2)}, u32[]{:S(2)}) collective-permute-start(bf16[2,128,384]{2,1,0:T(8,128)(2,1)S(1)} %get-tuple-element.73), channel_id=1, source_target_pairs={{0,24},{1,25},{2,26},{3,27},{4,28},{5,29},{6,30},{7,31},{8,16},{9,... | collective-permute-start | bytes 589832 | tf_op jit(solution)/shard_map/ppermute | solution.py:517
  61.7 7.1 %collective-permute-done.20.refs_0_ = bf16[3,2,128,384]{3,2,1,0:T(8,128)(2,1)S(1)} collective-permute-done((bf16[3,2,128,384]{3,2,1,0:T(8,128)(2,1)S(1)}, bf16[3,2,128,384]{3,2,1,0:T(8,128)(2,1)S(1)}, u32[]{:S(2)}, u32[]{:S(2)}) %collective-permute-start.20) | collective-permute-done | bytes 589856 | tf_op jit(solution)/shard_map/ppermute | solution.py:517
  69.5 2.2 %collective-permute-start.27 = (bf16[2,128,384]{2,1,0:T(8,128)(2,1)S(1)}, bf16[2,128,384]{2,1,0:T(8,128)(2,1)S(1)}, u32[]{:S(2)}, u32[]{:S(2)}) collective-permute-start(bf16[2,128,384]{2,1,0:T(8,128)(2,1)S(1)} %get-tuple-element.88), channel_id=1, source_target_pairs={{0,16},{1,17},{2,18},{3,19},{4,20},{5,21},{6,22},{7,23},{8,24},{9,... | collective-permute-start | bytes 589832 | tf_op jit(solution)/shard_map/ppermute | solution.py:517
  71.7 1.2 %collective-permute-start.28 = (bf16[2,128,384]{2,1,0:T(8,128)(2,1)S(1)}, bf16[2,128,384]{2,1,0:T(8,128)(2,1)S(1)}, u32[]{:S(2)}, u32[]{:S(2)}) collective-permute-start(bf16[2,128,384]{2,1,0:T(8,128)(2,1)S(1)} %get-tuple-element.89), channel_id=1, source_target_pairs={{0,24},{1,25},{2,26},{3,27},{4,28},{5,29},{6,30},{7,31},{8,16},{9,... | collective-permute-start | bytes 589832 | tf_op jit(solution)/shard_map/ppermute | solution.py:517
  72.9 1.5 %unpack.2 = (bf16[128,1536]{1,0:T(8,128)(2,1)}, bf16[128,1536]{1,0:T(8,128)(2,1)}) custom-call(s32[3]{0:T(128)S(1)} %pad_add_fusion.pos_ref, bf16[2,128,384]{2,1,0:T(8,128)(2,1)S(1)} %get-tuple-element.70.refs_0_, bf16[2,128,384]{2,1,0:T(8,128)(2,1)S(1)} %collective-permute-done.16.refs_1_, bf16[2,128,384]{2,1,0:T(8,128)(2,1)S(1)} %collective-permute-done.17.refs_2_, ...), custom_call_target="tpu_custom_call" | custom-call | tf_op jit(solution)/shard_map/unpack/pallas_call | solution.py:483
  74.4 2.8 %collective-permute-done.25.refs_2_ = bf16[2,128,384]{2,1,0:T(8,128)(2,1)S(1)} collective-permute-done((bf16[2,128,384]{2,1,0:T(8,128)(2,1)S(1)}, bf16[2,128,384]{2,1,0:T(8,128)(2,1)S(1)}, u32[]{:S(2)}, u32[]{:S(2)}) %collective-permute-start.25) | collective-permute-done | bytes 196640 | tf_op jit(solution)/shard_map/ppermute | solution.py:517
  77.1 2.0 %collective-permute-done.27.refs_4_ = bf16[2,128,384]{2,1,0:T(8,128)(2,1)S(1)} collective-permute-done((bf16[2,128,384]{2,1,0:T(8,128)(2,1)S(1)}, bf16[2,128,384]{2,1,0:T(8,128)(2,1)S(1)}, u32[]{:S(2)}, u32[]{:S(2)}) %collective-permute-start.27) | collective-permute-done | bytes 196640 | tf_op jit(solution)/shard_map/ppermute | solution.py:517
  79.1 1.4 %collective-permute-done.28.refs_5_ = bf16[2,128,384]{2,1,0:T(8,128)(2,1)S(1)} collective-permute-done((bf16[2,128,384]{2,1,0:T(8,128)(2,1)S(1)}, bf16[2,128,384]{2,1,0:T(8,128)(2,1)S(1)}, u32[]{:S(2)}, u32[]{:S(2)}) %collective-permute-start.28) | collective-permute-done | bytes 196640 | tf_op jit(solution)/shard_map/ppermute | solution.py:517
  80.6 1.5 %unpack.3 = (bf16[128,1536]{1,0:T(8,128)(2,1)}, bf16[128,1536]{1,0:T(8,128)(2,1)}) custom-call(s32[3]{0:T(128)S(1)} %pad_add_fusion.pos_ref, bf16[2,128,384]{2,1,0:T(8,128)(2,1)S(1)} %get-tuple-element.76.refs_0_, bf16[2,128,384]{2,1,0:T(8,128)(2,1)S(1)} %collective-permute-done.19.refs_1_, bf16[2,128,384]{2,1,0:T(8,128)(2,1)S(1)} %collective-permute-done.25.refs_2_, ...), custom_call_target="tpu_custom_call" | custom-call | tf_op jit(solution)/shard_map/unpack/pallas_call | solution.py:483
  (52 shorter events, 9.6 us)
Async XLA Ops:
  2.8 12.9 %collective-permute-start = (bf16[4,128,384]{2,1,0:T(8,128)(2,1)S(1)}, bf16[4,128,384]{2,1,0:T(8,128)(2,1)S(1)}, u32[]{:S(2)}, u32[]{:S(2)}) collective-permute-start(bf16[4,128,384]{2,1,0:T(8,128)(2,1)S(1)} %get-tuple-element.48), channel_id=1, source_target_pairs={{0,8},{1,9},{2,10},{3,11},{4,12},{5,13},{6,14},{7,15},{8,0},{9,1},... | collective-permute-start | bytes 1179656 | tf_op jit(solution)/shard_map/ppermute | solution.py:517
  5.8 19.0 %collective-permute-start.1 = (bf16[4,128,384]{2,1,0:T(8,128)(2,1)S(1)}, bf16[4,128,384]{2,1,0:T(8,128)(2,1)S(1)}, u32[]{:S(2)}, u32[]{:S(2)}) collective-permute-start(bf16[4,128,384]{2,1,0:T(8,128)(2,1)S(1)} %get-tuple-element.50), channel_id=1, source_target_pairs={{0,16},{1,17},{2,18},{3,19},{4,20},{5,21},{6,22},{7,23},{8,24},{9,... | collective-permute-start | bytes 1179656 | tf_op jit(solution)/shard_map/ppermute | solution.py:517
  7.4 9.9 %collective-permute-start.5 = (bf16[2,128,384]{2,1,0:T(8,128)(2,1)S(1)}, bf16[2,128,384]{2,1,0:T(8,128)(2,1)S(1)}, u32[]{:S(2)}, u32[]{:S(2)}) collective-permute-start(bf16[2,128,384]{2,1,0:T(8,128)(2,1)S(1)} %get-tuple-element.53), channel_id=1, source_target_pairs={{0,3},{1,0},{2,1},{3,2},{4,7},{5,4},{6,5},{7,6},{8,11},{9,8},{10,9... | collective-permute-start | bytes 589832 | tf_op jit(solution)/shard_map/ppermute | solution.py:517
  11.0 7.8 %collective-permute-start.4 = (bf16[2,128,384]{2,1,0:T(8,128)(2,1)S(1)}, bf16[2,128,384]{2,1,0:T(8,128)(2,1)S(1)}, u32[]{:S(2)}, u32[]{:S(2)}) collective-permute-start(bf16[2,128,384]{2,1,0:T(8,128)(2,1)S(1)} %get-tuple-element.52), channel_id=1, source_target_pairs={{0,3},{1,0},{2,1},{3,2},{4,7},{5,4},{6,5},{7,6},{8,11},{9,8},{10,9... | collective-permute-start | bytes 589832 | tf_op jit(solution)/shard_map/ppermute | solution.py:517
  11.4 17.4 %collective-permute-start.2 = (bf16[4,128,384]{2,1,0:T(8,128)(2,1)S(1)}, bf16[4,128,384]{2,1,0:T(8,128)(2,1)S(1)}, u32[]{:S(2)}, u32[]{:S(2)}) collective-permute-start(bf16[4,128,384]{2,1,0:T(8,128)(2,1)S(1)} %get-tuple-element.51), channel_id=1, source_target_pairs={{0,24},{1,25},{2,26},{3,27},{4,28},{5,29},{6,30},{7,31},{8,16},{9,... | collective-permute-start | bytes 1179656 | tf_op jit(solution)/shard_map/ppermute | solution.py:517
  24.9 5.8 %collective-permute-start.6 = (bf16[2,2,128,384]{3,2,1,0:T(8,128)(2,1)S(1)}, bf16[2,2,128,384]{3,2,1,0:T(8,128)(2,1)S(1)}, u32[]{:S(2)}, u32[]{:S(2)}) collective-permute-start(bf16[2,2,128,384]{3,2,1,0:T(8,128)(2,1)S(1)} %stack.17), channel_id=1, source_target_pairs={{0,4},{4,0},{8,12},{12,8},{16,20},{20,16},{24,28},{28,24},{1,5},{5... | collective-permute-start | bytes 1179656 | tf_op jit(solution)/shard_map/ppermute | solution.py:521
  25.0 12.6 %collective-permute-start.8 = (bf16[2,2,128,384]{3,2,1,0:T(8,128)(2,1)S(1)}, bf16[2,2,128,384]{3,2,1,0:T(8,128)(2,1)S(1)}, u32[]{:S(2)}, u32[]{:S(2)}) collective-permute-start(bf16[2,2,128,384]{3,2,1,0:T(8,128)(2,1)S(1)} %stack.17), channel_id=1, source_target_pairs={{0,3},{1,0},{2,1},{3,2},{4,7},{5,4},{6,5},{7,6},{8,11},{9,8},{10,9... | collective-permute-start | bytes 1179656 | tf_op jit(solution)/shard_map/ppermute | solution.py:517
  28.6 2.1 %collective-permute-start.3 = (bf16[2,128,384]{2,1,0:T(8,128)(2,1)S(1)}, bf16[2,128,384]{2,1,0:T(8,128)(2,1)S(1)}, u32[]{:S(2)}, u32[]{:S(2)}) collective-permute-start(bf16[2,128,384]{2,1,0:T(8,128)(2,1)S(1)} %get-tuple-element.52), channel_id=1, source_target_pairs={{0,4},{4,0},{8,12},{12,8},{16,20},{20,16},{24,28},{28,24},{1,5},{5... | collective-permute-start | bytes 589832 | tf_op jit(solution)/shard_map/ppermute | solution.py:521
  28.8 1.9 %collective-permute-start.7 = (bf16[2,128,384]{2,1,0:T(8,128)(2,1)S(1)}, bf16[2,128,384]{2,1,0:T(8,128)(2,1)S(1)}, u32[]{:S(2)}, u32[]{:S(2)}) collective-permute-start(bf16[2,128,384]{2,1,0:T(8,128)(2,1)S(1)} %tile.1), channel_id=1, source_target_pairs={{0,4},{4,0},{8,12},{12,8},{16,20},{20,16},{24,28},{28,24},{1,5},{5... | collective-permute-start | bytes 589832 | tf_op jit(solution)/shard_map/ppermute | solution.py:521
  29.2 8.9 %collective-permute-start.9 = (bf16[2,128,384]{2,1,0:T(8,128)(2,1)S(1)}, bf16[2,128,384]{2,1,0:T(8,128)(2,1)S(1)}, u32[]{:S(2)}, u32[]{:S(2)}) collective-permute-start(bf16[2,128,384]{2,1,0:T(8,128)(2,1)S(1)} %collective-permute-done.5.refs_3_), channel_id=1, source_target_pairs={{0,24},{1,25},{2,26},{3,27},{4,28},{5,29},{6,30},{7,31},{8,16},{9,... | collective-permute-start | bytes 589832 | tf_op jit(solution)/shard_map/ppermute | solution.py:517
  37.6 2.3 %collective-permute-start.11 = (bf16[2,2,128,384]{3,2,1,0:T(8,128)(2,1)S(1)}, bf16[2,2,128,384]{3,2,1,0:T(8,128)(2,1)S(1)}, u32[]{:S(2)}, u32[]{:S(2)}) collective-permute-start(bf16[2,2,128,384]{3,2,1,0:T(8,128)(2,1)S(1)} %after.4.refs_1_), channel_id=1, source_target_pairs={{0,4},{4,0},{8,12},{12,8},{16,20},{20,16},{24,28},{28,24},{1,5},{5... | collective-permute-start | bytes 1179656 | tf_op jit(solution)/shard_map/ppermute | solution.py:521
  37.6 2.0 %collective-permute-start.10 = (bf16[2,128,384]{2,1,0:T(8,128)(2,1)S(1)}, bf16[2,128,384]{2,1,0:T(8,128)(2,1)S(1)}, u32[]{:S(2)}, u32[]{:S(2)}) collective-permute-start(bf16[2,128,384]{2,1,0:T(8,128)(2,1)S(1)} %after.3.refs_0_), channel_id=1, source_target_pairs={{0,4},{4,0},{8,12},{12,8},{16,20},{20,16},{24,28},{28,24},{1,5},{5... | collective-permute-start | bytes 589832 | tf_op jit(solution)/shard_map/ppermute | solution.py:521
  51.5 17.3 %collective-permute-start.20 = (bf16[3,2,128,384]{3,2,1,0:T(8,128)(2,1)S(1)}, bf16[3,2,128,384]{3,2,1,0:T(8,128)(2,1)S(1)}, u32[]{:S(2)}, u32[]{:S(2)}) collective-permute-start(bf16[3,2,128,384]{3,2,1,0:T(8,128)(2,1)S(1)} %join.1.refs_0_), channel_id=1, source_target_pairs={{0,1},{1,2},{2,3},{3,0},{4,5},{5,6},{6,7},{7,4},{8,9},{9,10},{10,1... | collective-permute-start | bytes 1769480 | tf_op jit(solution)/shard_map/ppermute | solution.py:517
  51.5 6.7 %collective-permute-start.24 = (bf16[2,128,384]{2,1,0:T(8,128)(2,1)S(1)}, bf16[2,128,384]{2,1,0:T(8,128)(2,1)S(1)}, u32[]{:S(2)}, u32[]{:S(2)}) collective-permute-start(bf16[2,128,384]{2,1,0:T(8,128)(2,1)S(1)} %get-tuple-element.85), channel_id=1, source_target_pairs={{0,4},{4,0},{8,12},{12,8},{16,20},{20,16},{24,28},{28,24},{1,5},{5... | collective-permute-start | bytes 589832 | tf_op jit(solution)/shard_map/ppermute | solution.py:521
  57.6 2.9 %collective-permute-start.22 = (bf16[2,128,384]{2,1,0:T(8,128)(2,1)S(1)}, bf16[2,128,384]{2,1,0:T(8,128)(2,1)S(1)}, u32[]{:S(2)}, u32[]{:S(2)}) collective-permute-start(bf16[2,128,384]{2,1,0:T(8,128)(2,1)S(1)} %get-tuple-element.81), channel_id=1, source_target_pairs={{0,4},{4,0},{8,12},{12,8},{16,20},{20,16},{24,28},{28,24},{1,5},{5... | collective-permute-start | bytes 589832 | tf_op jit(solution)/shard_map/ppermute | solution.py:521
  58.1 3.6 %collective-permute-start.23 = (bf16[2,128,384]{2,1,0:T(8,128)(2,1)S(1)}, bf16[2,128,384]{2,1,0:T(8,128)(2,1)S(1)}, u32[]{:S(2)}, u32[]{:S(2)}) collective-permute-start(bf16[2,128,384]{2,1,0:T(8,128)(2,1)S(1)} %get-tuple-element.83), channel_id=1, source_target_pairs={{0,4},{4,0},{8,12},{12,8},{16,20},{20,16},{24,28},{28,24},{1,5},{5... | collective-permute-start | bytes 589832 | tf_op jit(solution)/shard_map/ppermute | solution.py:521
  58.2 10.9 %collective-permute-start.16 = (bf16[2,128,384]{2,1,0:T(8,128)(2,1)S(1)}, bf16[2,128,384]{2,1,0:T(8,128)(2,1)S(1)}, u32[]{:S(2)}, u32[]{:S(2)}) collective-permute-start(bf16[2,128,384]{2,1,0:T(8,128)(2,1)S(1)} %get-tuple-element.71), channel_id=1, source_target_pairs={{0,8},{1,9},{2,10},{3,11},{4,12},{5,13},{6,14},{7,15},{8,0},{9,1},... | collective-permute-start | bytes 589832 | tf_op jit(solution)/shard_map/ppermute | solution.py:517
  59.0 10.4 %collective-permute-start.17 = (bf16[2,128,384]{2,1,0:T(8,128)(2,1)S(1)}, bf16[2,128,384]{2,1,0:T(8,128)(2,1)S(1)}, u32[]{:S(2)}, u32[]{:S(2)}) collective-permute-start(bf16[2,128,384]{2,1,0:T(8,128)(2,1)S(1)} %get-tuple-element.72), channel_id=1, source_target_pairs={{0,16},{1,17},{2,18},{3,19},{4,20},{5,21},{6,22},{7,23},{8,24},{9,... | collective-permute-start | bytes 589832 | tf_op jit(solution)/shard_map/ppermute | solution.py:517
  60.6 11.2 %collective-permute-start.18 = (bf16[2,128,384]{2,1,0:T(8,128)(2,1)S(1)}, bf16[2,128,384]{2,1,0:T(8,128)(2,1)S(1)}, u32[]{:S(2)}, u32[]{:S(2)}) collective-permute-start(bf16[2,128,384]{2,1,0:T(8,128)(2,1)S(1)} %get-tuple-element.73), channel_id=1, source_target_pairs={{0,24},{1,25},{2,26},{3,27},{4,28},{5,29},{6,30},{7,31},{8,16},{9,... | collective-permute-start | bytes 589832 | tf_op jit(solution)/shard_map/ppermute | solution.py:517
  61.7 12.7 %collective-permute-start.19 = (bf16[2,128,384]{2,1,0:T(8,128)(2,1)S(1)}, bf16[2,128,384]{2,1,0:T(8,128)(2,1)S(1)}, u32[]{:S(2)}, u32[]{:S(2)}) collective-permute-start(bf16[2,128,384]{2,1,0:T(8,128)(2,1)S(1)} %get-tuple-element.77), channel_id=1, source_target_pairs={{0,4},{4,0},{8,12},{12,8},{16,20},{20,16},{24,28},{28,24},{1,5},{5... | collective-permute-start | bytes 589832 | tf_op jit(solution)/shard_map/ppermute | solution.py:521
  69.1 8.1 %collective-permute-start.25 = (bf16[2,128,384]{2,1,0:T(8,128)(2,1)S(1)}, bf16[2,128,384]{2,1,0:T(8,128)(2,1)S(1)}, u32[]{:S(2)}, u32[]{:S(2)}) collective-permute-start(bf16[2,128,384]{2,1,0:T(8,128)(2,1)S(1)} %get-tuple-element.86), channel_id=1, source_target_pairs={{0,1},{1,2},{2,3},{3,0},{4,5},{5,6},{6,7},{7,4},{8,9},{9,10},{10,1... | collective-permute-start | bytes 589832 | tf_op jit(solution)/shard_map/ppermute | solution.py:517
  69.1 8.0 %collective-permute-start.26 = (bf16[2,128,384]{2,1,0:T(8,128)(2,1)S(1)}, bf16[2,128,384]{2,1,0:T(8,128)(2,1)S(1)}, u32[]{:S(2)}, u32[]{:S(2)}) collective-permute-start(bf16[2,128,384]{2,1,0:T(8,128)(2,1)S(1)} %get-tuple-element.87), channel_id=1, source_target_pairs={{0,8},{1,9},{2,10},{3,11},{4,12},{5,13},{6,14},{7,15},{8,0},{9,1},... | collective-permute-start | bytes 589832 | tf_op jit(solution)/shard_map/ppermute | solution.py:517
  69.5 9.7 %collective-permute-start.27 = (bf16[2,128,384]{2,1,0:T(8,128)(2,1)S(1)}, bf16[2,128,384]{2,1,0:T(8,128)(2,1)S(1)}, u32[]{:S(2)}, u32[]{:S(2)}) collective-permute-start(bf16[2,128,384]{2,1,0:T(8,128)(2,1)S(1)} %get-tuple-element.88), channel_id=1, source_target_pairs={{0,16},{1,17},{2,18},{3,19},{4,20},{5,21},{6,22},{7,23},{8,24},{9,... | collective-permute-start | bytes 589832 | tf_op jit(solution)/shard_map/ppermute | solution.py:517
  71.7 8.9 %collective-permute-start.28 = (bf16[2,128,384]{2,1,0:T(8,128)(2,1)S(1)}, bf16[2,128,384]{2,1,0:T(8,128)(2,1)S(1)}, u32[]{:S(2)}, u32[]{:S(2)}) collective-permute-start(bf16[2,128,384]{2,1,0:T(8,128)(2,1)S(1)} %get-tuple-element.89), channel_id=1, source_target_pairs={{0,24},{1,25},{2,26},{3,27},{4,28},{5,29},{6,30},{7,31},{8,16},{9,... | collective-permute-start | bytes 589832 | tf_op jit(solution)/shard_map/ppermute | solution.py:517
  (6 other events, 8.8 us)
where the time goes:
time: 81 us; the launch traced here: 82.1 us
  waiting for transfers between devices  29 us (36%)
  Pallas kernels  26.9 us (33%)
  starting transfers between devices  23.8 us (29%)
  local copies, waits for them, and re-layouts  1.6 us (2%)
    ppermute x15, waiting for transfers between devices, to_shard(): return lax.ppermute(x, ('tm', 'tile'), pairs)  25.3 us
    ppermute x15, starting transfers between devices, to_shard(): return lax.ppermute(x, ('tm', 'tile'), pairs)  21 us
    pallas_call x3, Pallas kernels, call(): pl.pallas_call(functools.partial(kernel, self), grid=(self.own_heads // s...  20.6 us
    ppermute x14, waiting for transfers between devices, to_replica(): return lax.ppermute(x, 'tm', pairs)  3.7 us
    pallas_call x2, Pallas kernels, unpack(): pl.pallas_call(kernel, out_shape=[jax.ShapeDtypeStruct((tok, cols * shard...  3.01 us
    ppermute x14, starting transfers between devices, to_replica(): return lax.ppermute(x, 'tm', pairs)  2.82 us
    pallas_call x1, Pallas kernels, pack(): pl.pallas_call(functools.partial(pack_kernel, z), out_shape=[shape((4, z....  2.1 us
  transfers between devices with their start and end apart: 29, of which 14 were waited for; matrix products, arithmetic and copies ran while one was open for 1% of the time, Pallas kernels for 17%

commit v1 on v0

--- a/solution.py
+++ b/solution.py
@@ -38,7 +38,7 @@
 
 def pack_kernel(z, pos_ref, *refs):
     sources, refs = refs[:4], refs[4:]
-    outs, (pair, early, held, sems) = refs[: z.shards], refs[z.shards :]
+    outs, (pair, pair_rows, early, held, sems) = refs[: z.shards], refs[z.shards :]
     half, cols = z.tok // 2, z.own_heads * z.width
     copies = []
     for i, src in enumerate(sources):
@@ -54,8 +54,8 @@
             lanes = pl.ds(pl.multiple_of((pos_ref[0] ^ hop) * cols, 128), cols)
             part = held[i, :, lanes]
             outs[hop][i] = part
-            if hop == 0 and i < 2:
-                pair[i] = part
+            if hop == 0:
+                (pair if i < 2 else pair_rows)[i % 2] = part
             if hop == z.shards - 1 and i < 2:
                 early[i] = part
 
@@ -67,9 +67,9 @@
     results = pl.pallas_call(
         functools.partial(pack_kernel, z),
         out_shape=[shape((4, z.tok, cols), BF16)] * z.shards
-        + [shape((2, z.tok, cols), BF16)] * 2,
+        + [shape((2, z.tok, cols), BF16)] * 3,
         in_specs=[whole(SMEM)] + [whole(pltpu.HBM)] * 4,
-        out_specs=[whole(VMEM)] * (z.shards + 2),
+        out_specs=[whole(VMEM)] * (z.shards + 3),
         scratch_shapes=[
             VMEM((4, z.tok, cols * z.shards), BF16),
             pltpu.SemaphoreType.DMA((4, 2)),
@@ -77,7 +77,7 @@
         compiler_params=params(8),
         name="pack",
     )(pos, *sources)
-    return results[:-2], results[-2], results[-1]
+    return results[:-3], results[-3:]
 
 
 def bias_kernel(z, meta_ref, table_ref, after_ref, bias):
@@ -102,33 +102,21 @@
     )(meta, table, other)
 
 
-def tile_kernel(full_ref, out):
-    for i in range(2):
-        out[i] = full_ref[i]
-
-
-def tile_of(full):
-    return pl.pallas_call(
-        tile_kernel,
-        out_shape=jax.ShapeDtypeStruct((2,) + full.shape[1:], BF16),
-        in_specs=[whole(VMEM)],
-        out_specs=whole(VMEM),
-        compiler_params=params(8),
-        name="tile",
-    )(full)
-
-
-def stack_kernel(count, *refs):
+def stack_kernel(count, base, *refs):
+    out = refs[-1]
     for i in range(count):
         for j in range(2):
-            refs[-1][i, j] = refs[i][j]
-
-
-def stack(parts, *others):
-    one = parts[0].shape
+            if len(out.shape) == 4:
+                out[i, j] = refs[i][base + j]
+            else:
+                out[j] = refs[i][base + j]
+
+
+def stack(parts, base, others=(), flat=False):
+    one = (2,) + parts[0].shape[1:]
     return pl.pallas_call(
-        functools.partial(stack_kernel, len(parts)),
-        out_shape=jax.ShapeDtypeStruct((len(parts), 2) + one[1:], BF16),
+        functools.partial(stack_kernel, len(parts), base),
+        out_shape=jax.ShapeDtypeStruct(one if flat else (len(parts),) + one, BF16),
         in_specs=[whole(VMEM)] * len(parts) + [whole(pl.ANY)] * len(others),
         out_specs=whole(VMEM),
         compiler_params=params(8),
@@ -169,14 +157,22 @@
     def level(self, meta_ref, span):
         return meta_ref[3 + self.groups + span]
 
-    def live(self, meta_ref, hop):
-        tile = self.group_of(meta_ref, 0, hop) * self.tiles + meta_ref[2]
+    def live(self, meta_ref, turn, hop):
+        tile = self.group_of(meta_ref, turn, hop) * self.tiles + meta_ref[2]
         return meta_ref[3 + 2 * self.groups + tile]
 
-    def slots(self, meta_ref):
+    def ranks(self, meta_ref, ahead):
+        turn = self.replicas - 1 if ahead else 0
+        spans = [self.span(meta_ref, turn, hop) for hop in range(self.shards)]
+        return spans, [sum(jnp.where(x < span, 1, 0) for x in spans) for span in spans]
+
+    def queries(self, meta_ref, ahead):
+        spans, _ = self.ranks(meta_ref, ahead)
         for turn in range(self.replicas):
             for hop in range(self.shards):
-                yield turn, hop, self.span(meta_ref, turn, hop)
+                span = self.span(meta_ref, turn, hop)
+                count = sum(jnp.where(x <= span, 1, 0) for x in spans)
+                yield turn * self.shards + hop, count, self.live(meta_ref, turn, hop)
 
     def lanes(self, h):
         return pl.ds(h * self.width, self.width)
@@ -216,7 +212,7 @@
         )(*(x for x, kind in operands))
 
 
-def by_slot(z, refs):
+def by_hop(z, refs):
     found = []
     for turn in range(len(refs) // 3):
         first, middle, last = refs[3 * turn : 3 * turn + 3]
@@ -224,17 +220,16 @@
     return found
 
 
-def order_tiles(z, meta_ref, tiles, kv, kt, vt):
-    for turn, hop, span in z.slots(meta_ref):
-        ref = tiles[turn * z.shards + hop]
-        rows = pl.ds(pl.multiple_of(span * z.tok, z.tok), z.tok)
-        half = pl.ds(pl.multiple_of(lax.rem(span, 2) * z.tok, z.tok), z.tok)
+def order_tiles(z, tiles, ranks, kv, kt, vt):
+    for ref, rank in zip(tiles, ranks):
+        rows = pl.ds(pl.multiple_of(rank * z.tok, z.tok), z.tok)
+        half = pl.ds(pl.multiple_of(lax.rem(rank, 2) * z.tok, z.tok), z.tok)
         for h in range(z.batch):
             k, v = ref[0, :, z.lanes(h)], ref[1, :, z.lanes(h)]
             kv[h, rows, : z.width] = k
             kv[h, rows, z.width :] = v
-            kt[h, lax.div(span, 2), :, half] = k.T
-            vt[h, lax.div(span, 2), :, half] = v.T
+            kt[h, lax.div(rank, 2), :, half] = k.T
+            vt[h, lax.div(rank, 2), :, half] = v.T
 
 
 def softmax_sums(z, first, count, bias, kv, both, score, dprob):
@@ -245,11 +240,11 @@
         rows = pl.ds(pl.multiple_of(c * 2 * tok, 2 * tok), 2 * tok)
         new = []
         for h in heads:
-            sd = jnp.dot(kv[h, rows, :], both[h][...], preferred_element_type=F32)
+            sd = lax.dot_general(kv[h, rows, :], both[h][...], NT, preferred_element_type=F32)
             parts = []
             for j in range(2):
-                span = 2 * c + j
-                shift = bias[span, pl.ds(first + h, 1), :] + jnp.where(span < count, 0.0, DEAD)
+                rank = 2 * c + j
+                shift = bias[rank, pl.ds(first + h, 1), :] + jnp.where(rank < count, 0.0, DEAD)
                 parts.append(sd[j * tok : (j + 1) * tok, :tok] * scale + shift)
             s, dp = jnp.concatenate(parts, axis=0), sd[:, tok:]
             score[h][c] = s
@@ -293,119 +288,151 @@
     lax.fori_loop(0, z.steps(count), grad_step, 0)
 
 
-def write_sums(z, meta_ref, acc, sums):
-    for turn, hop, span in z.slots(meta_ref):
-        goal = sums[turn * z.shards + hop]
-        rows = pl.ds(pl.multiple_of(span * z.tok, z.tok), z.tok)
+def write_sums(z, goals, ranks, acc):
+    for goal, rank in zip(goals, ranks):
+        rows = pl.ds(pl.multiple_of(rank * z.tok, z.tok), z.tok)
         for h in range(z.batch):
             goal[0, :, z.lanes(h)] = (acc[h, rows, : z.width] * z.inv_root).astype(BF16)
             goal[1, :, z.lanes(h)] = acc[h, rows, z.width :].astype(BF16)
 
 
+def merge_sums(parts):
+    merged = []
+    for h in range(len(parts[0][0])):
+        peak = parts[0][0][h]
+        for part in parts[1:]:
+            peak = jnp.maximum(peak, part[0][h])
+        fades = [jnp.exp2(part[0][h] - peak) for part in parts]
+        merged.append(
+            [peak] + [sum(part[i][h] * fade for part, fade in zip(parts, fades)) for i in (1, 2)]
+        )
+    return merged
+
+
+def read_sums(stats, heads, at):
+    return [[stats[h, at, i : i + 1, :] for h in heads] for i in range(3)]
+
+
 def own_kernel(z, meta_ref, bias, *refs):
     full, refs = refs[: z.shards], refs[z.shards :]
     count = 3 * (z.replicas - 1)
-    others, (kt, vt, both, turned, score, dprob, stats, kv) = refs[:count], refs[count:]
+    others, (kt, vt, both, score, dprob, stats, kv, ranked) = by_hop(z, refs[:count]), refs[count:]
     first = z.first_head(meta_ref)
-    order_tiles(z, meta_ref, list(full) + by_slot(z, others), kv, kt, vt)
-    for hop in range(z.shards):
-        for h in range(z.batch):
+    heads = range(z.batch)
+    spans, ranks = z.ranks(meta_ref, False)
+    order_tiles(z, full, ranks, kv, kt, vt)
+    for span, rank in zip(spans, ranks):
+        ranked[rank] = bias[span]
+    for at, count, _ in z.queries(meta_ref, False):
+        for h in heads:
             for i in range(2):
                 for j in range(2):
-                    block = full[hop][2 + i, :, z.lanes(h)]
-                    block = block if i == j else jnp.zeros_like(block)
-                    both[h, hop, pl.ds(i * z.tok, z.tok), z.lanes(j)] = block
-                    turned[h, hop, pl.ds(i * z.width, z.width), pl.ds(j * z.tok, z.tok)] = block.T
-        count = z.span(meta_ref, 0, hop) + 1
-        heads = range(z.batch)
+                    ref, base = (full[at], 2) if at < z.shards else (others[at - z.shards], 0)
+                    block = ref[base + i, :, z.lanes(h)]
+                    both[h, at, pl.ds(i * z.tok, z.tok), z.lanes(j)] = (
+                        block if i == j else jnp.zeros_like(block)
+                    )
         sums = softmax_sums(
             z,
             first,
             count,
-            bias,
+            ranked,
             kv,
-            [turned.at[h, hop] for h in heads],
-            [score.at[h, hop] for h in heads],
-            [dprob.at[h, hop] for h in heads],
+            [both.at[h, at] for h in heads],
+            [score.at[h, at] for h in heads],
+            [dprob.at[h, at] for h in heads],
         )
         for h in heads:
             for i in range(3):
-                stats[h, hop, i : i + 1, :] = sums[i][h]
-
-
-def ahead_kernel(z, meta_ref, bias, both, turned, stats, *refs):
-    tiles, refs = by_slot(z, refs[: 3 * z.replicas]), refs[3 * z.replicas :]
-    (final, ot, dqt), sums, refs = refs[:3], refs[3 : 3 + z.groups], refs[3 + z.groups :]
-    kv, kt, vt, score, dprob, acc = refs
+                stats[h, at, i : i + 1, :] = sums[i][h]
+
+
+def ahead_kernel(z, meta_ref, bias, both, stats, *refs):
+    tiles, (merged, kt, vt, score, dprob, kv, ranked) = by_hop(z, refs[:3]), refs[3:]
     first = z.first_head(meta_ref)
     heads = range(z.batch)
-    order_tiles(z, meta_ref, tiles, kv, kt, vt)
+    spans, ranks = z.ranks(meta_ref, True)
+    order_tiles(z, tiles, ranks, kv, kt, vt)
+    for span, rank in zip(spans, ranks):
+        ranked[rank] = bias[span]
+    for at, count, live in z.queries(meta_ref, True):
+        merged[:, at] = stats[:, at]
+
+        @pl.when(live == 1)
+        def _():
+            far = softmax_sums(
+                z,
+                first,
+                count,
+                ranked,
+                kv,
+                [both.at[h, at] for h in heads],
+                [score.at[h, at] for h in heads],
+                [dprob.at[h, at] for h in heads],
+            )
+            sums = merge_sums([read_sums(stats, heads, at), far])
+            for h in heads:
+                for i in range(3):
+                    merged[h, at, i : i + 1, :] = sums[h][i]
+
+
+def back_kernel(z, meta_ref, both, stats, kt, vt, score, dprob, *refs):
+    others, refs = refs[: z.replicas - 1], refs[z.replicas - 1 :]
+    final, ot, dqt, own_sums, sums, acc = refs
+    heads = range(z.batch)
     acc[...] = jnp.zeros_like(acc)
     ot[...] = jnp.zeros_like(ot)
     dqt[...] = jnp.zeros_like(dqt)
-    for hop in range(z.shards):
-        count = z.span(meta_ref, 0, hop) + 1
-        live = z.live(meta_ref, hop)
-        near = [[stats[h, hop, i : i + 1, :] for h in heads] for i in range(3)]
-
-        @pl.when(live != 1)
-        def _():
-            for h in heads:
-                final[h, hop, 0:1, :] = near[0][h] + jnp.log2(near[1][h])
-                final[h, hop, 1:2, :] = near[2][h] / near[1][h]
+    for at, count, live in z.queries(meta_ref, True):
+        parts = [read_sums(stats, heads, at)]
+        for turn, other in enumerate(others, 1):
+            place = (at // z.shards - turn) % z.replicas * z.shards + at % z.shards
+            parts.append(read_sums(other, heads, place))
+        log_total, delta = [], []
+        for h, (peak, total, mixed) in enumerate(merge_sums(parts)):
+            log_total.append(peak + jnp.log2(total))
+            delta.append(mixed / total)
+            final[h, at, 0:1, :] = log_total[h]
+            final[h, at, 1:2, :] = delta[h]
 
         @pl.when(live == 1)
         def _():
-            views = (
-                [score.at[h] for h in heads],
-                [dprob.at[h] for h in heads],
-                [both.at[h, hop] for h in heads],
-            )
-            far = softmax_sums(z, first, count, bias, kv, [turned.at[h, hop] for h in heads], views[0], views[1])
-            log_total, delta = [], []
-            for h in heads:
-                peak = jnp.maximum(near[0][h], far[0][h])
-                a, b = jnp.exp2(near[0][h] - peak), jnp.exp2(far[0][h] - peak)
-                total = near[1][h] * a + far[1][h] * b
-                log_total.append(peak + jnp.log2(total))
-                delta.append((near[2][h] * a + far[2][h] * b) / total)
-                final[h, hop, 0:1, :] = log_total[h]
-                final[h, hop, 1:2, :] = delta[h]
             gradients(
                 z,
                 count,
                 log_total,
                 delta,
-                *views,
+                [score.at[h, at] for h in heads],
+                [dprob.at[h, at] for h in heads],
+                [both.at[h, at] for h in heads],
                 kt,
                 vt,
                 acc,
-                [ot.at[h, hop] for h in heads],
-                [dqt.at[h, hop] for h in heads],
+                [ot.at[h, at] for h in heads],
+                [dqt.at[h, at] for h in heads],
             )
 
-    write_sums(z, meta_ref, acc, sums)
+    goals = [own_sums] + [sums.at[i] for i in range(z.shards - 1)]
+    write_sums(z, goals, z.ranks(meta_ref, True)[1], acc)
 
 
 def rows_kernel(z, meta_ref, kt, vt, both, score, dprob, final, ot_in, dqt_in, *refs):
-    refs = refs[1:]
-    rows_out, sums, refs = refs[: z.shards], refs[z.shards : z.shards + z.groups], refs[-3:]
-    acc, ot, dqt = refs
+    rows_out, refs = refs[1 : 1 + z.groups], refs[1 + z.groups :]
+    sums, (acc, ot, dqt) = refs[: z.shards], refs[z.shards :]
     heads = range(z.batch)
     acc[...] = jnp.zeros_like(acc)
-    for hop in range(z.shards):
-        count = z.span(meta_ref, 0, hop) + 1
+    for at, count, _ in z.queries(meta_ref, False):
         for h in heads:
-            ot[h] = ot_in[h, hop]
-            dqt[h] = dqt_in[h, hop]
+            ot[h] = ot_in[h, at]
+            dqt[h] = dqt_in[h, at]
         gradients(
             z,
             count,
-            [final[h, hop, 0:1, :] for h in heads],
-            [final[h, hop, 1:2, :] for h in heads],
-            [score.at[h, hop] for h in heads],
-            [dprob.at[h, hop] for h in heads],
-            [both.at[h, hop] for h in heads],
+            [final[h, at, 0:1, :] for h in heads],
+            [final[h, at, 1:2, :] for h in heads],
+            [score.at[h, at] for h in heads],
+            [dprob.at[h, at] for h in heads],
+            [both.at[h, at] for h in heads],
             kt,
             vt,
             acc,
@@ -413,9 +440,9 @@
             [dqt.at[h] for h in heads],
         )
         for h in heads:
-            rows_out[hop][0, :, z.lanes(h)] = ot[h].astype(BF16).T
-            rows_out[hop][1, :, z.lanes(h)] = (dqt[h] * z.inv_root).astype(BF16).T
-    write_sums(z, meta_ref, acc, sums)
+            rows_out[at][0, :, z.lanes(h)] = ot[h].astype(BF16).T
+            rows_out[at][1, :, z.lanes(h)] = (dqt[h] * z.inv_root).astype(BF16).T
+    write_sums(z, sums, z.ranks(meta_ref, False)[1], acc)
 
 
 def add_up(terms, at=()):
@@ -425,22 +452,22 @@
     return total.astype(BF16)
 
 
-def join(lists):
+def add(lists):
     count = len(lists[0])
 
     def kernel(*refs):
         for i in range(len(lists)):
             for which in range(2):
-                refs[-1][i, which] = add_up(refs[i * count : (i + 1) * count], which)
+                refs[i - len(lists)][which] = add_up(refs[i * count : (i + 1) * count], which)
 
     operands = [x for parts in lists for x in parts]
     return pl.pallas_call(
         kernel,
-        out_shape=jax.ShapeDtypeStruct((len(lists),) + operands[0].shape, BF16),
+        out_shape=[jax.ShapeDtypeStruct(operands[0].shape, BF16)] * len(lists),
         in_specs=[whole(VMEM)] * len(operands),
-        out_specs=whole(VMEM),
+        out_specs=[whole(VMEM)] * len(lists),
         compiler_params=params(8),
-        name="join",
+        name="add",
     )(*operands)
 
 
@@ -511,7 +538,7 @@
             return x
         pairs = []
         for t in range(groups):
-            goal = ((t // replicas) ^ hop) * replicas + t % replicas
+            goal = ((t // replicas) ^ hop) * replicas + (t - lift) % replicas
             for s in range(tiles):
                 pairs.append((t * tiles + s, goal * tiles + (s + lift) % tiles))
         return lax.ppermute(x, ("tm", "tile"), pairs)
@@ -535,88 +562,93 @@
 
     hops = list(range(shards))
     last = shards - 1
-    packed, pair, early = pack(z, pos, (keys, values, queries, grad_out))
+    packed, (pair, pair_rows, early) = pack(z, pos, (keys, values, queries, grad_out))
     full = [to_shard(packed[hop], hop, 0) for hop in hops]
-    bias = bias_rows(z, meta, level_bias.T, full[1])
     far_first, far_last = to_shard(pair, 0, -1), to_shard(early, 0, -1)
-    direct = stack(full[1:last], far_first, far_last, bias)
-    near = [pair, direct, tile_of(full[last])]
+    bias = bias_rows(z, meta, level_bias.T, far_first)
+    direct = stack(full[1:last], 0, (far_first, far_last, bias))
     far = [far_first, to_shard(direct, 0, -1), to_shard(far_last, last, 0)]
+    rows = swapped([pair_rows, stack(full[1:last], 2, (bias,)), stack(full[last:], 2, flat=True)])
 
     scalars = [(meta, "scalar")]
+    half = shards // 2
     one = shape((2, tok, cols), BF16)
-    half = groups // 2
     square = shape((own, half, width, 2 * tok), BF16)
-    block = shape((own, shards, half, 2 * tok, tok), F32)
-    stat = shape((own, shards, 8, tok), F32)
-    part = shape((own, shards, width, tok), F32)
+    block = shape((own, groups, half, 2 * tok, tok), F32)
+    stat = shape((own, groups, 8, tok), F32)
+    part = shape((own, groups, width, tok), F32)
     batch = z.batch
-    kt, vt, both, turned, score, dprob, stats = z.call(
+    limit = 8 if batch == own else 56
+    tiles_scratch = VMEM((batch, shards * tok, 2 * width), BF16)
+    ranked_scratch = VMEM((shards, heads, tok), F32)
+    sums_scratch = VMEM((batch, shards * tok, 2 * width), F32)
+    kt, vt, both, score, dprob, stats = z.call(
         own_kernel,
         "own",
-        8 if batch == own else 48,
-        scalars
-        + [(bias, "all")]
-        + [(x, "lanes") for x in full + swapped(near)],
+        limit,
+        scalars + [(bias, "all")] + [(x, "lanes") for x in full + rows],
         [
             (square, "heads"),
             (square, "heads"),
-            (shape((own, shards, 2 * tok, 2 * width), BF16), "heads"),
-            (shape((own, shards, 2 * width, 2 * tok), BF16), "heads"),
+            (shape((own, groups, 2 * tok, 2 * width), BF16), "heads"),
             (block, "heads"),
             (block, "heads"),
             (stat, "heads"),
         ],
-        [
-            VMEM((batch, groups * tok, 2 * width), BF16),
-        ],
+        [tiles_scratch, ranked_scratch],
     )
-    far = [after(x, stats) for x in far]
-    far += swapped(far)
-    results = z.call(
+    merged, far_kt, far_vt, far_score, far_dprob = z.call(
         ahead_kernel,
         "ahead",
-        16 if batch == own else 48,
+        limit,
         scalars
-        + [(bias, "all"), (both, "heads"), (turned, "heads"), (stats, "heads")]
-        + [(x, "lanes") for x in far],
-        [(stat, "heads"), (part, "heads"), (part, "heads")]
-        + [(one, "lanes")] * groups,
+        + [(bias, "all"), (both, "heads"), (stats, "heads")]
+        + [(after(x, stats), "lanes") for x in far],
         [
-            VMEM((batch, groups * tok, 2 * width), BF16),
-            VMEM((batch, half, width, 2 * tok), BF16),
-            VMEM((batch, half, width, 2 * tok), BF16),
-            VMEM((batch, half, 2 * tok, tok), F32),
-            VMEM((batch, half, 2 * tok, tok), F32),
-            VMEM((batch, groups * tok, 2 * width), F32),
+            (stat, "heads"),
+            (square, "heads"),
+            (square, "heads"),
+            (block, "heads"),
+            (block, "heads"),
         ],
+        [tiles_scratch, ranked_scratch],
     )
-    final, ot, dqt = results[:3]
-    far_parts = with_others(results[3:])
-    far_sums = join(far_parts[1:])
+    final, ot, dqt, first_sums, far_sums = z.call(
+        back_kernel,
+        "back",
+        limit,
+        scalars
+        + [(x, "heads") for x in (both, merged, far_kt, far_vt, far_score, far_dprob)]
+        + [(x, "heads") for x in swapped([merged])],
+        [
+            (stat, "heads"),
+            (part, "heads"),
+            (part, "heads"),
+            (one, "lanes"),
+            (shape((last, 2, tok, cols), BF16), "lanes"),
+        ],
+        [sums_scratch],
+    )
     far_home = to_shard(far_sums, 0, 1)
     results = z.call(
         rows_kernel,
         "rows",
-        8 if batch == own else 48,
+        limit,
         scalars
         + [(x, "heads") for x in (kt, vt, both, score, dprob, final, ot, dqt)]
-        + [(far_sums, "lanes")],
-        [(one, "lanes")] * (shards + groups),
-        [
-            VMEM((batch, groups * tok, 2 * width), F32),
-            VMEM((batch, width, tok), F32),
-            VMEM((batch, width, tok), F32),
-        ],
+        + [(first_sums, "lanes")],
+        [(one, "lanes")] * (groups + shards),
+        [sums_scratch, VMEM((batch, width, tok), F32), VMEM((batch, width, tok), F32)],
     )
-    rows_home = [to_shard(results[hop], hop, 0) for hop in hops]
-    near_parts = with_others(results[shards:])
-    *sums, far_last = merge(near_parts[1:], far_home, far_parts[0])
+    row_sums = add(with_others(results[:groups]))
+    rows_home = [to_shard(row_sums[hop], hop, 0) for hop in hops]
+    near_sums = results[groups:]
+    *sums, first_late = merge([[x] for x in near_sums[1:]], far_home, [first_sums])
     sums_home = [to_shard(x, hop, 0) for hop, x in zip(hops[1:], sums)]
-    last_home = to_shard(far_last, 0, 1)
+    first_home = to_shard(first_late, 0, 1)
     attended, grad_queries = unpack(pos, [[x] for x in rows_home])
     grad_keys, grad_values = unpack(
-        pos, [near_parts[0] + [last_home]] + [[x] for x in sums_home]
+        pos, [[near_sums[0], first_home]] + [[x] for x in sums_home]
     )
     return attended, grad_queries, grad_keys, grad_values
 

time: 81 us -> 82.8 us (1.022); the launches traced: 82.1 us -> 81.8 us
  starting transfers between devices: 23.8 us -> 31.5 us
  waiting for transfers between devices: 29 us -> 22.3 us
  Pallas kernels: 26.9 us -> 25.5 us
    ppermute x15, starting transfers between devices: 21 us -> 28.8 us  [to_shard(): return lax.ppermute(x, ('tm', 'tile'), pairs)]
    ppermute x15, waiting for transfers between devices: 25.3 us -> 20 us  [to_shard(): return lax.ppermute(x, ('tm', 'tile'), pairs)]
    pallas_call x3 -> x4, Pallas kernels: 20.6 us -> 18.7 us  [call(): pl.pallas_call(functools.partial(kernel, self), grid=(self.own_heads // s...]
    ppermute x14 -> x8, waiting for transfers between devices: 3.7 us -> 2.21 us  [to_replica(): return lax.ppermute(x, 'tm', pairs)]
    ppermute x14 -> x8, starting transfers between devices: 2.82 us -> 2.76 us  [to_replica(): return lax.ppermute(x, 'tm', pairs)]
  transfers between devices with their start and end apart: 29 -> 23, of which waited for: 14 -> 11; matrix products, arithmetic and copies ran while one was open for 1% -> 1% of each run, Pallas kernels for 17% -> 20%
where the time goes in v1:
time: 82.8 us; the launch traced here: 81.8 us
  starting transfers between devices  31.5 us (38%)
  Pallas kernels  25.5 us (31%)
  waiting for transfers between devices  22.3 us (27%)
  local copies, waits for them, and re-layouts  1.6 us (2%)
    ppermute x15, starting transfers between devices, to_shard(): return lax.ppermute(x, ('tm', 'tile'), pairs)  28.8 us
    ppermute x15, waiting for transfers between devices, to_shard(): return lax.ppermute(x, ('tm', 'tile'), pairs)  20 us
    pallas_call x4, Pallas kernels, call(): pl.pallas_call(functools.partial(kernel, self), grid=(self.own_heads // s...  18.7 us
    pallas_call x2, Pallas kernels, unpack(): pl.pallas_call(kernel, out_shape=[jax.ShapeDtypeStruct((tok, cols * shard...  2.99 us
    ppermute x8, starting transfers between devices, to_replica(): return lax.ppermute(x, 'tm', pairs)  2.76 us
    pallas_call x1, Pallas kernels, pack(): pl.pallas_call(functools.partial(pack_kernel, z), out_shape=[shape((4, z....  2.74 us
    ppermute x8, waiting for transfers between devices, to_replica(): return lax.ppermute(x, 'tm', pairs)  2.21 us
  transfers between devices with their start and end apart: 23, of which 11 were waited for; matrix products, arithmetic and copies ran while one was open for 1% of the time, Pallas kernels for 20%

profile of v1, /device:TPU:0, one launch (start us, length us, event | category | flops | bytes accessed | tf_op | source)
XLA Modules:
  0.0 81.8 jit_solution(14655937147832520034)
XLA Ops:
  0.7 2.7 %pack.1 = (bf16[4,128,384]{2,1,0:T(8,128)(2,1)S(1)}, bf16[4,128,384]{2,1,0:T(8,128)(2,1)S(1)}, bf16[4,128,384]{2,1,0:T(8,128)(2,1)S(1)}, bf16[4,128,384]{2,1,0:T...) custom-call(s32[3]{0:T(128)S(1)} %pad_add_fusion.pos_ref, ...), custom_call_target="tpu_custom_call" | custom-call | tf_op jit(solution)/shard_map/pack/pallas_call | solution.py:67
  3.5 3.0 %collective-permute-start.1 = (bf16[4,128,384]{2,1,0:T(8,128)(2,1)S(1)}, bf16[4,128,384]{2,1,0:T(8,128)(2,1)S(1)}, u32[]{:S(2)}, u32[]{:S(2)}) collective-permute-start(bf16[4,128,384]{2,1,0:T(8,128)(2,1)S(1)} %get-tuple-element.53), channel_id=1, source_target_pairs={{0,8},{1,9},{2,10},{3,11},{4,12},{5,13},{6,14},{7,15},{8,0},{9,1},... | collective-permute-start | bytes 1179656 | tf_op jit(solution)/shard_map/ppermute | solution.py:544
  6.5 1.5 %collective-permute-start.2 = (bf16[4,128,384]{2,1,0:T(8,128)(2,1)S(1)}, bf16[4,128,384]{2,1,0:T(8,128)(2,1)S(1)}, u32[]{:S(2)}, u32[]{:S(2)}) collective-permute-start(bf16[4,128,384]{2,1,0:T(8,128)(2,1)S(1)} %get-tuple-element.54), channel_id=1, source_target_pairs={{0,16},{1,17},{2,18},{3,19},{4,20},{5,21},{6,22},{7,23},{8,24},{9,... | collective-permute-start | bytes 1179656 | tf_op jit(solution)/shard_map/ppermute | solution.py:544
  8.0 2.5 %collective-permute-start = (bf16[2,128,384]{2,1,0:T(8,128)(2,1)}, bf16[2,128,384]{2,1,0:T(8,128)(2,1)S(1)}, u32[]{:S(2)}, u32[]{:S(2)}) collective-permute-start(bf16[2,128,384]{2,1,0:T(8,128)(2,1)} %get-tuple-element.51), channel_id=1, source_target_pairs={{0,7},{1,4},{2,5},{3,6},{4,3},{5,0},{6,1},{7,2},{8,15},{9,12},{10,... | collective-permute-start | bytes 589832 | tf_op jit(solution)/shard_map/ppermute | solution.py:544
  11.0 1.0 %collective-permute-start.7 = (bf16[2,128,384]{2,1,0:T(8,128)(2,1)S(1)}, bf16[2,128,384]{2,1,0:T(8,128)(2,1)S(1)}, u32[]{:S(2)}, u32[]{:S(2)}) collective-permute-start(bf16[2,128,384]{2,1,0:T(8,128)(2,1)S(1)} %get-tuple-element.63), channel_id=1, source_target_pairs={{0,7},{1,4},{2,5},{3,6},{4,3},{5,0},{6,1},{7,2},{8,15},{9,12},{10,... | collective-permute-start | bytes 589832 | tf_op jit(solution)/shard_map/ppermute | solution.py:544
  12.7 2.9 %collective-permute-done.after_ref.refs_0_.refs_2_ = bf16[2,128,384]{2,1,0:T(8,128)(2,1)S(1)} collective-permute-done((bf16[2,128,384]{2,1,0:T(8,128)(2,1)}, bf16[2,128,384]{2,1,0:T(8,128)(2,1)S(1)}, u32[]{:S(2)}, u32[]{:S(2)}) %collective-permute-start) | collective-permute-done | bytes 196640 | tf_op jit(solution)/shard_map/ppermute | solution.py:544
  17.1 8.3 %collective-permute-done.2.refs_1_.refs_2_ = bf16[4,128,384]{2,1,0:T(8,128)(2,1)S(1)} collective-permute-done((bf16[4,128,384]{2,1,0:T(8,128)(2,1)S(1)}, bf16[4,128,384]{2,1,0:T(8,128)(2,1)S(1)}, u32[]{:S(2)}, u32[]{:S(2)}) %collective-permute-start.2) | collective-permute-done | bytes 393248 | tf_op jit(solution)/shard_map/ppermute | solution.py:544
  25.7 3.7 %collective-permute-start.8 = (bf16[2,2,128,384]{3,2,1,0:T(8,128)(2,1)S(1)}, bf16[2,2,128,384]{3,2,1,0:T(8,128)(2,1)S(1)}, u32[]{:S(2)}, u32[]{:S(2)}) collective-permute-start(bf16[2,2,128,384]{3,2,1,0:T(8,128)(2,1)S(1)} %stack.21), channel_id=1, source_target_pairs={{0,7},{1,4},{2,5},{3,6},{4,3},{5,0},{6,1},{7,2},{8,15},{9,12},{10,... | collective-permute-start | bytes 1179656 | tf_op jit(solution)/shard_map/ppermute | solution.py:544
  30.0 1.5 %collective-permute-start.9 = (bf16[2,128,384]{2,1,0:T(8,128)(2,1)S(1)}, bf16[2,128,384]{2,1,0:T(8,128)(2,1)S(1)}, u32[]{:S(2)}, u32[]{:S(2)}) collective-permute-start(bf16[2,128,384]{2,1,0:T(8,128)(2,1)S(1)} %collective-permute-done.7.refs_3_), channel_id=1, source_target_pairs={{0,24},{1,25},{2,26},{3,27},{4,28},{5,29},{6,30},{7,31},{8,16},{9,... | collective-permute-start | bytes 589832 | tf_op jit(solution)/shard_map/ppermute | solution.py:544
  31.5 6.8 %own.1 = (bf16[3,2,128,256]{3,2,1,0:T(8,128)(2,1)S(1)}, bf16[3,2,128,256]{3,2,1,0:T(8,128)(2,1)S(1)}, bf16[3,8,256,256]{3,2,1,0:T(8,128)(2,1)S(1)}, f32[3,8,2,25...) custom-call(s32[51]{0:T(128)S(1)} %concatenate.4.meta_ref, ...), custom_call_target="tpu_custom_call" | custom-call | tf_op jit(solution)/shard_map/own/pallas_call | solution.py:203
  38.3 2.3 %ahead.1 = (f32[3,8,8,128]{3,2,1,0:T(8,128)S(1)}, bf16[3,2,128,256]{3,2,1,0:T(8,128)(2,1)S(1)}, bf16[3,2,128,256]{3,2,1,0:T(8,128)(2,1)S(1)}, f32[3,8,2,256,128]...) custom-call(s32[51]{0:T(128)S(1)} %concatenate.4.meta_ref, f32[8,12,128]{2,1,0:T(8,128)S(1)} %bias.1.refs_2_.refs_4_, ...), custom_call_target="tpu_custom_call" | custom-call | tf_op jit(solution)/shard_map/ahead/pallas_call | solution.py:203
  40.6 1.0 %collective-permute-start.10 = (f32[3,8,8,128]{3,2,1,0:T(8,128)S(1)}, f32[3,8,8,128]{3,2,1,0:T(8,128)S(1)}, u32[]{:S(2)}, u32[]{:S(2)}) collective-permute-start(f32[3,8,8,128]{3,2,1,0:T(8,128)S(1)} %get-tuple-element.64.stats), channel_id=1, source_target_pairs={{0,4},{4,0},{8,12},{12,8},{16,20},{20,16},{24,28},{28,24},{1,5},{5... | collective-permute-start | bytes 294920 | tf_op jit(solution)/shard_map/ppermute | solution.py:548
  41.6 0.9 %collective-permute-done.10.refs_0_ = f32[3,8,8,128]{3,2,1,0:T(8,128)S(1)} collective-permute-done((f32[3,8,8,128]{3,2,1,0:T(8,128)S(1)}, f32[3,8,8,128]{3,2,1,0:T(8,128)S(1)}, u32[]{:S(2)}, u32[]{:S(2)}) %collective-permute-start.10) | collective-permute-done | bytes 98336 | tf_op jit(solution)/shard_map/ppermute | solution.py:548
  42.6 2.3 %back.1 = (f32[3,8,8,128]{3,2,1,0:T(8,128)S(1)}, f32[3,8,128,128]{3,2,1,0:T(8,128)S(1)}, f32[3,8,128,128]{3,2,1,0:T(8,128)S(1)}, bf16[2,128,384]{2,1,0:T(8,128)(2,1)S(1)}, bf16[3,2,128,384]{3,2,1,0:T(8,128)(2,1)S(1)}) custom-call(s32[51]{0:T(128)S(1)} %concatenate.4.meta_ref, bf16[3,8,256,256]{3,2,1,0:T(8,128)(2,1)S(1)} %get-tuple-element.59.both, ...), custom_call_target="tpu_custom_call" | custom-call | tf_op jit(solution)/shard_map/back/pallas_call | solution.py:203
  44.9 4.7 %collective-permute-start.18 = (bf16[3,2,128,384]{3,2,1,0:T(8,128)(2,1)S(1)}, bf16[3,2,128,384]{3,2,1,0:T(8,128)(2,1)S(1)}, u32[]{:S(2)}, u32[]{:S(2)}) collective-permute-start(bf16[3,2,128,384]{3,2,1,0:T(8,128)(2,1)S(1)} %get-tuple-element.88), channel_id=1, source_target_pairs={{0,5},{1,6},{2,7},{3,4},{4,1},{5,2},{6,3},{7,0},{8,13},{9,14},{10,... | collective-permute-start | bytes 1769480 | tf_op jit(solution)/shard_map/ppermute | solution.py:544
  49.7 7.3 %rows.1 = (bf16[2,128,384]{2,1,0:T(8,128)(2,1)S(1)}, bf16[2,128,384]{2,1,0:T(8,128)(2,1)S(1)}, bf16[2,128,384]{2,1,0:T(8,128)(2,1)S(1)}, bf16[2,128,384]{2,1,0:T...) custom-call(s32[51]{0:T(128)S(1)} %concatenate.4.meta_ref, ...), custom_call_target="tpu_custom_call" | custom-call | tf_op jit(solution)/shard_map/rows/pallas_call | solution.py:203
  59.6 2.0 %collective-permute-start.16 = (bf16[2,128,384]{2,1,0:T(8,128)(2,1)S(1)}, bf16[2,128,384]{2,1,0:T(8,128)(2,1)S(1)}, u32[]{:S(2)}, u32[]{:S(2)}) collective-permute-start(bf16[2,128,384]{2,1,0:T(8,128)(2,1)S(1)} %get-tuple-element.83), channel_id=1, source_target_pairs={{0,16},{1,17},{2,18},{3,19},{4,20},{5,21},{6,22},{7,23},{8,24},{9,... | collective-permute-start | bytes 589832 | tf_op jit(solution)/shard_map/ppermute | solution.py:544
  61.7 1.4 %collective-permute-start.17 = (bf16[2,128,384]{2,1,0:T(8,128)(2,1)S(1)}, bf16[2,128,384]{2,1,0:T(8,128)(2,1)S(1)}, u32[]{:S(2)}, u32[]{:S(2)}) collective-permute-start(bf16[2,128,384]{2,1,0:T(8,128)(2,1)S(1)} %get-tuple-element.84), channel_id=1, source_target_pairs={{0,24},{1,25},{2,26},{3,27},{4,28},{5,29},{6,30},{7,31},{8,16},{9,... | collective-permute-start | bytes 589832 | tf_op jit(solution)/shard_map/ppermute | solution.py:544
  63.4 3.9 %collective-permute-done.15.refs_1_ = bf16[2,128,384]{2,1,0:T(8,128)(2,1)S(1)} collective-permute-done((bf16[2,128,384]{2,1,0:T(8,128)(2,1)S(1)}, bf16[2,128,384]{2,1,0:T(8,128)(2,1)S(1)}, u32[]{:S(2)}, u32[]{:S(2)}) %collective-permute-start.15) | collective-permute-done | bytes 196640 | tf_op jit(solution)/shard_map/ppermute | solution.py:544
  67.3 1.5 %collective-permute-start.21 = (bf16[2,128,384]{2,1,0:T(8,128)(2,1)S(1)}, bf16[2,128,384]{2,1,0:T(8,128)(2,1)S(1)}, u32[]{:S(2)}, u32[]{:S(2)}) collective-permute-start(bf16[2,128,384]{2,1,0:T(8,128)(2,1)S(1)} %get-tuple-element.94), channel_id=1, source_target_pairs={{0,16},{1,17},{2,18},{3,19},{4,20},{5,21},{6,22},{7,23},{8,24},{9,... | collective-permute-start | bytes 589832 | tf_op jit(solution)/shard_map/ppermute | solution.py:544
  69.6 5.0 %collective-permute-start.22 = (bf16[2,128,384]{2,1,0:T(8,128)(2,1)S(1)}, bf16[2,128,384]{2,1,0:T(8,128)(2,1)S(1)}, u32[]{:S(2)}, u32[]{:S(2)}) collective-permute-start(bf16[2,128,384]{2,1,0:T(8,128)(2,1)S(1)} %get-tuple-element.95), channel_id=1, source_target_pairs={{0,24},{1,25},{2,26},{3,27},{4,28},{5,29},{6,30},{7,31},{8,16},{9,... | collective-permute-start | bytes 589832 | tf_op jit(solution)/shard_map/ppermute | solution.py:544
  74.6 1.5 %unpack.2 = (bf16[128,1536]{1,0:T(8,128)(2,1)}, bf16[128,1536]{1,0:T(8,128)(2,1)}) custom-call(s32[3]{0:T(128)S(1)} %pad_add_fusion.pos_ref, bf16[2,128,384]{2,1,0:T(8,128)(2,1)S(1)} %get-tuple-element.81.refs_0_, bf16[2,128,384]{2,1,0:T(8,128)(2,1)S(1)} %collective-permute-done.15.refs_1_, bf16[2,128,384]{2,1,0:T(8,128)(2,1)S(1)} %collective-permute-done.16.refs_2_, ...), custom_call_target="tpu_custom_call" | custom-call | tf_op jit(solution)/shard_map/unpack/pallas_call | solution.py:510
  76.7 3.6 %collective-permute-done.22.refs_4_ = bf16[2,128,384]{2,1,0:T(8,128)(2,1)S(1)} collective-permute-done((bf16[2,128,384]{2,1,0:T(8,128)(2,1)S(1)}, bf16[2,128,384]{2,1,0:T(8,128)(2,1)S(1)}, u32[]{:S(2)}, u32[]{:S(2)}) %collective-permute-start.22) | collective-permute-done | bytes 196640 | tf_op jit(solution)/shard_map/ppermute | solution.py:544
  80.3 1.5 %unpack.3 = (bf16[128,1536]{1,0:T(8,128)(2,1)}, bf16[128,1536]{1,0:T(8,128)(2,1)}) custom-call(s32[3]{0:T(128)S(1)} %pad_add_fusion.pos_ref, bf16[2,128,384]{2,1,0:T(8,128)(2,1)S(1)} %get-tuple-element.87.refs_0_, bf16[2,128,384]{2,1,0:T(8,128)(2,1)S(1)} %collective-permute-done.19.refs_1_, bf16[2,128,384]{2,1,0:T(8,128)(2,1)S(1)} %collective-permute-done.20.refs_2_, ...), custom_call_target="tpu_custom_call" | custom-call | tf_op jit(solution)/shard_map/unpack/pallas_call | solution.py:510
  (42 shorter events, 7.9 us)
Async XLA Ops:
  3.5 13.7 %collective-permute-start.1 = (bf16[4,128,384]{2,1,0:T(8,128)(2,1)S(1)}, bf16[4,128,384]{2,1,0:T(8,128)(2,1)S(1)}, u32[]{:S(2)}, u32[]{:S(2)}) collective-permute-start(bf16[4,128,384]{2,1,0:T(8,128)(2,1)S(1)} %get-tuple-element.53), channel_id=1, source_target_pairs={{0,8},{1,9},{2,10},{3,11},{4,12},{5,13},{6,14},{7,15},{8,0},{9,1},... | collective-permute-start | bytes 1179656 | tf_op jit(solution)/shard_map/ppermute | solution.py:544
  6.5 19.0 %collective-permute-start.2 = (bf16[4,128,384]{2,1,0:T(8,128)(2,1)S(1)}, bf16[4,128,384]{2,1,0:T(8,128)(2,1)S(1)}, u32[]{:S(2)}, u32[]{:S(2)}) collective-permute-start(bf16[4,128,384]{2,1,0:T(8,128)(2,1)S(1)} %get-tuple-element.54), channel_id=1, source_target_pairs={{0,16},{1,17},{2,18},{3,19},{4,20},{5,21},{6,22},{7,23},{8,24},{9,... | collective-permute-start | bytes 1179656 | tf_op jit(solution)/shard_map/ppermute | solution.py:544
  8.0 7.6 %collective-permute-start = (bf16[2,128,384]{2,1,0:T(8,128)(2,1)}, bf16[2,128,384]{2,1,0:T(8,128)(2,1)S(1)}, u32[]{:S(2)}, u32[]{:S(2)}) collective-permute-start(bf16[2,128,384]{2,1,0:T(8,128)(2,1)} %get-tuple-element.51), channel_id=1, source_target_pairs={{0,7},{1,4},{2,5},{3,6},{4,3},{5,0},{6,1},{7,2},{8,15},{9,12},{10,... | collective-permute-start | bytes 589832 | tf_op jit(solution)/shard_map/ppermute | solution.py:544
  10.5 18.9 %collective-permute-start.3 = (bf16[4,128,384]{2,1,0:T(8,128)(2,1)S(1)}, bf16[4,128,384]{2,1,0:T(8,128)(2,1)S(1)}, u32[]{:S(2)}, u32[]{:S(2)}) collective-permute-start(bf16[4,128,384]{2,1,0:T(8,128)(2,1)S(1)} %get-tuple-element.55), channel_id=1, source_target_pairs={{0,24},{1,25},{2,26},{3,27},{4,28},{5,29},{6,30},{7,31},{8,16},{9,... | collective-permute-start | bytes 1179656 | tf_op jit(solution)/shard_map/ppermute | solution.py:544
  11.0 14.6 %collective-permute-start.7 = (bf16[2,128,384]{2,1,0:T(8,128)(2,1)S(1)}, bf16[2,128,384]{2,1,0:T(8,128)(2,1)S(1)}, u32[]{:S(2)}, u32[]{:S(2)}) collective-permute-start(bf16[2,128,384]{2,1,0:T(8,128)(2,1)S(1)} %get-tuple-element.63), channel_id=1, source_target_pairs={{0,7},{1,4},{2,5},{3,6},{4,3},{5,0},{6,1},{7,2},{8,15},{9,12},{10,... | collective-permute-start | bytes 589832 | tf_op jit(solution)/shard_map/ppermute | solution.py:544
  15.6 0.8 %copy-start = (f32[1000,12]{0,1:T(8,128)S(1)}, f32[1000,12]{0,1:T(8,128)}, u32[]{:S(2)}) copy-start(f32[1000,12]{0,1:T(8,128)} %param.15) | copy-start | bytes 144004
  25.5 6.0 %collective-permute-start.5 = (bf16[2,2,128,384]{3,2,1,0:T(8,128)(2,1)S(1)}, bf16[2,2,128,384]{3,2,1,0:T(8,128)(2,1)S(1)}, u32[]{:S(2)}, u32[]{:S(2)}) collective-permute-start(bf16[2,2,128,384]{3,2,1,0:T(8,128)(2,1)S(1)} %stack.19), channel_id=1, source_target_pairs={{0,4},{4,0},{8,12},{12,8},{16,20},{20,16},{24,28},{28,24},{1,5},{5... | collective-permute-start | bytes 1179656 | tf_op jit(solution)/shard_map/ppermute | solution.py:548
  25.7 12.6 %collective-permute-start.8 = (bf16[2,2,128,384]{3,2,1,0:T(8,128)(2,1)S(1)}, bf16[2,2,128,384]{3,2,1,0:T(8,128)(2,1)S(1)}, u32[]{:S(2)}, u32[]{:S(2)}) collective-permute-start(bf16[2,2,128,384]{3,2,1,0:T(8,128)(2,1)S(1)} %stack.21), channel_id=1, source_target_pairs={{0,7},{1,4},{2,5},{3,6},{4,3},{5,0},{6,1},{7,2},{8,15},{9,12},{10,... | collective-permute-start | bytes 1179656 | tf_op jit(solution)/shard_map/ppermute | solution.py:544
  29.4 2.1 %collective-permute-start.4 = (bf16[2,128,384]{2,1,0:T(8,128)(2,1)S(1)}, bf16[2,128,384]{2,1,0:T(8,128)(2,1)S(1)}, u32[]{:S(2)}, u32[]{:S(2)}) collective-permute-start(bf16[2,128,384]{2,1,0:T(8,128)(2,1)S(1)} %get-tuple-element.56), channel_id=1, source_target_pairs={{0,4},{4,0},{8,12},{12,8},{16,20},{20,16},{24,28},{28,24},{1,5},{5... | collective-permute-start | bytes 589832 | tf_op jit(solution)/shard_map/ppermute | solution.py:548
  29.5 2.0 %collective-permute-start.6 = (bf16[2,128,384]{2,1,0:T(8,128)(2,1)S(1)}, bf16[2,128,384]{2,1,0:T(8,128)(2,1)S(1)}, u32[]{:S(2)}, u32[]{:S(2)}) collective-permute-start(bf16[2,128,384]{2,1,0:T(8,128)(2,1)S(1)} %stack.20), channel_id=1, source_target_pairs={{0,4},{4,0},{8,12},{12,8},{16,20},{20,16},{24,28},{28,24},{1,5},{5... | collective-permute-start | bytes 589832 | tf_op jit(solution)/shard_map/ppermute | solution.py:548
  30.0 8.3 %collective-permute-start.9 = (bf16[2,128,384]{2,1,0:T(8,128)(2,1)S(1)}, bf16[2,128,384]{2,1,0:T(8,128)(2,1)S(1)}, u32[]{:S(2)}, u32[]{:S(2)}) collective-permute-start(bf16[2,128,384]{2,1,0:T(8,128)(2,1)S(1)} %collective-permute-done.7.refs_3_), channel_id=1, source_target_pairs={{0,24},{1,25},{2,26},{3,27},{4,28},{5,29},{6,30},{7,31},{8,16},{9,... | collective-permute-start | bytes 589832 | tf_op jit(solution)/shard_map/ppermute | solution.py:544
  40.6 2.0 %collective-permute-start.10 = (f32[3,8,8,128]{3,2,1,0:T(8,128)S(1)}, f32[3,8,8,128]{3,2,1,0:T(8,128)S(1)}, u32[]{:S(2)}, u32[]{:S(2)}) collective-permute-start(f32[3,8,8,128]{3,2,1,0:T(8,128)S(1)} %get-tuple-element.64.stats), channel_id=1, source_target_pairs={{0,4},{4,0},{8,12},{12,8},{16,20},{20,16},{24,28},{28,24},{1,5},{5... | collective-permute-start | bytes 294920 | tf_op jit(solution)/shard_map/ppermute | solution.py:548
  44.9 18.2 %collective-permute-start.18 = (bf16[3,2,128,384]{3,2,1,0:T(8,128)(2,1)S(1)}, bf16[3,2,128,384]{3,2,1,0:T(8,128)(2,1)S(1)}, u32[]{:S(2)}, u32[]{:S(2)}) collective-permute-start(bf16[3,2,128,384]{3,2,1,0:T(8,128)(2,1)S(1)} %get-tuple-element.88), channel_id=1, source_target_pairs={{0,5},{1,6},{2,7},{3,4},{4,1},{5,2},{6,3},{7,0},{8,13},{9,14},{10,... | collective-permute-start | bytes 1769480 | tf_op jit(solution)/shard_map/ppermute | solution.py:544
  57.0 1.5 %collective-permute-start.11 = (bf16[2,128,384]{2,1,0:T(8,128)(2,1)S(1)}, bf16[2,128,384]{2,1,0:T(8,128)(2,1)S(1)}, u32[]{:S(2)}, u32[]{:S(2)}) collective-permute-start(bf16[2,128,384]{2,1,0:T(8,128)(2,1)S(1)} %get-tuple-element.74), channel_id=1, source_target_pairs={{0,4},{4,0},{8,12},{12,8},{16,20},{20,16},{24,28},{28,24},{1,5},{5... | collective-permute-start | bytes 589832 | tf_op jit(solution)/shard_map/ppermute | solution.py:548
  57.1 1.7 %collective-permute-start.12 = (bf16[2,128,384]{2,1,0:T(8,128)(2,1)S(1)}, bf16[2,128,384]{2,1,0:T(8,128)(2,1)S(1)}, u32[]{:S(2)}, u32[]{:S(2)}) collective-permute-start(bf16[2,128,384]{2,1,0:T(8,128)(2,1)S(1)} %get-tuple-element.76), channel_id=1, source_target_pairs={{0,4},{4,0},{8,12},{12,8},{16,20},{20,16},{24,28},{28,24},{1,5},{5... | collective-permute-start | bytes 589832 | tf_op jit(solution)/shard_map/ppermute | solution.py:548
  57.6 1.5 %collective-permute-start.13 = (bf16[2,128,384]{2,1,0:T(8,128)(2,1)S(1)}, bf16[2,128,384]{2,1,0:T(8,128)(2,1)S(1)}, u32[]{:S(2)}, u32[]{:S(2)}) collective-permute-start(bf16[2,128,384]{2,1,0:T(8,128)(2,1)S(1)} %get-tuple-element.78), channel_id=1, source_target_pairs={{0,4},{4,0},{8,12},{12,8},{16,20},{20,16},{24,28},{28,24},{1,5},{5... | collective-permute-start | bytes 589832 | tf_op jit(solution)/shard_map/ppermute | solution.py:548
  57.6 1.7 %collective-permute-start.14 = (bf16[2,128,384]{2,1,0:T(8,128)(2,1)S(1)}, bf16[2,128,384]{2,1,0:T(8,128)(2,1)S(1)}, u32[]{:S(2)}, u32[]{:S(2)}) collective-permute-start(bf16[2,128,384]{2,1,0:T(8,128)(2,1)S(1)} %get-tuple-element.80), channel_id=1, source_target_pairs={{0,4},{4,0},{8,12},{12,8},{16,20},{20,16},{24,28},{28,24},{1,5},{5... | collective-permute-start | bytes 589832 | tf_op jit(solution)/shard_map/ppermute | solution.py:548
  59.5 7.8 %collective-permute-start.15 = (bf16[2,128,384]{2,1,0:T(8,128)(2,1)S(1)}, bf16[2,128,384]{2,1,0:T(8,128)(2,1)S(1)}, u32[]{:S(2)}, u32[]{:S(2)}) collective-permute-start(bf16[2,128,384]{2,1,0:T(8,128)(2,1)S(1)} %get-tuple-element.82), channel_id=1, source_target_pairs={{0,8},{1,9},{2,10},{3,11},{4,12},{5,13},{6,14},{7,15},{8,0},{9,1},... | collective-permute-start | bytes 589832 | tf_op jit(solution)/shard_map/ppermute | solution.py:544
  59.6 10.0 %collective-permute-start.16 = (bf16[2,128,384]{2,1,0:T(8,128)(2,1)S(1)}, bf16[2,128,384]{2,1,0:T(8,128)(2,1)S(1)}, u32[]{:S(2)}, u32[]{:S(2)}) collective-permute-start(bf16[2,128,384]{2,1,0:T(8,128)(2,1)S(1)} %get-tuple-element.83), channel_id=1, source_target_pairs={{0,16},{1,17},{2,18},{3,19},{4,20},{5,21},{6,22},{7,23},{8,24},{9,... | collective-permute-start | bytes 589832 | tf_op jit(solution)/shard_map/ppermute | solution.py:544
  61.7 12.9 %collective-permute-start.17 = (bf16[2,128,384]{2,1,0:T(8,128)(2,1)S(1)}, bf16[2,128,384]{2,1,0:T(8,128)(2,1)S(1)}, u32[]{:S(2)}, u32[]{:S(2)}) collective-permute-start(bf16[2,128,384]{2,1,0:T(8,128)(2,1)S(1)} %get-tuple-element.84), channel_id=1, source_target_pairs={{0,24},{1,25},{2,26},{3,27},{4,28},{5,29},{6,30},{7,31},{8,16},{9,... | collective-permute-start | bytes 589832 | tf_op jit(solution)/shard_map/ppermute | solution.py:544
  63.2 12.8 %collective-permute-start.19 = (bf16[2,128,384]{2,1,0:T(8,128)(2,1)S(1)}, bf16[2,128,384]{2,1,0:T(8,128)(2,1)S(1)}, u32[]{:S(2)}, u32[]{:S(2)}) collective-permute-start(bf16[2,128,384]{2,1,0:T(8,128)(2,1)S(1)} %get-tuple-element.92), channel_id=1, source_target_pairs={{0,5},{1,6},{2,7},{3,4},{4,1},{5,2},{6,3},{7,0},{8,13},{9,14},{10,... | collective-permute-start | bytes 589832 | tf_op jit(solution)/shard_map/ppermute | solution.py:544
  63.3 12.8 %collective-permute-start.20 = (bf16[2,128,384]{2,1,0:T(8,128)(2,1)S(1)}, bf16[2,128,384]{2,1,0:T(8,128)(2,1)S(1)}, u32[]{:S(2)}, u32[]{:S(2)}) collective-permute-start(bf16[2,128,384]{2,1,0:T(8,128)(2,1)S(1)} %get-tuple-element.93), channel_id=1, source_target_pairs={{0,8},{1,9},{2,10},{3,11},{4,12},{5,13},{6,14},{7,15},{8,0},{9,1},... | collective-permute-start | bytes 589832 | tf_op jit(solution)/shard_map/ppermute | solution.py:544
  67.3 9.4 %collective-permute-start.21 = (bf16[2,128,384]{2,1,0:T(8,128)(2,1)S(1)}, bf16[2,128,384]{2,1,0:T(8,128)(2,1)S(1)}, u32[]{:S(2)}, u32[]{:S(2)}) collective-permute-start(bf16[2,128,384]{2,1,0:T(8,128)(2,1)S(1)} %get-tuple-element.94), channel_id=1, source_target_pairs={{0,16},{1,17},{2,18},{3,19},{4,20},{5,21},{6,22},{7,23},{8,24},{9,... | collective-permute-start | bytes 589832 | tf_op jit(solution)/shard_map/ppermute | solution.py:544
  69.6 10.7 %collective-permute-start.22 = (bf16[2,128,384]{2,1,0:T(8,128)(2,1)S(1)}, bf16[2,128,384]{2,1,0:T(8,128)(2,1)S(1)}, u32[]{:S(2)}, u32[]{:S(2)}) collective-permute-start(bf16[2,128,384]{2,1,0:T(8,128)(2,1)S(1)} %get-tuple-element.95), channel_id=1, source_target_pairs={{0,24},{1,25},{2,26},{3,27},{4,28},{5,29},{6,30},{7,31},{8,16},{9,... | collective-permute-start | bytes 589832 | tf_op jit(solution)/shard_map/ppermute | solution.py:544

commit v2 on v1

--- a/solution.py
+++ b/solution.py
@@ -38,7 +38,7 @@
 
 def pack_kernel(z, pos_ref, *refs):
     sources, refs = refs[:4], refs[4:]
-    outs, (pair, pair_rows, early, held, sems) = refs[: z.shards], refs[z.shards :]
+    outs, (pair, early, held, sems) = refs[: z.shards], refs[z.shards :]
     half, cols = z.tok // 2, z.own_heads * z.width
     copies = []
     for i, src in enumerate(sources):
@@ -54,8 +54,8 @@
             lanes = pl.ds(pl.multiple_of((pos_ref[0] ^ hop) * cols, 128), cols)
             part = held[i, :, lanes]
             outs[hop][i] = part
-            if hop == 0:
-                (pair if i < 2 else pair_rows)[i % 2] = part
+            if hop == 0 and i < 2:
+                pair[i] = part
             if hop == z.shards - 1 and i < 2:
                 early[i] = part
 
@@ -67,9 +67,9 @@
     results = pl.pallas_call(
         functools.partial(pack_kernel, z),
         out_shape=[shape((4, z.tok, cols), BF16)] * z.shards
-        + [shape((2, z.tok, cols), BF16)] * 3,
+        + [shape((2, z.tok, cols), BF16)] * 2,
         in_specs=[whole(SMEM)] + [whole(pltpu.HBM)] * 4,
-        out_specs=[whole(VMEM)] * (z.shards + 3),
+        out_specs=[whole(VMEM)] * (z.shards + 2),
         scratch_shapes=[
             VMEM((4, z.tok, cols * z.shards), BF16),
             pltpu.SemaphoreType.DMA((4, 2)),
@@ -77,7 +77,7 @@
         compiler_params=params(8),
         name="pack",
     )(pos, *sources)
-    return results[:-3], results[-3:]
+    return results[:-2], results[-2:]
 
 
 def bias_kernel(z, meta_ref, table_ref, after_ref, bias):
@@ -181,8 +181,9 @@
         base = 0 if self.batch == self.own_heads else pl.program_id(0) * self.batch
         return meta_ref[0] * self.own_heads + base
 
-    def steps(self, count):
-        return lax.div(count + 1, 2)
+    def blocks(self, count):
+        for steps in range(1, self.shards // 2 + 1):
+            yield 2 * steps * self.tok, lax.div(count + 1, 2) == steps
 
     def call(self, kernel, name, limit, operands, outs, scratch):
         split = self.batch != self.own_heads
@@ -223,69 +224,50 @@
 def order_tiles(z, tiles, ranks, kv, kt, vt):
     for ref, rank in zip(tiles, ranks):
         rows = pl.ds(pl.multiple_of(rank * z.tok, z.tok), z.tok)
-        half = pl.ds(pl.multiple_of(lax.rem(rank, 2) * z.tok, z.tok), z.tok)
         for h in range(z.batch):
             k, v = ref[0, :, z.lanes(h)], ref[1, :, z.lanes(h)]
             kv[h, rows, : z.width] = k
             kv[h, rows, z.width :] = v
-            kt[h, lax.div(rank, 2), :, half] = k.T
-            vt[h, lax.div(rank, 2), :, half] = v.T
-
-
-def softmax_sums(z, first, count, bias, kv, both, score, dprob):
-    heads, tok = range(z.batch), z.tok
+            kt[h, :, rows] = k.T
+            vt[h, :, rows] = v.T
+
+
+def softmax_sums(z, first, count, rows, bias, kv, both, score, dprob):
     scale = z.inv_root * LOG2E
-
-    def step(c, carry):
-        rows = pl.ds(pl.multiple_of(c * 2 * tok, 2 * tok), 2 * tok)
-        new = []
-        for h in heads:
-            sd = lax.dot_general(kv[h, rows, :], both[h][...], NT, preferred_element_type=F32)
-            parts = []
-            for j in range(2):
-                rank = 2 * c + j
-                shift = bias[rank, pl.ds(first + h, 1), :] + jnp.where(rank < count, 0.0, DEAD)
-                parts.append(sd[j * tok : (j + 1) * tok, :tok] * scale + shift)
-            s, dp = jnp.concatenate(parts, axis=0), sd[:, tok:]
-            score[h][c] = s
-            dprob[h][c] = dp
-            old, total, mixed = carry[3 * h : 3 * h + 3]
-            peak = jnp.maximum(old, fold(jnp.max, s))
-            e = jnp.exp2(s.reshape(-1, 8, tok) - peak[None])
-            fade = jnp.exp2(old - peak)
-            new += [
-                peak,
-                total * fade + jnp.sum(e, axis=0),
-                mixed * fade + jnp.sum(e * dp.reshape(-1, 8, tok), axis=0),
-            ]
-        return tuple(new)
-
-    start = (jnp.full((8, tok), -3e38, F32), jnp.zeros((8, tok), F32), jnp.zeros((8, tok), F32))
-    sums = lax.fori_loop(0, z.steps(count), step, start * z.batch)
-    peaks = [jnp.max(x, axis=0, keepdims=True) for x in sums[::3]]
-    fades = [jnp.exp2(x - peak) for x, peak in zip(sums[::3], peaks)]
-    totals, mixed = (
-        [jnp.sum(x * fade, axis=0, keepdims=True) for x, fade in zip(sums[i::3], fades)]
-        for i in (1, 2)
-    )
-    return peaks, totals, mixed
-
-
-def gradients(z, count, log_total, delta, score, dprob, both, kt, vt, acc, ot, dqt):
-    def grad_step(c, carry):
-        rows = pl.ds(pl.multiple_of(c * 2 * z.tok, 2 * z.tok), 2 * z.tok)
-        for h in range(z.batch):
-            w = jnp.exp2(score[h][c] - log_total[h])
-            ds = (w * (dprob[h][c] - delta[h])).astype(BF16)
-            w = w.astype(BF16)
-            acc[h, rows, :] += jnp.dot(
-                jnp.concatenate([ds, w], axis=1), both[h][...], preferred_element_type=F32
+    sums = []
+    for h in range(z.batch):
+        sd = lax.dot_general(kv[h, :rows, :], both[h][...], NT, preferred_element_type=F32)
+        parts = []
+        for rank in range(rows // z.tok):
+            shift = bias[rank, pl.ds(first + h, 1), :] + jnp.where(rank < count, 0.0, DEAD)
+            parts.append(sd[rank * z.tok : (rank + 1) * z.tok, : z.tok] * scale + shift)
+        s, dp = jnp.concatenate(parts, axis=0), sd[:, z.tok :]
+        score[h][:rows, :] = s
+        dprob[h][:rows, :] = dp
+        peak = jnp.max(fold(jnp.max, s), axis=0, keepdims=True)
+        e = jnp.exp2(s - peak)
+        total = jnp.sum(fold(jnp.sum, e), axis=0, keepdims=True)
+        mixed = jnp.sum(fold(jnp.sum, e * dp), axis=0, keepdims=True)
+        sums.append((peak, total, mixed))
+    return [[x[i] for x in sums] for i in range(3)]
+
+
+def gradients(z, rows, log_total, delta, score, dprob, both, kt, vt, acc):
+    found = []
+    for h in range(z.batch):
+        w = jnp.exp2(score[h][:rows, :] - log_total[h])
+        ds = (w * (dprob[h][:rows, :] - delta[h])).astype(BF16)
+        w = w.astype(BF16)
+        acc[h, :rows, :] += jnp.dot(
+            jnp.concatenate([ds, w], axis=1), both[h][...], preferred_element_type=F32
+        )
+        found.append(
+            (
+                jnp.dot(vt[h, :, :rows], w, preferred_element_type=F32),
+                jnp.dot(kt[h, :, :rows], ds, preferred_element_type=F32),
             )
-            ot[h][...] += jnp.dot(vt[h, c], w, preferred_element_type=F32)
-            dqt[h][...] += jnp.dot(kt[h, c], ds, preferred_element_type=F32)
-        return carry
-
-    lax.fori_loop(0, z.steps(count), grad_step, 0)
+        )
+    return found
 
 
 def write_sums(z, goals, ranks, acc):
@@ -332,19 +314,27 @@
                     both[h, at, pl.ds(i * z.tok, z.tok), z.lanes(j)] = (
                         block if i == j else jnp.zeros_like(block)
                     )
-        sums = softmax_sums(
-            z,
-            first,
-            count,
-            ranked,
-            kv,
-            [both.at[h, at] for h in heads],
-            [score.at[h, at] for h in heads],
-            [dprob.at[h, at] for h in heads],
-        )
         for h in heads:
             for i in range(3):
-                stats[h, at, i : i + 1, :] = sums[i][h]
+                stats[h, at, i : i + 1, :] = jnp.full((1, z.tok), 0.0 if i else -3e38, F32)
+        for rows, needed in z.blocks(count):
+
+            @pl.when(needed)
+            def _():
+                sums = softmax_sums(
+                    z,
+                    first,
+                    count,
+                    rows,
+                    ranked,
+                    kv,
+                    [both.at[h, at] for h in heads],
+                    [score.at[h, at] for h in heads],
+                    [dprob.at[h, at] for h in heads],
+                )
+                for h in heads:
+                    for i in range(3):
+                        stats[h, at, i : i + 1, :] = sums[i][h]
 
 
 def ahead_kernel(z, meta_ref, bias, both, stats, *refs):
@@ -358,22 +348,25 @@
     for at, count, live in z.queries(meta_ref, True):
         merged[:, at] = stats[:, at]
 
-        @pl.when(live == 1)
-        def _():
-            far = softmax_sums(
-                z,
-                first,
-                count,
-                ranked,
-                kv,
-                [both.at[h, at] for h in heads],
-                [score.at[h, at] for h in heads],
-                [dprob.at[h, at] for h in heads],
-            )
-            sums = merge_sums([read_sums(stats, heads, at), far])
-            for h in heads:
-                for i in range(3):
-                    merged[h, at, i : i + 1, :] = sums[h][i]
+        for rows, needed in z.blocks(count):
+
+            @pl.when(needed & (live == 1))
+            def _():
+                far = softmax_sums(
+                    z,
+                    first,
+                    count,
+                    rows,
+                    ranked,
+                    kv,
+                    [both.at[h, at] for h in heads],
+                    [score.at[h, at] for h in heads],
+                    [dprob.at[h, at] for h in heads],
+                )
+                sums = merge_sums([read_sums(stats, heads, at), far])
+                for h in heads:
+                    for i in range(3):
+                        merged[h, at, i : i + 1, :] = sums[h][i]
 
 
 def back_kernel(z, meta_ref, both, stats, kt, vt, score, dprob, *refs):
@@ -381,8 +374,6 @@
     final, ot, dqt, own_sums, sums, acc = refs
     heads = range(z.batch)
     acc[...] = jnp.zeros_like(acc)
-    ot[...] = jnp.zeros_like(ot)
-    dqt[...] = jnp.zeros_like(dqt)
     for at, count, live in z.queries(meta_ref, True):
         parts = [read_sums(stats, heads, at)]
         for turn, other in enumerate(others, 1):
@@ -395,54 +386,79 @@
             final[h, at, 0:1, :] = log_total[h]
             final[h, at, 1:2, :] = delta[h]
 
-        @pl.when(live == 1)
+        for rows, needed in z.blocks(count):
+
+            @pl.when(needed & (live == 1))
+            def _():
+                found = gradients(
+                    z,
+                    rows,
+                    log_total,
+                    delta,
+                    [score.at[h, at] for h in heads],
+                    [dprob.at[h, at] for h in heads],
+                    [both.at[h, at] for h in heads],
+                    kt,
+                    vt,
+                    acc,
+                )
+                for h in heads:
+                    ot[h, at], dqt[h, at] = found[h]
+
+        @pl.when((count == 0) | (live != 1))
         def _():
-            gradients(
-                z,
-                count,
-                log_total,
-                delta,
-                [score.at[h, at] for h in heads],
-                [dprob.at[h, at] for h in heads],
-                [both.at[h, at] for h in heads],
-                kt,
-                vt,
-                acc,
-                [ot.at[h, at] for h in heads],
-                [dqt.at[h, at] for h in heads],
-            )
+            ot[:, at] = jnp.zeros_like(ot[:, at])
+            dqt[:, at] = jnp.zeros_like(dqt[:, at])
 
     goals = [own_sums] + [sums.at[i] for i in range(z.shards - 1)]
     write_sums(z, goals, z.ranks(meta_ref, True)[1], acc)
 
 
-def rows_kernel(z, meta_ref, kt, vt, both, score, dprob, final, ot_in, dqt_in, *refs):
-    rows_out, refs = refs[1 : 1 + z.groups], refs[1 + z.groups :]
-    sums, (acc, ot, dqt) = refs[: z.shards], refs[z.shards :]
+def rows_kernel(z, meta_ref, kt, vt, both, score, dprob, final, ot_in, dqt_in, *refs, mine):
     heads = range(z.batch)
-    acc[...] = jnp.zeros_like(acc)
+    if mine:
+        acc_in, rows_out, sums, acc = refs[1], refs[2 : 2 + z.shards], refs[2 + z.shards : -1], refs[-1]
+        acc[...] = acc_in[...]
+    else:
+        rows_out, acc = refs[1:-1], refs[-1]
+        acc[...] = jnp.zeros_like(acc)
     for at, count, _ in z.queries(meta_ref, False):
-        for h in heads:
-            ot[h] = ot_in[h, at]
-            dqt[h] = dqt_in[h, at]
-        gradients(
-            z,
-            count,
-            [final[h, at, 0:1, :] for h in heads],
-            [final[h, at, 1:2, :] for h in heads],
-            [score.at[h, at] for h in heads],
-            [dprob.at[h, at] for h in heads],
-            [both.at[h, at] for h in heads],
-            kt,
-            vt,
-            acc,
-            [ot.at[h] for h in heads],
-            [dqt.at[h] for h in heads],
-        )
-        for h in heads:
-            rows_out[at][0, :, z.lanes(h)] = ot[h].astype(BF16).T
-            rows_out[at][1, :, z.lanes(h)] = (dqt[h] * z.inv_root).astype(BF16).T
-    write_sums(z, sums, z.ranks(meta_ref, False)[1], acc)
+        if mine != (at < z.shards):
+            continue
+        log_total = [final[h, at, 0:1, :] for h in heads]
+        delta = [final[h, at, 1:2, :] for h in heads]
+
+        def write(h, out, dq):
+            goal = rows_out[at if mine else at - z.shards]
+            goal[0, :, z.lanes(h)] = out.astype(BF16).T
+            goal[1, :, z.lanes(h)] = (dq * z.inv_root).astype(BF16).T
+
+        for rows, needed in z.blocks(count):
+
+            @pl.when(needed)
+            def _():
+                found = gradients(
+                    z,
+                    rows,
+                    log_total,
+                    delta,
+                    [score.at[h, at] for h in heads],
+                    [dprob.at[h, at] for h in heads],
+                    [both.at[h, at] for h in heads],
+                    kt,
+                    vt,
+                    acc,
+                )
+                for h in heads:
+                    write(h, ot_in[h, at] + found[h][0], dqt_in[h, at] + found[h][1])
+
+        @pl.when(count == 0)
+        def _():
+            for h in heads:
+                write(h, ot_in[h, at], dqt_in[h, at])
+
+    if mine:
+        write_sums(z, sums, z.ranks(meta_ref, False)[1], acc)
 
 
 def add_up(terms, at=()):
@@ -562,19 +578,18 @@
 
     hops = list(range(shards))
     last = shards - 1
-    packed, (pair, pair_rows, early) = pack(z, pos, (keys, values, queries, grad_out))
+    packed, (pair, early) = pack(z, pos, (keys, values, queries, grad_out))
     full = [to_shard(packed[hop], hop, 0) for hop in hops]
     far_first, far_last = to_shard(pair, 0, -1), to_shard(early, 0, -1)
     bias = bias_rows(z, meta, level_bias.T, far_first)
     direct = stack(full[1:last], 0, (far_first, far_last, bias))
     far = [far_first, to_shard(direct, 0, -1), to_shard(far_last, last, 0)]
-    rows = swapped([pair_rows, stack(full[1:last], 2, (bias,)), stack(full[last:], 2, flat=True)])
+    rows = swapped([stack(full[:1], 2, flat=True), stack(full[1:last], 2, (bias,)), stack(full[last:], 2, flat=True)])
 
     scalars = [(meta, "scalar")]
-    half = shards // 2
     one = shape((2, tok, cols), BF16)
-    square = shape((own, half, width, 2 * tok), BF16)
-    block = shape((own, groups, half, 2 * tok, tok), F32)
+    square = shape((own, width, shards * tok), BF16)
+    block = shape((own, groups, shards * tok, tok), F32)
     stat = shape((own, groups, 8, tok), F32)
     part = shape((own, groups, width, tok), F32)
     batch = z.batch
@@ -630,19 +645,27 @@
         [sums_scratch],
     )
     far_home = to_shard(far_sums, 0, 1)
+    operands = scalars + [(x, "heads") for x in (kt, vt, both, score, dprob, final, ot, dqt)]
+    *rows_others, partial_sums = z.call(
+        functools.partial(rows_kernel, mine=False),
+        "rows_others",
+        limit,
+        operands + [(first_sums, "lanes")],
+        [(one, "lanes")] * (groups - shards)
+        + [(shape((own, shards * tok, 2 * width), F32), "heads")],
+        [],
+    )
     results = z.call(
-        rows_kernel,
+        functools.partial(rows_kernel, mine=True),
         "rows",
         limit,
-        scalars
-        + [(x, "heads") for x in (kt, vt, both, score, dprob, final, ot, dqt)]
-        + [(first_sums, "lanes")],
-        [(one, "lanes")] * (groups + shards),
-        [sums_scratch, VMEM((batch, width, tok), F32), VMEM((batch, width, tok), F32)],
+        operands + [(first_sums, "lanes"), (partial_sums, "heads")],
+        [(one, "lanes")] * (2 * shards),
+        [sums_scratch],
     )
-    row_sums = add(with_others(results[:groups]))
+    row_sums = add(with_others([*results[:shards], *rows_others]))
     rows_home = [to_shard(row_sums[hop], hop, 0) for hop in hops]
-    near_sums = results[groups:]
+    near_sums = results[shards:]
     *sums, first_late = merge([[x] for x in near_sums[1:]], far_home, [first_sums])
     sums_home = [to_shard(x, hop, 0) for hop, x in zip(hops[1:], sums)]
     first_home = to_shard(first_late, 0, 1)

time: 82.8 us -> 77.2 us (0.932); the launches traced: 81.8 us -> 78.6 us
  starting transfers between devices: 31.5 us -> 23.4 us
  waiting for transfers between devices: 22.3 us -> 26.8 us
    ppermute x15, starting transfers between devices: 28.8 us -> 21.5 us  [to_shard(): return lax.ppermute(x, ('tm', 'tile'), pairs)]
    ppermute x15, waiting for transfers between devices: 20 us -> 25.5 us  [to_shard(): return lax.ppermute(x, ('tm', 'tile'), pairs)]
    pallas_call x4 -> x5, Pallas kernels: 18.7 us -> 19.6 us  [call(): pl.pallas_call(functools.partial(kernel, self), grid=(self.own_heads // s...]
    ppermute x8, waiting for transfers between devices: 2.21 us -> 1.31 us  [to_replica(): return lax.ppermute(x, 'tm', pairs)]
    ppermute x8, starting transfers between devices: 2.76 us -> 1.86 us  [to_replica(): return lax.ppermute(x, 'tm', pairs)]
  transfers between devices with their start and end apart: 23 -> 23, of which waited for: 11 -> 9; matrix products, arithmetic and copies ran while one was open for 1% -> 1% of each run, Pallas kernels for 20% -> 17%
where the time goes in v2:
time: 77.2 us; the launch traced here: 78.6 us
  waiting for transfers between devices  26.8 us (35%)
  Pallas kernels  25.9 us (34%)
  starting transfers between devices  23.4 us (30%)
  local copies, waits for them, and re-layouts  1.6 us (2%)
  between operations  0.86 us (1%)
    ppermute x15, waiting for transfers between devices, to_shard(): return lax.ppermute(x, ('tm', 'tile'), pairs)  25.5 us
    ppermute x15, starting transfers between devices, to_shard(): return lax.ppermute(x, ('tm', 'tile'), pairs)  21.5 us
    pallas_call x5, Pallas kernels, call(): pl.pallas_call(functools.partial(kernel, self), grid=(self.own_heads // s...  19.6 us
    pallas_call x2, Pallas kernels, unpack(): pl.pallas_call(kernel, out_shape=[jax.ShapeDtypeStruct((tok, cols * shard...  2.99 us
    pallas_call x1, Pallas kernels, pack(): pl.pallas_call(functools.partial(pack_kernel, z), out_shape=[shape((4, z....  2.1 us
    ppermute x8, starting transfers between devices, to_replica(): return lax.ppermute(x, 'tm', pairs)  1.86 us
  transfers between devices with their start and end apart: 23, of which 9 were waited for; matrix products, arithmetic and copies ran while one was open for 1% of the time, Pallas kernels for 17%

profile of v2, /device:TPU:0, one launch (start us, length us, event | category | flops | bytes accessed | tf_op | source)
XLA Modules:
  0.0 78.6 jit_solution(17385299306020459104)
XLA Ops:
  0.7 2.1 %pack.1 = (bf16[4,128,384]{2,1,0:T(8,128)(2,1)S(1)}, bf16[4,128,384]{2,1,0:T(8,128)(2,1)S(1)}, bf16[4,128,384]{2,1,0:T(8,128)(2,1)S(1)}, bf16[4,128,384]{2,1,0:T...) custom-call(s32[3]{0:T(128)S(1)} %pad_add_fusion.pos_ref, ...), custom_call_target="tpu_custom_call" | custom-call | tf_op jit(solution)/shard_map/pack/pallas_call | solution.py:67
  2.8 3.0 %collective-permute-start.1 = (bf16[4,128,384]{2,1,0:T(8,128)(2,1)S(1)}, bf16[4,128,384]{2,1,0:T(8,128)(2,1)S(1)}, u32[]{:S(2)}, u32[]{:S(2)}) collective-permute-start(bf16[4,128,384]{2,1,0:T(8,128)(2,1)S(1)} %get-tuple-element.53), channel_id=1, source_target_pairs={{0,8},{1,9},{2,10},{3,11},{4,12},{5,13},{6,14},{7,15},{8,0},{9,1},... | collective-permute-start | bytes 1179656 | tf_op jit(solution)/shard_map/ppermute | solution.py:560
  5.8 1.5 %collective-permute-start.2 = (bf16[4,128,384]{2,1,0:T(8,128)(2,1)S(1)}, bf16[4,128,384]{2,1,0:T(8,128)(2,1)S(1)}, u32[]{:S(2)}, u32[]{:S(2)}) collective-permute-start(bf16[4,128,384]{2,1,0:T(8,128)(2,1)S(1)} %get-tuple-element.54), channel_id=1, source_target_pairs={{0,16},{1,17},{2,18},{3,19},{4,20},{5,21},{6,22},{7,23},{8,24},{9,... | collective-permute-start | bytes 1179656 | tf_op jit(solution)/shard_map/ppermute | solution.py:560
  7.4 2.5 %collective-permute-start = (bf16[2,128,384]{2,1,0:T(8,128)(2,1)S(1)}, bf16[2,128,384]{2,1,0:T(8,128)(2,1)S(1)}, u32[]{:S(2)}, u32[]{:S(2)}) collective-permute-start(bf16[2,128,384]{2,1,0:T(8,128)(2,1)S(1)} %get-tuple-element.51), channel_id=1, source_target_pairs={{0,7},{1,4},{2,5},{3,6},{4,3},{5,0},{6,1},{7,2},{8,15},{9,12},{10,... | collective-permute-start | bytes 589832 | tf_op jit(solution)/shard_map/ppermute | solution.py:560
  12.1 2.6 %collective-permute-done.after_ref.refs_0_.refs_2_ = bf16[2,128,384]{2,1,0:T(8,128)(2,1)S(1)} collective-permute-done((bf16[2,128,384]{2,1,0:T(8,128)(2,1)S(1)}, bf16[2,128,384]{2,1,0:T(8,128)(2,1)S(1)}, u32[]{:S(2)}, u32[]{:S(2)}) %collective-permute-start) | collective-permute-done | bytes 196640 | tf_op jit(solution)/shard_map/ppermute | solution.py:560
  16.2 8.7 %collective-permute-done.2.refs_1_.refs_2_ = bf16[4,128,384]{2,1,0:T(8,128)(2,1)S(1)} collective-permute-done((bf16[4,128,384]{2,1,0:T(8,128)(2,1)S(1)}, bf16[4,128,384]{2,1,0:T(8,128)(2,1)S(1)}, u32[]{:S(2)}, u32[]{:S(2)}) %collective-permute-start.2) | collective-permute-done | bytes 393248 | tf_op jit(solution)/shard_map/ppermute | solution.py:560
  25.0 3.7 %collective-permute-start.8 = (bf16[2,2,128,384]{3,2,1,0:T(8,128)(2,1)S(1)}, bf16[2,2,128,384]{3,2,1,0:T(8,128)(2,1)S(1)}, u32[]{:S(2)}, u32[]{:S(2)}) collective-permute-start(bf16[2,2,128,384]{3,2,1,0:T(8,128)(2,1)S(1)} %stack.23), channel_id=1, source_target_pairs={{0,7},{1,4},{2,5},{3,6},{4,3},{5,0},{6,1},{7,2},{8,15},{9,12},{10,... | collective-permute-start | bytes 1179656 | tf_op jit(solution)/shard_map/ppermute | solution.py:560
  29.4 1.5 %collective-permute-start.9 = (bf16[2,128,384]{2,1,0:T(8,128)(2,1)S(1)}, bf16[2,128,384]{2,1,0:T(8,128)(2,1)S(1)}, u32[]{:S(2)}, u32[]{:S(2)}) collective-permute-start(bf16[2,128,384]{2,1,0:T(8,128)(2,1)S(1)} %collective-permute-done.7.refs_3_), channel_id=1, source_target_pairs={{0,24},{1,25},{2,26},{3,27},{4,28},{5,29},{6,30},{7,31},{8,16},{9,... | collective-permute-start | bytes 589832 | tf_op jit(solution)/shard_map/ppermute | solution.py:560
  31.0 4.9 %own.1 = (bf16[3,128,512]{2,1,0:T(8,128)(2,1)S(1)}, bf16[3,128,512]{2,1,0:T(8,128)(2,1)S(1)}, bf16[3,8,256,256]{3,2,1,0:T(8,128)(2,1)S(1)}, f32[3,8,512,128]{3,2...) custom-call(s32[51]{0:T(128)S(1)} %concatenate.4.meta_ref, ...), custom_call_target="tpu_custom_call" | custom-call | tf_op jit(solution)/shard_map/own/pallas_call | solution.py:204
  35.9 1.4 %collective-permute-done.9.refs_0_ = bf16[2,128,384]{2,1,0:T(8,128)(2,1)S(1)} collective-permute-done((bf16[2,128,384]{2,1,0:T(8,128)(2,1)S(1)}, bf16[2,128,384]{2,1,0:T(8,128)(2,1)S(1)}, u32[]{:S(2)}, u32[]{:S(2)}) %collective-permute-start.9) | collective-permute-done | bytes 196640 | tf_op jit(solution)/shard_map/ppermute | solution.py:560
  37.6 4.3 %ahead.1 = (f32[3,8,8,128]{3,2,1,0:T(8,128)S(1)}, bf16[3,128,512]{2,1,0:T(8,128)(2,1)S(1)}, bf16[3,128,512]{2,1,0:T(8,128)(2,1)S(1)}, f32[3,8,512,128]{3,2,1,0:T(8,128)S(1)}, f32[3,8,512,128]{3,2,1,0:T(8,128)S(1)}) custom-call(s32[51]{0:T(128)S(1)} %concatenate.4.meta_ref, f32[8,12,128]{2,1,0:T(8,128)S(1)} %bias.1.refs_2_.refs_4_, ...), custom_call_target="tpu_custom_call" | custom-call | tf_op jit(solution)/shard_map/ahead/pallas_call | solution.py:204
  43.3 4.2 %back.1 = (f32[3,8,8,128]{3,2,1,0:T(8,128)S(1)}, f32[3,8,128,128]{3,2,1,0:T(8,128)S(1)}, f32[3,8,128,128]{3,2,1,0:T(8,128)S(1)}, bf16[2,128,384]{2,1,0:T(8,128)(2,1)S(1)}, bf16[3,2,128,384]{3,2,1,0:T(8,128)(2,1)S(1)}) custom-call(s32[51]{0:T(128)S(1)} %concatenate.4.meta_ref, bf16[3,8,256,256]{3,2,1,0:T(8,128)(2,1)S(1)} %get-tuple-element.58.both, ...), custom_call_target="tpu_custom_call" | custom-call | tf_op jit(solution)/shard_map/back/pallas_call | solution.py:204
  47.6 3.1 %rows_others.1 = (bf16[2,128,384]{2,1,0:T(8,128)(2,1)S(1)}, bf16[2,128,384]{2,1,0:T(8,128)(2,1)S(1)}, bf16[2,128,384]{2,1,0:T(8,128)(2,1)S(1)}, bf16[2,128,384]{2,1,0:T(8,128)(2,1)S(1)}, f32[3,512,256]{2,1,0:T(8,128)S(1)}) custom-call(s32[51]{0:T(128)S(1)} %concatenate.4.meta_ref, bf16[3,128,512]{2,1,0:T(8,128)(2,1)S(1)} %get-tuple-element.56.kt, ...), custom_call_target="tpu_custom_call" | custom-call | tf_op jit(solution)/shard_map/rows_others/pallas_call | solution.py:204
  51.7 3.1 %rows.1 = (bf16[2,128,384]{2,1,0:T(8,128)(2,1)S(1)}, bf16[2,128,384]{2,1,0:T(8,128)(2,1)S(1)}, bf16[2,128,384]{2,1,0:T(8,128)(2,1)S(1)}, bf16[2,128,384]{2,1,0:T...) custom-call(s32[51]{0:T(128)S(1)} %concatenate.4.meta_ref, ...), custom_call_target="tpu_custom_call" | custom-call | tf_op jit(solution)/shard_map/rows/pallas_call | solution.py:204
  55.2 2.0 %collective-permute-start.16 = (bf16[2,128,384]{2,1,0:T(8,128)(2,1)S(1)}, bf16[2,128,384]{2,1,0:T(8,128)(2,1)S(1)}, u32[]{:S(2)}, u32[]{:S(2)}) collective-permute-start(bf16[2,128,384]{2,1,0:T(8,128)(2,1)S(1)} %get-tuple-element.83), channel_id=1, source_target_pairs={{0,16},{1,17},{2,18},{3,19},{4,20},{5,21},{6,22},{7,23},{8,24},{9,... | collective-permute-start | bytes 589832 | tf_op jit(solution)/shard_map/ppermute | solution.py:560
  57.2 1.5 %collective-permute-start.17 = (bf16[2,128,384]{2,1,0:T(8,128)(2,1)S(1)}, bf16[2,128,384]{2,1,0:T(8,128)(2,1)S(1)}, u32[]{:S(2)}, u32[]{:S(2)}) collective-permute-start(bf16[2,128,384]{2,1,0:T(8,128)(2,1)S(1)} %get-tuple-element.84), channel_id=1, source_target_pairs={{0,24},{1,25},{2,26},{3,27},{4,28},{5,29},{6,30},{7,31},{8,16},{9,... | collective-permute-start | bytes 589832 | tf_op jit(solution)/shard_map/ppermute | solution.py:560
  58.7 5.9 %collective-permute-done.18.refs_0_ = bf16[3,2,128,384]{3,2,1,0:T(8,128)(2,1)S(1)} collective-permute-done((bf16[3,2,128,384]{3,2,1,0:T(8,128)(2,1)S(1)}, bf16[3,2,128,384]{3,2,1,0:T(8,128)(2,1)S(1)}, u32[]{:S(2)}, u32[]{:S(2)}) %collective-permute-start.18) | collective-permute-done | bytes 589856 | tf_op jit(solution)/shard_map/ppermute | solution.py:560
  64.9 2.0 %collective-permute-start.21 = (bf16[2,128,384]{2,1,0:T(8,128)(2,1)S(1)}, bf16[2,128,384]{2,1,0:T(8,128)(2,1)S(1)}, u32[]{:S(2)}, u32[]{:S(2)}) collective-permute-start(bf16[2,128,384]{2,1,0:T(8,128)(2,1)S(1)} %get-tuple-element.94), channel_id=1, source_target_pairs={{0,16},{1,17},{2,18},{3,19},{4,20},{5,21},{6,22},{7,23},{8,24},{9,... | collective-permute-start | bytes 589832 | tf_op jit(solution)/shard_map/ppermute | solution.py:560
  66.9 2.1 %collective-permute-start.22 = (bf16[2,128,384]{2,1,0:T(8,128)(2,1)S(1)}, bf16[2,128,384]{2,1,0:T(8,128)(2,1)S(1)}, u32[]{:S(2)}, u32[]{:S(2)}) collective-permute-start(bf16[2,128,384]{2,1,0:T(8,128)(2,1)S(1)} %get-tuple-element.95), channel_id=1, source_target_pairs={{0,24},{1,25},{2,26},{3,27},{4,28},{5,29},{6,30},{7,31},{8,16},{9,... | collective-permute-start | bytes 589832 | tf_op jit(solution)/shard_map/ppermute | solution.py:560
  69.0 1.5 %unpack.2 = (bf16[128,1536]{1,0:T(8,128)(2,1)}, bf16[128,1536]{1,0:T(8,128)(2,1)}) custom-call(s32[3]{0:T(128)S(1)} %pad_add_fusion.pos_ref, bf16[2,128,384]{2,1,0:T(8,128)(2,1)S(1)} %get-tuple-element.81.refs_0_, bf16[2,128,384]{2,1,0:T(8,128)(2,1)S(1)} %collective-permute-done.15.refs_1_, bf16[2,128,384]{2,1,0:T(8,128)(2,1)S(1)} %collective-permute-done.16.refs_2_, ...), custom_call_target="tpu_custom_call" | custom-call | tf_op jit(solution)/shard_map/unpack/pallas_call | solution.py:526
  70.5 3.0 %collective-permute-done.19.refs_1_ = bf16[2,128,384]{2,1,0:T(8,128)(2,1)S(1)} collective-permute-done((bf16[2,128,384]{2,1,0:T(8,128)(2,1)S(1)}, bf16[2,128,384]{2,1,0:T(8,128)(2,1)S(1)}, u32[]{:S(2)}, u32[]{:S(2)}) %collective-permute-start.19) | collective-permute-done | bytes 196640 | tf_op jit(solution)/shard_map/ppermute | solution.py:560
  73.5 1.9 %collective-permute-done.21.refs_3_ = bf16[2,128,384]{2,1,0:T(8,128)(2,1)S(1)} collective-permute-done((bf16[2,128,384]{2,1,0:T(8,128)(2,1)S(1)}, bf16[2,128,384]{2,1,0:T(8,128)(2,1)S(1)}, u32[]{:S(2)}, u32[]{:S(2)}) %collective-permute-start.21) | collective-permute-done | bytes 196640 | tf_op jit(solution)/shard_map/ppermute | solution.py:560
  75.4 1.6 %collective-permute-done.22.refs_4_ = bf16[2,128,384]{2,1,0:T(8,128)(2,1)S(1)} collective-permute-done((bf16[2,128,384]{2,1,0:T(8,128)(2,1)S(1)}, bf16[2,128,384]{2,1,0:T(8,128)(2,1)S(1)}, u32[]{:S(2)}, u32[]{:S(2)}) %collective-permute-start.22) | collective-permute-done | bytes 196640 | tf_op jit(solution)/shard_map/ppermute | solution.py:560
  77.1 1.5 %unpack.3 = (bf16[128,1536]{1,0:T(8,128)(2,1)}, bf16[128,1536]{1,0:T(8,128)(2,1)}) custom-call(s32[3]{0:T(128)S(1)} %pad_add_fusion.pos_ref, bf16[2,128,384]{2,1,0:T(8,128)(2,1)S(1)} %get-tuple-element.87.refs_0_, bf16[2,128,384]{2,1,0:T(8,128)(2,1)S(1)} %collective-permute-done.19.refs_1_, bf16[2,128,384]{2,1,0:T(8,128)(2,1)S(1)} %collective-permute-done.20.refs_2_, ...), custom_call_target="tpu_custom_call" | custom-call | tf_op jit(solution)/shard_map/unpack/pallas_call | solution.py:526
  (44 shorter events, 8.1 us)
Async XLA Ops:
  2.8 13.3 %collective-permute-start.1 = (bf16[4,128,384]{2,1,0:T(8,128)(2,1)S(1)}, bf16[4,128,384]{2,1,0:T(8,128)(2,1)S(1)}, u32[]{:S(2)}, u32[]{:S(2)}) collective-permute-start(bf16[4,128,384]{2,1,0:T(8,128)(2,1)S(1)} %get-tuple-element.53), channel_id=1, source_target_pairs={{0,8},{1,9},{2,10},{3,11},{4,12},{5,13},{6,14},{7,15},{8,0},{9,1},... | collective-permute-start | bytes 1179656 | tf_op jit(solution)/shard_map/ppermute | solution.py:560
  5.8 19.0 %collective-permute-start.2 = (bf16[4,128,384]{2,1,0:T(8,128)(2,1)S(1)}, bf16[4,128,384]{2,1,0:T(8,128)(2,1)S(1)}, u32[]{:S(2)}, u32[]{:S(2)}) collective-permute-start(bf16[4,128,384]{2,1,0:T(8,128)(2,1)S(1)} %get-tuple-element.54), channel_id=1, source_target_pairs={{0,16},{1,17},{2,18},{3,19},{4,20},{5,21},{6,22},{7,23},{8,24},{9,... | collective-permute-start | bytes 1179656 | tf_op jit(solution)/shard_map/ppermute | solution.py:560
  7.4 7.3 %collective-permute-start = (bf16[2,128,384]{2,1,0:T(8,128)(2,1)S(1)}, bf16[2,128,384]{2,1,0:T(8,128)(2,1)S(1)}, u32[]{:S(2)}, u32[]{:S(2)}) collective-permute-start(bf16[2,128,384]{2,1,0:T(8,128)(2,1)S(1)} %get-tuple-element.51), channel_id=1, source_target_pairs={{0,7},{1,4},{2,5},{3,6},{4,3},{5,0},{6,1},{7,2},{8,15},{9,12},{10,... | collective-permute-start | bytes 589832 | tf_op jit(solution)/shard_map/ppermute | solution.py:560
  9.8 19.0 %collective-permute-start.3 = (bf16[4,128,384]{2,1,0:T(8,128)(2,1)S(1)}, bf16[4,128,384]{2,1,0:T(8,128)(2,1)S(1)}, u32[]{:S(2)}, u32[]{:S(2)}) collective-permute-start(bf16[4,128,384]{2,1,0:T(8,128)(2,1)S(1)} %get-tuple-element.55), channel_id=1, source_target_pairs={{0,24},{1,25},{2,26},{3,27},{4,28},{5,29},{6,30},{7,31},{8,16},{9,... | collective-permute-start | bytes 1179656 | tf_op jit(solution)/shard_map/ppermute | solution.py:560
  10.3 14.6 %collective-permute-start.7 = (bf16[2,128,384]{2,1,0:T(8,128)(2,1)S(1)}, bf16[2,128,384]{2,1,0:T(8,128)(2,1)S(1)}, u32[]{:S(2)}, u32[]{:S(2)}) collective-permute-start(bf16[2,128,384]{2,1,0:T(8,128)(2,1)S(1)} %get-tuple-element.62), channel_id=1, source_target_pairs={{0,7},{1,4},{2,5},{3,6},{4,3},{5,0},{6,1},{7,2},{8,15},{9,12},{10,... | collective-permute-start | bytes 589832 | tf_op jit(solution)/shard_map/ppermute | solution.py:560
  14.7 0.8 %copy-start = (f32[1000,12]{0,1:T(8,128)S(1)}, f32[1000,12]{0,1:T(8,128)}, u32[]{:S(2)}) copy-start(f32[1000,12]{0,1:T(8,128)} %param.15) | copy-start | bytes 144004
  24.9 6.1 %collective-permute-start.5 = (bf16[2,2,128,384]{3,2,1,0:T(8,128)(2,1)S(1)}, bf16[2,2,128,384]{3,2,1,0:T(8,128)(2,1)S(1)}, u32[]{:S(2)}, u32[]{:S(2)}) collective-permute-start(bf16[2,2,128,384]{3,2,1,0:T(8,128)(2,1)S(1)} %stack.21), channel_id=1, source_target_pairs={{0,4},{4,0},{8,12},{12,8},{16,20},{20,16},{24,28},{28,24},{1,5},{5... | collective-permute-start | bytes 1179656 | tf_op jit(solution)/shard_map/ppermute | solution.py:564
  25.0 12.6 %collective-permute-start.8 = (bf16[2,2,128,384]{3,2,1,0:T(8,128)(2,1)S(1)}, bf16[2,2,128,384]{3,2,1,0:T(8,128)(2,1)S(1)}, u32[]{:S(2)}, u32[]{:S(2)}) collective-permute-start(bf16[2,2,128,384]{3,2,1,0:T(8,128)(2,1)S(1)} %stack.23), channel_id=1, source_target_pairs={{0,7},{1,4},{2,5},{3,6},{4,3},{5,0},{6,1},{7,2},{8,15},{9,12},{10,... | collective-permute-start | bytes 1179656 | tf_op jit(solution)/shard_map/ppermute | solution.py:560
  28.8 2.2 %collective-permute-start.4 = (bf16[2,128,384]{2,1,0:T(8,128)(2,1)S(1)}, bf16[2,128,384]{2,1,0:T(8,128)(2,1)S(1)}, u32[]{:S(2)}, u32[]{:S(2)}) collective-permute-start(bf16[2,128,384]{2,1,0:T(8,128)(2,1)S(1)} %stack.20), channel_id=1, source_target_pairs={{0,4},{4,0},{8,12},{12,8},{16,20},{20,16},{24,28},{28,24},{1,5},{5... | collective-permute-start | bytes 589832 | tf_op jit(solution)/shard_map/ppermute | solution.py:564
  28.9 2.0 %collective-permute-start.6 = (bf16[2,128,384]{2,1,0:T(8,128)(2,1)S(1)}, bf16[2,128,384]{2,1,0:T(8,128)(2,1)S(1)}, u32[]{:S(2)}, u32[]{:S(2)}) collective-permute-start(bf16[2,128,384]{2,1,0:T(8,128)(2,1)S(1)} %stack.22), channel_id=1, source_target_pairs={{0,4},{4,0},{8,12},{12,8},{16,20},{20,16},{24,28},{28,24},{1,5},{5... | collective-permute-start | bytes 589832 | tf_op jit(solution)/shard_map/ppermute | solution.py:564
  29.4 7.8 %collective-permute-start.9 = (bf16[2,128,384]{2,1,0:T(8,128)(2,1)S(1)}, bf16[2,128,384]{2,1,0:T(8,128)(2,1)S(1)}, u32[]{:S(2)}, u32[]{:S(2)}) collective-permute-start(bf16[2,128,384]{2,1,0:T(8,128)(2,1)S(1)} %collective-permute-done.7.refs_3_), channel_id=1, source_target_pairs={{0,24},{1,25},{2,26},{3,27},{4,28},{5,29},{6,30},{7,31},{8,16},{9,... | collective-permute-start | bytes 589832 | tf_op jit(solution)/shard_map/ppermute | solution.py:560
  41.9 1.4 %collective-permute-start.10 = (f32[3,8,8,128]{3,2,1,0:T(8,128)S(1)}, f32[3,8,8,128]{3,2,1,0:T(8,128)S(1)}, u32[]{:S(2)}, u32[]{:S(2)}) collective-permute-start(f32[3,8,8,128]{3,2,1,0:T(8,128)S(1)} %get-tuple-element.63.stats), channel_id=1, source_target_pairs={{0,4},{4,0},{8,12},{12,8},{16,20},{20,16},{24,28},{28,24},{1,5},{5... | collective-permute-start | bytes 294920 | tf_op jit(solution)/shard_map/ppermute | solution.py:564
  47.5 17.1 %collective-permute-start.18 = (bf16[3,2,128,384]{3,2,1,0:T(8,128)(2,1)S(1)}, bf16[3,2,128,384]{3,2,1,0:T(8,128)(2,1)S(1)}, u32[]{:S(2)}, u32[]{:S(2)}) collective-permute-start(bf16[3,2,128,384]{3,2,1,0:T(8,128)(2,1)S(1)} %get-tuple-element.88), channel_id=1, source_target_pairs={{0,5},{1,6},{2,7},{3,4},{4,1},{5,2},{6,3},{7,0},{8,13},{9,14},{10,... | collective-permute-start | bytes 1769480 | tf_op jit(solution)/shard_map/ppermute | solution.py:560
  50.7 4.2 %collective-permute-start.11 = (bf16[2,128,384]{2,1,0:T(8,128)(2,1)S(1)}, bf16[2,128,384]{2,1,0:T(8,128)(2,1)S(1)}, u32[]{:S(2)}, u32[]{:S(2)}) collective-permute-start(bf16[2,128,384]{2,1,0:T(8,128)(2,1)S(1)} %get-tuple-element.74), channel_id=1, source_target_pairs={{0,4},{4,0},{8,12},{12,8},{16,20},{20,16},{24,28},{28,24},{1,5},{5... | collective-permute-start | bytes 589832 | tf_op jit(solution)/shard_map/ppermute | solution.py:564
  50.7 4.2 %collective-permute-start.12 = (bf16[2,128,384]{2,1,0:T(8,128)(2,1)S(1)}, bf16[2,128,384]{2,1,0:T(8,128)(2,1)S(1)}, u32[]{:S(2)}, u32[]{:S(2)}) collective-permute-start(bf16[2,128,384]{2,1,0:T(8,128)(2,1)S(1)} %get-tuple-element.76), channel_id=1, source_target_pairs={{0,4},{4,0},{8,12},{12,8},{16,20},{20,16},{24,28},{28,24},{1,5},{5... | collective-permute-start | bytes 589832 | tf_op jit(solution)/shard_map/ppermute | solution.py:564
  51.2 3.7 %collective-permute-start.13 = (bf16[2,128,384]{2,1,0:T(8,128)(2,1)S(1)}, bf16[2,128,384]{2,1,0:T(8,128)(2,1)S(1)}, u32[]{:S(2)}, u32[]{:S(2)}) collective-permute-start(bf16[2,128,384]{2,1,0:T(8,128)(2,1)S(1)} %get-tuple-element.78), channel_id=1, source_target_pairs={{0,4},{4,0},{8,12},{12,8},{16,20},{20,16},{24,28},{28,24},{1,5},{5... | collective-permute-start | bytes 589832 | tf_op jit(solution)/shard_map/ppermute | solution.py:564
  51.3 3.6 %collective-permute-start.14 = (bf16[2,128,384]{2,1,0:T(8,128)(2,1)S(1)}, bf16[2,128,384]{2,1,0:T(8,128)(2,1)S(1)}, u32[]{:S(2)}, u32[]{:S(2)}) collective-permute-start(bf16[2,128,384]{2,1,0:T(8,128)(2,1)S(1)} %get-tuple-element.80), channel_id=1, source_target_pairs={{0,4},{4,0},{8,12},{12,8},{16,20},{20,16},{24,28},{28,24},{1,5},{5... | collective-permute-start | bytes 589832 | tf_op jit(solution)/shard_map/ppermute | solution.py:564
  55.1 9.8 %collective-permute-start.15 = (bf16[2,128,384]{2,1,0:T(8,128)(2,1)S(1)}, bf16[2,128,384]{2,1,0:T(8,128)(2,1)S(1)}, u32[]{:S(2)}, u32[]{:S(2)}) collective-permute-start(bf16[2,128,384]{2,1,0:T(8,128)(2,1)S(1)} %get-tuple-element.82), channel_id=1, source_target_pairs={{0,8},{1,9},{2,10},{3,11},{4,12},{5,13},{6,14},{7,15},{8,0},{9,1},... | collective-permute-start | bytes 589832 | tf_op jit(solution)/shard_map/ppermute | solution.py:560
  55.2 11.7 %collective-permute-start.16 = (bf16[2,128,384]{2,1,0:T(8,128)(2,1)S(1)}, bf16[2,128,384]{2,1,0:T(8,128)(2,1)S(1)}, u32[]{:S(2)}, u32[]{:S(2)}) collective-permute-start(bf16[2,128,384]{2,1,0:T(8,128)(2,1)S(1)} %get-tuple-element.83), channel_id=1, source_target_pairs={{0,16},{1,17},{2,18},{3,19},{4,20},{5,21},{6,22},{7,23},{8,24},{9,... | collective-permute-start | bytes 589832 | tf_op jit(solution)/shard_map/ppermute | solution.py:560
  57.2 11.8 %collective-permute-start.17 = (bf16[2,128,384]{2,1,0:T(8,128)(2,1)S(1)}, bf16[2,128,384]{2,1,0:T(8,128)(2,1)S(1)}, u32[]{:S(2)}, u32[]{:S(2)}) collective-permute-start(bf16[2,128,384]{2,1,0:T(8,128)(2,1)S(1)} %get-tuple-element.84), channel_id=1, source_target_pairs={{0,24},{1,25},{2,26},{3,27},{4,28},{5,29},{6,30},{7,31},{8,16},{9,... | collective-permute-start | bytes 589832 | tf_op jit(solution)/shard_map/ppermute | solution.py:560
  64.8 8.8 %collective-permute-start.19 = (bf16[2,128,384]{2,1,0:T(8,128)(2,1)S(1)}, bf16[2,128,384]{2,1,0:T(8,128)(2,1)S(1)}, u32[]{:S(2)}, u32[]{:S(2)}) collective-permute-start(bf16[2,128,384]{2,1,0:T(8,128)(2,1)S(1)} %get-tuple-element.92), channel_id=1, source_target_pairs={{0,5},{1,6},{2,7},{3,4},{4,1},{5,2},{6,3},{7,0},{8,13},{9,14},{10,... | collective-permute-start | bytes 589832 | tf_op jit(solution)/shard_map/ppermute | solution.py:560
  64.8 8.7 %collective-permute-start.20 = (bf16[2,128,384]{2,1,0:T(8,128)(2,1)S(1)}, bf16[2,128,384]{2,1,0:T(8,128)(2,1)S(1)}, u32[]{:S(2)}, u32[]{:S(2)}) collective-permute-start(bf16[2,128,384]{2,1,0:T(8,128)(2,1)S(1)} %get-tuple-element.93), channel_id=1, source_target_pairs={{0,8},{1,9},{2,10},{3,11},{4,12},{5,13},{6,14},{7,15},{8,0},{9,1},... | collective-permute-start | bytes 589832 | tf_op jit(solution)/shard_map/ppermute | solution.py:560
  64.9 10.5 %collective-permute-start.21 = (bf16[2,128,384]{2,1,0:T(8,128)(2,1)S(1)}, bf16[2,128,384]{2,1,0:T(8,128)(2,1)S(1)}, u32[]{:S(2)}, u32[]{:S(2)}) collective-permute-start(bf16[2,128,384]{2,1,0:T(8,128)(2,1)S(1)} %get-tuple-element.94), channel_id=1, source_target_pairs={{0,16},{1,17},{2,18},{3,19},{4,20},{5,21},{6,22},{7,23},{8,24},{9,... | collective-permute-start | bytes 589832 | tf_op jit(solution)/shard_map/ppermute | solution.py:560
  66.9 10.1 %collective-permute-start.22 = (bf16[2,128,384]{2,1,0:T(8,128)(2,1)S(1)}, bf16[2,128,384]{2,1,0:T(8,128)(2,1)S(1)}, u32[]{:S(2)}, u32[]{:S(2)}) collective-permute-start(bf16[2,128,384]{2,1,0:T(8,128)(2,1)S(1)} %get-tuple-element.95), channel_id=1, source_target_pairs={{0,24},{1,25},{2,26},{3,27},{4,28},{5,29},{6,30},{7,31},{8,16},{9,... | collective-permute-start | bytes 589832 | tf_op jit(solution)/shard_map/ppermute | solution.py:560

commit v3 on v2

--- a/solution.py
+++ b/solution.py
@@ -252,22 +252,27 @@
     return [[x[i] for x in sums] for i in range(3)]
 
 
-def gradients(z, rows, log_total, delta, score, dprob, both, kt, vt, acc):
-    found = []
+def weights(z, rows, log_total, delta, score, dprob):
     for h in range(z.batch):
         w = jnp.exp2(score[h][:rows, :] - log_total[h])
-        ds = (w * (dprob[h][:rows, :] - delta[h])).astype(BF16)
-        w = w.astype(BF16)
+        yield h, w.astype(BF16), (w * (dprob[h][:rows, :] - delta[h])).astype(BF16)
+
+
+def add_key_gradients(rows, pairs, both, acc):
+    for h, w, ds in pairs:
         acc[h, :rows, :] += jnp.dot(
             jnp.concatenate([ds, w], axis=1), both[h][...], preferred_element_type=F32
         )
-        found.append(
-            (
-                jnp.dot(vt[h, :, :rows], w, preferred_element_type=F32),
-                jnp.dot(kt[h, :, :rows], ds, preferred_element_type=F32),
-            )
+
+
+def row_gradients(rows, pairs, kt, vt):
+    return [
+        (
+            jnp.dot(vt[h, :, :rows], w, preferred_element_type=F32),
+            jnp.dot(kt[h, :, :rows], ds, preferred_element_type=F32),
         )
-    return found
+        for h, w, ds in pairs
+    ]
 
 
 def write_sums(z, goals, ranks, acc):
@@ -390,75 +395,84 @@
 
             @pl.when(needed & (live == 1))
             def _():
-                found = gradients(
+                pairs = list(
+                    weights(
+                        z,
+                        rows,
+                        log_total,
+                        delta,
+                        [score.at[h, at] for h in heads],
+                        [dprob.at[h, at] for h in heads],
+                    )
+                )
+                add_key_gradients(rows, pairs, [both.at[h, at] for h in heads], acc)
+                for h, found in enumerate(row_gradients(rows, pairs, kt, vt)):
+                    ot[h, at], dqt[h, at] = found
+
+        @pl.when((count == 0) | (live != 1))
+        def _():
+            ot[:, at] = jnp.zeros_like(ot[:, at])
+            dqt[:, at] = jnp.zeros_like(dqt[:, at])
+
+    goals = [own_sums] + [sums.at[i] for i in range(z.shards - 1)]
+    write_sums(z, goals, z.ranks(meta_ref, True)[1], acc)
+
+
+def rows_kernel(z, meta_ref, kt, vt, score, dprob, final, ot_in, dqt_in, *refs, mine):
+    rows_out = refs[1:]
+    heads = range(z.batch)
+    for at, count, _ in z.queries(meta_ref, False):
+        if mine != (at < z.shards):
+            continue
+        log_total = [final[h, at, 0:1, :] for h in heads]
+        delta = [final[h, at, 1:2, :] for h in heads]
+
+        def write(h, out, dq):
+            goal = rows_out[at if mine else at - z.shards]
+            goal[0, :, z.lanes(h)] = out.astype(BF16).T
+            goal[1, :, z.lanes(h)] = (dq * z.inv_root).astype(BF16).T
+
+        for rows, needed in z.blocks(count):
+
+            @pl.when(needed)
+            def _():
+                pairs = weights(
                     z,
                     rows,
                     log_total,
                     delta,
                     [score.at[h, at] for h in heads],
                     [dprob.at[h, at] for h in heads],
-                    [both.at[h, at] for h in heads],
-                    kt,
-                    vt,
-                    acc,
                 )
-                for h in heads:
-                    ot[h, at], dqt[h, at] = found[h]
-
-        @pl.when((count == 0) | (live != 1))
-        def _():
-            ot[:, at] = jnp.zeros_like(ot[:, at])
-            dqt[:, at] = jnp.zeros_like(dqt[:, at])
-
-    goals = [own_sums] + [sums.at[i] for i in range(z.shards - 1)]
-    write_sums(z, goals, z.ranks(meta_ref, True)[1], acc)
-
-
-def rows_kernel(z, meta_ref, kt, vt, both, score, dprob, final, ot_in, dqt_in, *refs, mine):
-    heads = range(z.batch)
-    if mine:
-        acc_in, rows_out, sums, acc = refs[1], refs[2 : 2 + z.shards], refs[2 + z.shards : -1], refs[-1]
-        acc[...] = acc_in[...]
-    else:
-        rows_out, acc = refs[1:-1], refs[-1]
-        acc[...] = jnp.zeros_like(acc)
-    for at, count, _ in z.queries(meta_ref, False):
-        if mine != (at < z.shards):
-            continue
-        log_total = [final[h, at, 0:1, :] for h in heads]
-        delta = [final[h, at, 1:2, :] for h in heads]
-
-        def write(h, out, dq):
-            goal = rows_out[at if mine else at - z.shards]
-            goal[0, :, z.lanes(h)] = out.astype(BF16).T
-            goal[1, :, z.lanes(h)] = (dq * z.inv_root).astype(BF16).T
-
-        for rows, needed in z.blocks(count):
-
-            @pl.when(needed)
-            def _():
-                found = gradients(
-                    z,
-                    rows,
-                    log_total,
-                    delta,
-                    [score.at[h, at] for h in heads],
-                    [dprob.at[h, at] for h in heads],
-                    [both.at[h, at] for h in heads],
-                    kt,
-                    vt,
-                    acc,
-                )
-                for h in heads:
-                    write(h, ot_in[h, at] + found[h][0], dqt_in[h, at] + found[h][1])
+                for h, (out, dq) in enumerate(row_gradients(rows, pairs, kt, vt)):
+                    write(h, ot_in[h, at] + out, dqt_in[h, at] + dq)
 
         @pl.when(count == 0)
         def _():
             for h in heads:
                 write(h, ot_in[h, at], dqt_in[h, at])
 
-    if mine:
-        write_sums(z, sums, z.ranks(meta_ref, False)[1], acc)
+
+def sums_kernel(z, meta_ref, both, score, dprob, final, *refs):
+    sums, acc = refs[1:-1], refs[-1]
+    heads = range(z.batch)
+    acc[...] = jnp.zeros_like(acc)
+    for at, count, _ in z.queries(meta_ref, False):
+        for rows, needed in z.blocks(count):
+
+            @pl.when(needed)
+            def _():
+                pairs = weights(
+                    z,
+                    rows,
+                    [final[h, at, 0:1, :] for h in heads],
+                    [final[h, at, 1:2, :] for h in heads],
+                    [score.at[h, at] for h in heads],
+                    [dprob.at[h, at] for h in heads],
+                )
+                add_key_gradients(rows, pairs, [both.at[h, at] for h in heads], acc)
+
+    write_sums(z, sums, z.ranks(meta_ref, False)[1], acc)
 
 
 def add_up(terms, at=()):
@@ -645,29 +659,37 @@
         [sums_scratch],
     )
     far_home = to_shard(far_sums, 0, 1)
-    operands = scalars + [(x, "heads") for x in (kt, vt, both, score, dprob, final, ot, dqt)]
-    *rows_others, partial_sums = z.call(
+    operands = scalars + [(x, "heads") for x in (kt, vt, score, dprob, final, ot, dqt)]
+    rows_others = z.call(
         functools.partial(rows_kernel, mine=False),
         "rows_others",
         limit,
         operands + [(first_sums, "lanes")],
-        [(one, "lanes")] * (groups - shards)
-        + [(shape((own, shards * tok, 2 * width), F32), "heads")],
+        [(one, "lanes")] * (groups - shards),
         [],
     )
-    results = z.call(
+    rows_mine = z.call(
         functools.partial(rows_kernel, mine=True),
         "rows",
         limit,
-        operands + [(first_sums, "lanes"), (partial_sums, "heads")],
-        [(one, "lanes")] * (2 * shards),
+        operands + [(first_sums, "lanes")],
+        [(one, "lanes")] * shards,
+        [],
+    )
+    row_sums = add(with_others([*rows_mine, *rows_others]))
+    rows_home = [to_shard(row_sums[hop], hop, 0) for hop in hops[::-1]][::-1]
+    near_sums = z.call(
+        sums_kernel,
+        "sums",
+        limit,
+        scalars
+        + [(x, "heads") for x in (both, score, dprob, final)]
+        + [(row_sums[0], "lanes")],
+        [(one, "lanes")] * shards,
         [sums_scratch],
     )
-    row_sums = add(with_others([*results[:shards], *rows_others]))
-    rows_home = [to_shard(row_sums[hop], hop, 0) for hop in hops]
-    near_sums = results[shards:]
     *sums, first_late = merge([[x] for x in near_sums[1:]], far_home, [first_sums])
-    sums_home = [to_shard(x, hop, 0) for hop, x in zip(hops[1:], sums)]
+    sums_home = [to_shard(x, hop, 0) for hop, x in zip(hops[:0:-1], sums[::-1])][::-1]
     first_home = to_shard(first_late, 0, 1)
     attended, grad_queries = unpack(pos, [[x] for x in rows_home])
     grad_keys, grad_values = unpack(

time: 77.2 us -> 75.6 us (0.979); the launches traced: 78.6 us -> 75.6 us
  waiting for transfers between devices: 26.8 us -> 24 us
  Pallas kernels: 25.9 us -> 24 us
  starting transfers between devices: 23.4 us -> 25.2 us
    ppermute x15, waiting for transfers between devices: 25.5 us -> 22.7 us  [to_shard(): return lax.ppermute(x, ('tm', 'tile'), pairs)]
    pallas_call x5 -> x6, Pallas kernels: 19.6 us -> 17.8 us  [call(): pl.pallas_call(functools.partial(kernel, self), grid=(self.own_heads // s...]
    ppermute x15, starting transfers between devices: 21.5 us -> 22.9 us  [to_shard(): return lax.ppermute(x, ('tm', 'tile'), pairs)]
  transfers between devices with their start and end apart: 23 -> 23, of which waited for: 9 -> 11; matrix products, arithmetic and copies ran while one was open for 1% -> 1% of each run, Pallas kernels for 17% -> 20%
where the time goes in v3:
time: 75.6 us
  starting transfers between devices  25.2 us (33%)
  Pallas kernels  24 us (32%)
  waiting for transfers between devices  24 us (32%)
  local copies, waits for them, and re-layouts  1.6 us (2%)
  between operations  0.83 us (1%)
    ppermute x15, starting transfers between devices, to_shard(): return lax.ppermute(x, ('tm', 'tile'), pairs)  22.9 us
    ppermute x15, waiting for transfers between devices, to_shard(): return lax.ppermute(x, ('tm', 'tile'), pairs)  22.7 us
    pallas_call x6, Pallas kernels, call(): pl.pallas_call(functools.partial(kernel, self), grid=(self.own_heads // s...  17.8 us
    pallas_call x2, Pallas kernels, unpack(): pl.pallas_call(kernel, out_shape=[jax.ShapeDtypeStruct((tok, cols * shard...  3 us
    ppermute x8, starting transfers between devices, to_replica(): return lax.ppermute(x, 'tm', pairs)  2.29 us
    pallas_call x1, Pallas kernels, pack(): pl.pallas_call(functools.partial(pack_kernel, z), out_shape=[shape((4, z....  2.1 us
  transfers between devices with their start and end apart: 23, of which 11 were waited for; matrix products, arithmetic and copies ran while one was open for 1% of the time, Pallas kernels for 20%

profile of v3, /device:TPU:0, one launch (start us, length us, event | category | flops | bytes accessed | tf_op | source)
XLA Modules:
  0.0 75.6 jit_solution(4108687339574845216)
XLA Ops:
  0.7 2.1 %pack.1 = (bf16[4,128,384]{2,1,0:T(8,128)(2,1)S(1)}, bf16[4,128,384]{2,1,0:T(8,128)(2,1)S(1)}, bf16[4,128,384]{2,1,0:T(8,128)(2,1)S(1)}, bf16[4,128,384]{2,1,0:T...) custom-call(s32[3]{0:T(128)S(1)} %pad_add_fusion.pos_ref, ...), custom_call_target="tpu_custom_call" | custom-call | tf_op jit(solution)/shard_map/pack/pallas_call | solution.py:67
  2.8 3.0 %collective-permute-start.1 = (bf16[4,128,384]{2,1,0:T(8,128)(2,1)S(1)}, bf16[4,128,384]{2,1,0:T(8,128)(2,1)S(1)}, u32[]{:S(2)}, u32[]{:S(2)}) collective-permute-start(bf16[4,128,384]{2,1,0:T(8,128)(2,1)S(1)} %get-tuple-element.52), channel_id=1, source_target_pairs={{0,8},{1,9},{2,10},{3,11},{4,12},{5,13},{6,14},{7,15},{8,0},{9,1},... | collective-permute-start | bytes 1179656 | tf_op jit(solution)/shard_map/ppermute | solution.py:574
  5.8 1.5 %collective-permute-start.2 = (bf16[4,128,384]{2,1,0:T(8,128)(2,1)S(1)}, bf16[4,128,384]{2,1,0:T(8,128)(2,1)S(1)}, u32[]{:S(2)}, u32[]{:S(2)}) collective-permute-start(bf16[4,128,384]{2,1,0:T(8,128)(2,1)S(1)} %get-tuple-element.53), channel_id=1, source_target_pairs={{0,16},{1,17},{2,18},{3,19},{4,20},{5,21},{6,22},{7,23},{8,24},{9,... | collective-permute-start | bytes 1179656 | tf_op jit(solution)/shard_map/ppermute | solution.py:574
  7.4 2.5 %collective-permute-start = (bf16[2,128,384]{2,1,0:T(8,128)(2,1)S(1)}, bf16[2,128,384]{2,1,0:T(8,128)(2,1)S(1)}, u32[]{:S(2)}, u32[]{:S(2)}) collective-permute-start(bf16[2,128,384]{2,1,0:T(8,128)(2,1)S(1)} %get-tuple-element.50), channel_id=1, source_target_pairs={{0,7},{1,4},{2,5},{3,6},{4,3},{5,0},{6,1},{7,2},{8,15},{9,12},{10,... | collective-permute-start | bytes 589832 | tf_op jit(solution)/shard_map/ppermute | solution.py:574
  12.1 2.6 %collective-permute-done.after_ref.refs_0_.refs_2_ = bf16[2,128,384]{2,1,0:T(8,128)(2,1)S(1)} collective-permute-done((bf16[2,128,384]{2,1,0:T(8,128)(2,1)S(1)}, bf16[2,128,384]{2,1,0:T(8,128)(2,1)S(1)}, u32[]{:S(2)}, u32[]{:S(2)}) %collective-permute-start) | collective-permute-done | bytes 196640 | tf_op jit(solution)/shard_map/ppermute | solution.py:574
  16.2 8.7 %collective-permute-done.2.refs_1_.refs_2_ = bf16[4,128,384]{2,1,0:T(8,128)(2,1)S(1)} collective-permute-done((bf16[4,128,384]{2,1,0:T(8,128)(2,1)S(1)}, bf16[4,128,384]{2,1,0:T(8,128)(2,1)S(1)}, u32[]{:S(2)}, u32[]{:S(2)}) %collective-permute-start.2) | collective-permute-done | bytes 393248 | tf_op jit(solution)/shard_map/ppermute | solution.py:574
  25.0 3.7 %collective-permute-start.8 = (bf16[2,2,128,384]{3,2,1,0:T(8,128)(2,1)S(1)}, bf16[2,2,128,384]{3,2,1,0:T(8,128)(2,1)S(1)}, u32[]{:S(2)}, u32[]{:S(2)}) collective-permute-start(bf16[2,2,128,384]{3,2,1,0:T(8,128)(2,1)S(1)} %stack.23), channel_id=1, source_target_pairs={{0,7},{1,4},{2,5},{3,6},{4,3},{5,0},{6,1},{7,2},{8,15},{9,12},{10,... | collective-permute-start | bytes 1179656 | tf_op jit(solution)/shard_map/ppermute | solution.py:574
  29.4 1.5 %collective-permute-start.9 = (bf16[2,128,384]{2,1,0:T(8,128)(2,1)S(1)}, bf16[2,128,384]{2,1,0:T(8,128)(2,1)S(1)}, u32[]{:S(2)}, u32[]{:S(2)}) collective-permute-start(bf16[2,128,384]{2,1,0:T(8,128)(2,1)S(1)} %collective-permute-done.7.refs_3_), channel_id=1, source_target_pairs={{0,24},{1,25},{2,26},{3,27},{4,28},{5,29},{6,30},{7,31},{8,16},{9,... | collective-permute-start | bytes 589832 | tf_op jit(solution)/shard_map/ppermute | solution.py:574
  31.0 4.6 %own.1 = (bf16[3,128,512]{2,1,0:T(8,128)(2,1)S(1)}, bf16[3,128,512]{2,1,0:T(8,128)(2,1)S(1)}, bf16[3,8,256,256]{3,2,1,0:T(8,128)(2,1)S(1)}, f32[3,8,512,128]{3,2...) custom-call(s32[51]{0:T(128)S(1)} %concatenate.4.meta_ref, ...), custom_call_target="tpu_custom_call" | custom-call | tf_op jit(solution)/shard_map/own/pallas_call | solution.py:204
  35.6 1.7 %collective-permute-done.9.refs_0_ = bf16[2,128,384]{2,1,0:T(8,128)(2,1)S(1)} collective-permute-done((bf16[2,128,384]{2,1,0:T(8,128)(2,1)S(1)}, bf16[2,128,384]{2,1,0:T(8,128)(2,1)S(1)}, u32[]{:S(2)}, u32[]{:S(2)}) %collective-permute-start.9) | collective-permute-done | bytes 196640 | tf_op jit(solution)/shard_map/ppermute | solution.py:574
  37.6 2.8 %ahead.1 = (f32[3,8,8,128]{3,2,1,0:T(8,128)S(1)}, bf16[3,128,512]{2,1,0:T(8,128)(2,1)S(1)}, bf16[3,128,512]{2,1,0:T(8,128)(2,1)S(1)}, f32[3,8,512,128]{3,2,1,0:T(8,128)S(1)}, f32[3,8,512,128]{3,2,1,0:T(8,128)S(1)}) custom-call(s32[51]{0:T(128)S(1)} %concatenate.4.meta_ref, f32[8,12,128]{2,1,0:T(8,128)S(1)} %bias.1.refs_2_.refs_4_, ...), custom_call_target="tpu_custom_call" | custom-call | tf_op jit(solution)/shard_map/ahead/pallas_call | solution.py:204
  41.7 2.8 %back.1 = (f32[3,8,8,128]{3,2,1,0:T(8,128)S(1)}, f32[3,8,128,128]{3,2,1,0:T(8,128)S(1)}, f32[3,8,128,128]{3,2,1,0:T(8,128)S(1)}, bf16[2,128,384]{2,1,0:T(8,128)(2,1)S(1)}, bf16[3,2,128,384]{3,2,1,0:T(8,128)(2,1)S(1)}) custom-call(s32[51]{0:T(128)S(1)} %concatenate.4.meta_ref, bf16[3,8,256,256]{3,2,1,0:T(8,128)(2,1)S(1)} %get-tuple-element.59.both, ...), custom_call_target="tpu_custom_call" | custom-call | tf_op jit(solution)/shard_map/back/pallas_call | solution.py:204
  46.0 2.1 %rows_others.1 = (bf16[2,128,384]{2,1,0:T(8,128)(2,1)S(1)}, bf16[2,128,384]{2,1,0:T(8,128)(2,1)S(1)}, bf16[2,128,384]{2,1,0:T(8,128)(2,1)S(1)}, bf16[2,128,384]{2,1,0:T(8,128)(2,1)S(1)}) custom-call(s32[51]{0:T(128)S(1)} %concatenate.4.meta_ref, bf16[3,128,512]{2,1,0:T(8,128)(2,1)S(1)} %get-tuple-element.55.kt, ...), custom_call_target="tpu_custom_call" | custom-call | tf_op jit(solution)/shard_map/rows_others/pallas_call | solution.py:204
  49.6 2.3 %rows.1 = (bf16[2,128,384]{2,1,0:T(8,128)(2,1)S(1)}, bf16[2,128,384]{2,1,0:T(8,128)(2,1)S(1)}, bf16[2,128,384]{2,1,0:T(8,128)(2,1)S(1)}, bf16[2,128,384]{2,1,0:T(8,128)(2,1)S(1)}) custom-call(s32[51]{0:T(128)S(1)} %concatenate.4.meta_ref, bf16[3,128,512]{2,1,0:T(8,128)(2,1)S(1)} %get-tuple-element.55.kt, bf16[3,128,512]{2,1,0:T(8,128)(2,1)S(1)} %get-tuple-element.56.vt, ...), custom_call_target="tpu_custom_call" | custom-call | tf_op jit(solution)/shard_map/rows/pallas_call | solution.py:204
  52.2 2.1 %collective-permute-start.16 = (bf16[2,128,384]{2,1,0:T(8,128)(2,1)S(1)}, bf16[2,128,384]{2,1,0:T(8,128)(2,1)S(1)}, u32[]{:S(2)}, u32[]{:S(2)}) collective-permute-start(bf16[2,128,384]{2,1,0:T(8,128)(2,1)S(1)} %get-tuple-element.81), channel_id=1, source_target_pairs={{0,16},{1,17},{2,18},{3,19},{4,20},{5,21},{6,22},{7,23},{8,24},{9,... | collective-permute-start | bytes 589832 | tf_op jit(solution)/shard_map/ppermute | solution.py:574
  54.3 3.2 %sums.1 = (bf16[2,128,384]{2,1,0:T(8,128)(2,1)S(1)}, bf16[2,128,384]{2,1,0:T(8,128)(2,1)S(1)}, bf16[2,128,384]{2,1,0:T(8,128)(2,1)S(1)}, bf16[2,128,384]{2,1,0:T(8,128)(2,1)S(1)}) custom-call(s32[51]{0:T(128)S(1)} %concatenate.4.meta_ref, bf16[3,8,256,256]{3,2,1,0:T(8,128)(2,1)S(1)} %get-tuple-element.59.both, ...), custom_call_target="tpu_custom_call" | custom-call | tf_op jit(solution)/shard_map/sums/pallas_call | solution.py:204
  57.5 1.5 %collective-permute-start.17 = (bf16[2,128,384]{2,1,0:T(8,128)(2,1)S(1)}, bf16[2,128,384]{2,1,0:T(8,128)(2,1)S(1)}, u32[]{:S(2)}, u32[]{:S(2)}) collective-permute-start(bf16[2,128,384]{2,1,0:T(8,128)(2,1)S(1)} %get-tuple-element.82), channel_id=1, source_target_pairs={{0,24},{1,25},{2,26},{3,27},{4,28},{5,29},{6,30},{7,31},{8,16},{9,... | collective-permute-start | bytes 589832 | tf_op jit(solution)/shard_map/ppermute | solution.py:574
  59.0 1.9 %collective-permute-done.18.refs_0_ = bf16[3,2,128,384]{3,2,1,0:T(8,128)(2,1)S(1)} collective-permute-done((bf16[3,2,128,384]{3,2,1,0:T(8,128)(2,1)S(1)}, bf16[3,2,128,384]{3,2,1,0:T(8,128)(2,1)S(1)}, u32[]{:S(2)}, u32[]{:S(2)}) %collective-permute-start.18) | collective-permute-done | bytes 589856 | tf_op jit(solution)/shard_map/ppermute | solution.py:574
  61.7 2.3 %collective-permute-start.21 = (bf16[2,128,384]{2,1,0:T(8,128)(2,1)S(1)}, bf16[2,128,384]{2,1,0:T(8,128)(2,1)S(1)}, u32[]{:S(2)}, u32[]{:S(2)}) collective-permute-start(bf16[2,128,384]{2,1,0:T(8,128)(2,1)S(1)} %get-tuple-element.92), channel_id=1, source_target_pairs={{0,16},{1,17},{2,18},{3,19},{4,20},{5,21},{6,22},{7,23},{8,24},{9,... | collective-permute-start | bytes 589832 | tf_op jit(solution)/shard_map/ppermute | solution.py:574
  65.6 1.5 %unpack.2 = (bf16[128,1536]{1,0:T(8,128)(2,1)}, bf16[128,1536]{1,0:T(8,128)(2,1)}) custom-call(s32[3]{0:T(128)S(1)} %pad_add_fusion.pos_ref, bf16[2,128,384]{2,1,0:T(8,128)(2,1)S(1)} %get-tuple-element.79.refs_0_, bf16[2,128,384]{2,1,0:T(8,128)(2,1)S(1)} %collective-permute-done.15.refs_1_, bf16[2,128,384]{2,1,0:T(8,128)(2,1)S(1)} %collective-permute-done.16.refs_2_, ...), custom_call_target="tpu_custom_call" | custom-call | tf_op jit(solution)/shard_map/unpack/pallas_call | solution.py:540
  67.1 1.8 %collective-permute-done.19.refs_1_ = bf16[2,128,384]{2,1,0:T(8,128)(2,1)S(1)} collective-permute-done((bf16[2,128,384]{2,1,0:T(8,128)(2,1)S(1)}, bf16[2,128,384]{2,1,0:T(8,128)(2,1)S(1)}, u32[]{:S(2)}, u32[]{:S(2)}) %collective-permute-start.19) | collective-permute-done | bytes 196640 | tf_op jit(solution)/shard_map/ppermute | solution.py:574
  69.4 3.2 %collective-permute-done.21.refs_3_ = bf16[2,128,384]{2,1,0:T(8,128)(2,1)S(1)} collective-permute-done((bf16[2,128,384]{2,1,0:T(8,128)(2,1)S(1)}, bf16[2,128,384]{2,1,0:T(8,128)(2,1)S(1)}, u32[]{:S(2)}, u32[]{:S(2)}) %collective-permute-start.21) | collective-permute-done | bytes 196640 | tf_op jit(solution)/shard_map/ppermute | solution.py:574
  72.5 1.6 %collective-permute-done.22.refs_4_ = bf16[2,128,384]{2,1,0:T(8,128)(2,1)S(1)} collective-permute-done((bf16[2,128,384]{2,1,0:T(8,128)(2,1)S(1)}, bf16[2,128,384]{2,1,0:T(8,128)(2,1)S(1)}, u32[]{:S(2)}, u32[]{:S(2)}) %collective-permute-start.22) | collective-permute-done | bytes 196640 | tf_op jit(solution)/shard_map/ppermute | solution.py:574
  74.1 1.5 %unpack.3 = (bf16[128,1536]{1,0:T(8,128)(2,1)}, bf16[128,1536]{1,0:T(8,128)(2,1)}) custom-call(s32[3]{0:T(128)S(1)} %pad_add_fusion.pos_ref, bf16[2,128,384]{2,1,0:T(8,128)(2,1)S(1)} %get-tuple-element.85.refs_0_, bf16[2,128,384]{2,1,0:T(8,128)(2,1)S(1)} %collective-permute-done.19.refs_1_, bf16[2,128,384]{2,1,0:T(8,128)(2,1)S(1)} %collective-permute-done.20.refs_2_, ...), custom_call_target="tpu_custom_call" | custom-call | tf_op jit(solution)/shard_map/unpack/pallas_call | solution.py:540
  (45 shorter events, 12.5 us)
Async XLA Ops:
  2.8 13.3 %collective-permute-start.1 = (bf16[4,128,384]{2,1,0:T(8,128)(2,1)S(1)}, bf16[4,128,384]{2,1,0:T(8,128)(2,1)S(1)}, u32[]{:S(2)}, u32[]{:S(2)}) collective-permute-start(bf16[4,128,384]{2,1,0:T(8,128)(2,1)S(1)} %get-tuple-element.52), channel_id=1, source_target_pairs={{0,8},{1,9},{2,10},{3,11},{4,12},{5,13},{6,14},{7,15},{8,0},{9,1},... | collective-permute-start | bytes 1179656 | tf_op jit(solution)/shard_map/ppermute | solution.py:574
  5.8 19.0 %collective-permute-start.2 = (bf16[4,128,384]{2,1,0:T(8,128)(2,1)S(1)}, bf16[4,128,384]{2,1,0:T(8,128)(2,1)S(1)}, u32[]{:S(2)}, u32[]{:S(2)}) collective-permute-start(bf16[4,128,384]{2,1,0:T(8,128)(2,1)S(1)} %get-tuple-element.53), channel_id=1, source_target_pairs={{0,16},{1,17},{2,18},{3,19},{4,20},{5,21},{6,22},{7,23},{8,24},{9,... | collective-permute-start | bytes 1179656 | tf_op jit(solution)/shard_map/ppermute | solution.py:574
  7.4 7.3 %collective-permute-start = (bf16[2,128,384]{2,1,0:T(8,128)(2,1)S(1)}, bf16[2,128,384]{2,1,0:T(8,128)(2,1)S(1)}, u32[]{:S(2)}, u32[]{:S(2)}) collective-permute-start(bf16[2,128,384]{2,1,0:T(8,128)(2,1)S(1)} %get-tuple-element.50), channel_id=1, source_target_pairs={{0,7},{1,4},{2,5},{3,6},{4,3},{5,0},{6,1},{7,2},{8,15},{9,12},{10,... | collective-permute-start | bytes 589832 | tf_op jit(solution)/shard_map/ppermute | solution.py:574
  9.8 19.0 %collective-permute-start.3 = (bf16[4,128,384]{2,1,0:T(8,128)(2,1)S(1)}, bf16[4,128,384]{2,1,0:T(8,128)(2,1)S(1)}, u32[]{:S(2)}, u32[]{:S(2)}) collective-permute-start(bf16[4,128,384]{2,1,0:T(8,128)(2,1)S(1)} %get-tuple-element.54), channel_id=1, source_target_pairs={{0,24},{1,25},{2,26},{3,27},{4,28},{5,29},{6,30},{7,31},{8,16},{9,... | collective-permute-start | bytes 1179656 | tf_op jit(solution)/shard_map/ppermute | solution.py:574
  10.3 14.6 %collective-permute-start.7 = (bf16[2,128,384]{2,1,0:T(8,128)(2,1)S(1)}, bf16[2,128,384]{2,1,0:T(8,128)(2,1)S(1)}, u32[]{:S(2)}, u32[]{:S(2)}) collective-permute-start(bf16[2,128,384]{2,1,0:T(8,128)(2,1)S(1)} %get-tuple-element.61), channel_id=1, source_target_pairs={{0,7},{1,4},{2,5},{3,6},{4,3},{5,0},{6,1},{7,2},{8,15},{9,12},{10,... | collective-permute-start | bytes 589832 | tf_op jit(solution)/shard_map/ppermute | solution.py:574
  14.7 0.8 %copy-start = (f32[1000,12]{0,1:T(8,128)S(1)}, f32[1000,12]{0,1:T(8,128)}, u32[]{:S(2)}) copy-start(f32[1000,12]{0,1:T(8,128)} %param.15) | copy-start | bytes 144004
  24.9 6.1 %collective-permute-start.5 = (bf16[2,2,128,384]{3,2,1,0:T(8,128)(2,1)S(1)}, bf16[2,2,128,384]{3,2,1,0:T(8,128)(2,1)S(1)}, u32[]{:S(2)}, u32[]{:S(2)}) collective-permute-start(bf16[2,2,128,384]{3,2,1,0:T(8,128)(2,1)S(1)} %stack.21), channel_id=1, source_target_pairs={{0,4},{4,0},{8,12},{12,8},{16,20},{20,16},{24,28},{28,24},{1,5},{5... | collective-permute-start | bytes 1179656 | tf_op jit(solution)/shard_map/ppermute | solution.py:578
  25.0 12.6 %collective-permute-start.8 = (bf16[2,2,128,384]{3,2,1,0:T(8,128)(2,1)S(1)}, bf16[2,2,128,384]{3,2,1,0:T(8,128)(2,1)S(1)}, u32[]{:S(2)}, u32[]{:S(2)}) collective-permute-start(bf16[2,2,128,384]{3,2,1,0:T(8,128)(2,1)S(1)} %stack.23), channel_id=1, source_target_pairs={{0,7},{1,4},{2,5},{3,6},{4,3},{5,0},{6,1},{7,2},{8,15},{9,12},{10,... | collective-permute-start | bytes 1179656 | tf_op jit(solution)/shard_map/ppermute | solution.py:574
  28.8 2.2 %collective-permute-start.4 = (bf16[2,128,384]{2,1,0:T(8,128)(2,1)S(1)}, bf16[2,128,384]{2,1,0:T(8,128)(2,1)S(1)}, u32[]{:S(2)}, u32[]{:S(2)}) collective-permute-start(bf16[2,128,384]{2,1,0:T(8,128)(2,1)S(1)} %stack.20), channel_id=1, source_target_pairs={{0,4},{4,0},{8,12},{12,8},{16,20},{20,16},{24,28},{28,24},{1,5},{5... | collective-permute-start | bytes 589832 | tf_op jit(solution)/shard_map/ppermute | solution.py:578
  28.9 2.0 %collective-permute-start.6 = (bf16[2,128,384]{2,1,0:T(8,128)(2,1)S(1)}, bf16[2,128,384]{2,1,0:T(8,128)(2,1)S(1)}, u32[]{:S(2)}, u32[]{:S(2)}) collective-permute-start(bf16[2,128,384]{2,1,0:T(8,128)(2,1)S(1)} %stack.22), channel_id=1, source_target_pairs={{0,4},{4,0},{8,12},{12,8},{16,20},{20,16},{24,28},{28,24},{1,5},{5... | collective-permute-start | bytes 589832 | tf_op jit(solution)/shard_map/ppermute | solution.py:578
  29.4 7.8 %collective-permute-start.9 = (bf16[2,128,384]{2,1,0:T(8,128)(2,1)S(1)}, bf16[2,128,384]{2,1,0:T(8,128)(2,1)S(1)}, u32[]{:S(2)}, u32[]{:S(2)}) collective-permute-start(bf16[2,128,384]{2,1,0:T(8,128)(2,1)S(1)} %collective-permute-done.7.refs_3_), channel_id=1, source_target_pairs={{0,24},{1,25},{2,26},{3,27},{4,28},{5,29},{6,30},{7,31},{8,16},{9,... | collective-permute-start | bytes 589832 | tf_op jit(solution)/shard_map/ppermute | solution.py:574
  40.4 1.4 %collective-permute-start.10 = (f32[3,8,8,128]{3,2,1,0:T(8,128)S(1)}, f32[3,8,8,128]{3,2,1,0:T(8,128)S(1)}, u32[]{:S(2)}, u32[]{:S(2)}) collective-permute-start(f32[3,8,8,128]{3,2,1,0:T(8,128)S(1)} %get-tuple-element.62.stats), channel_id=1, source_target_pairs={{0,4},{4,0},{8,12},{12,8},{16,20},{20,16},{24,28},{28,24},{1,5},{5... | collective-permute-start | bytes 294920 | tf_op jit(solution)/shard_map/ppermute | solution.py:578
  44.5 16.4 %collective-permute-start.18 = (bf16[3,2,128,384]{3,2,1,0:T(8,128)(2,1)S(1)}, bf16[3,2,128,384]{3,2,1,0:T(8,128)(2,1)S(1)}, u32[]{:S(2)}, u32[]{:S(2)}) collective-permute-start(bf16[3,2,128,384]{3,2,1,0:T(8,128)(2,1)S(1)} %get-tuple-element.86), channel_id=1, source_target_pairs={{0,5},{1,6},{2,7},{3,4},{4,1},{5,2},{6,3},{7,0},{8,13},{9,14},{10,... | collective-permute-start | bytes 1769480 | tf_op jit(solution)/shard_map/ppermute | solution.py:574
  48.1 3.8 %collective-permute-start.11 = (bf16[2,128,384]{2,1,0:T(8,128)(2,1)S(1)}, bf16[2,128,384]{2,1,0:T(8,128)(2,1)S(1)}, u32[]{:S(2)}, u32[]{:S(2)}) collective-permute-start(bf16[2,128,384]{2,1,0:T(8,128)(2,1)S(1)} %get-tuple-element.72), channel_id=1, source_target_pairs={{0,4},{4,0},{8,12},{12,8},{16,20},{20,16},{24,28},{28,24},{1,5},{5... | collective-permute-start | bytes 589832 | tf_op jit(solution)/shard_map/ppermute | solution.py:578
  49.0 2.9 %collective-permute-start.12 = (bf16[2,128,384]{2,1,0:T(8,128)(2,1)S(1)}, bf16[2,128,384]{2,1,0:T(8,128)(2,1)S(1)}, u32[]{:S(2)}, u32[]{:S(2)}) collective-permute-start(bf16[2,128,384]{2,1,0:T(8,128)(2,1)S(1)} %get-tuple-element.74), channel_id=1, source_target_pairs={{0,4},{4,0},{8,12},{12,8},{16,20},{20,16},{24,28},{28,24},{1,5},{5... | collective-permute-start | bytes 589832 | tf_op jit(solution)/shard_map/ppermute | solution.py:578
  49.1 2.8 %collective-permute-start.13 = (bf16[2,128,384]{2,1,0:T(8,128)(2,1)S(1)}, bf16[2,128,384]{2,1,0:T(8,128)(2,1)S(1)}, u32[]{:S(2)}, u32[]{:S(2)}) collective-permute-start(bf16[2,128,384]{2,1,0:T(8,128)(2,1)S(1)} %get-tuple-element.76), channel_id=1, source_target_pairs={{0,4},{4,0},{8,12},{12,8},{16,20},{20,16},{24,28},{28,24},{1,5},{5... | collective-permute-start | bytes 589832 | tf_op jit(solution)/shard_map/ppermute | solution.py:578
  49.5 2.4 %collective-permute-start.14 = (bf16[2,128,384]{2,1,0:T(8,128)(2,1)S(1)}, bf16[2,128,384]{2,1,0:T(8,128)(2,1)S(1)}, u32[]{:S(2)}, u32[]{:S(2)}) collective-permute-start(bf16[2,128,384]{2,1,0:T(8,128)(2,1)S(1)} %get-tuple-element.78), channel_id=1, source_target_pairs={{0,4},{4,0},{8,12},{12,8},{16,20},{20,16},{24,28},{28,24},{1,5},{5... | collective-permute-start | bytes 589832 | tf_op jit(solution)/shard_map/ppermute | solution.py:578
  52.2 9.5 %collective-permute-start.15 = (bf16[2,128,384]{2,1,0:T(8,128)(2,1)S(1)}, bf16[2,128,384]{2,1,0:T(8,128)(2,1)S(1)}, u32[]{:S(2)}, u32[]{:S(2)}) collective-permute-start(bf16[2,128,384]{2,1,0:T(8,128)(2,1)S(1)} %get-tuple-element.80), channel_id=1, source_target_pairs={{0,8},{1,9},{2,10},{3,11},{4,12},{5,13},{6,14},{7,15},{8,0},{9,1},... | collective-permute-start | bytes 589832 | tf_op jit(solution)/shard_map/ppermute | solution.py:574
  52.2 11.7 %collective-permute-start.16 = (bf16[2,128,384]{2,1,0:T(8,128)(2,1)S(1)}, bf16[2,128,384]{2,1,0:T(8,128)(2,1)S(1)}, u32[]{:S(2)}, u32[]{:S(2)}) collective-permute-start(bf16[2,128,384]{2,1,0:T(8,128)(2,1)S(1)} %get-tuple-element.81), channel_id=1, source_target_pairs={{0,16},{1,17},{2,18},{3,19},{4,20},{5,21},{6,22},{7,23},{8,24},{9,... | collective-permute-start | bytes 589832 | tf_op jit(solution)/shard_map/ppermute | solution.py:574
  57.5 8.1 %collective-permute-start.17 = (bf16[2,128,384]{2,1,0:T(8,128)(2,1)S(1)}, bf16[2,128,384]{2,1,0:T(8,128)(2,1)S(1)}, u32[]{:S(2)}, u32[]{:S(2)}) collective-permute-start(bf16[2,128,384]{2,1,0:T(8,128)(2,1)S(1)} %get-tuple-element.82), channel_id=1, source_target_pairs={{0,24},{1,25},{2,26},{3,27},{4,28},{5,29},{6,30},{7,31},{8,16},{9,... | collective-permute-start | bytes 589832 | tf_op jit(solution)/shard_map/ppermute | solution.py:574
  61.0 7.9 %collective-permute-start.19 = (bf16[2,128,384]{2,1,0:T(8,128)(2,1)S(1)}, bf16[2,128,384]{2,1,0:T(8,128)(2,1)S(1)}, u32[]{:S(2)}, u32[]{:S(2)}) collective-permute-start(bf16[2,128,384]{2,1,0:T(8,128)(2,1)S(1)} %get-tuple-element.90), channel_id=1, source_target_pairs={{0,5},{1,6},{2,7},{3,4},{4,1},{5,2},{6,3},{7,0},{8,13},{9,14},{10,... | collective-permute-start | bytes 589832 | tf_op jit(solution)/shard_map/ppermute | solution.py:574
  61.7 7.7 %collective-permute-start.20 = (bf16[2,128,384]{2,1,0:T(8,128)(2,1)S(1)}, bf16[2,128,384]{2,1,0:T(8,128)(2,1)S(1)}, u32[]{:S(2)}, u32[]{:S(2)}) collective-permute-start(bf16[2,128,384]{2,1,0:T(8,128)(2,1)S(1)} %get-tuple-element.91), channel_id=1, source_target_pairs={{0,8},{1,9},{2,10},{3,11},{4,12},{5,13},{6,14},{7,15},{8,0},{9,1},... | collective-permute-start | bytes 589832 | tf_op jit(solution)/shard_map/ppermute | solution.py:574
  61.7 10.8 %collective-permute-start.21 = (bf16[2,128,384]{2,1,0:T(8,128)(2,1)S(1)}, bf16[2,128,384]{2,1,0:T(8,128)(2,1)S(1)}, u32[]{:S(2)}, u32[]{:S(2)}) collective-permute-start(bf16[2,128,384]{2,1,0:T(8,128)(2,1)S(1)} %get-tuple-element.92), channel_id=1, source_target_pairs={{0,16},{1,17},{2,18},{3,19},{4,20},{5,21},{6,22},{7,23},{8,24},{9,... | collective-permute-start | bytes 589832 | tf_op jit(solution)/shard_map/ppermute | solution.py:574
  64.0 10.2 %collective-permute-start.22 = (bf16[2,128,384]{2,1,0:T(8,128)(2,1)S(1)}, bf16[2,128,384]{2,1,0:T(8,128)(2,1)S(1)}, u32[]{:S(2)}, u32[]{:S(2)}) collective-permute-start(bf16[2,128,384]{2,1,0:T(8,128)(2,1)S(1)} %get-tuple-element.93), channel_id=1, source_target_pairs={{0,24},{1,25},{2,26},{3,27},{4,28},{5,29},{6,30},{7,31},{8,16},{9,... | collective-permute-start | bytes 589832 | tf_op jit(solution)/shard_map/ppermute | solution.py:574

commit v4 on v3

--- a/solution.py
+++ b/solution.py
@@ -595,10 +595,10 @@
     packed, (pair, early) = pack(z, pos, (keys, values, queries, grad_out))
     full = [to_shard(packed[hop], hop, 0) for hop in hops]
     far_first, far_last = to_shard(pair, 0, -1), to_shard(early, 0, -1)
-    bias = bias_rows(z, meta, level_bias.T, far_first)
-    direct = stack(full[1:last], 0, (far_first, far_last, bias))
+    bias = bias_rows(z, meta, level_bias.T, full[1])
+    direct = stack(full[1:last], 0, (bias,))
     far = [far_first, to_shard(direct, 0, -1), to_shard(far_last, last, 0)]
-    rows = swapped([stack(full[:1], 2, flat=True), stack(full[1:last], 2, (bias,)), stack(full[last:], 2, flat=True)])
+    rows = swapped([stack(full[:1], 2, flat=True), stack(full[1:last], 2, (bias,)), stack(full[last:], 2, (far_first, far_last), True)])
 
     scalars = [(meta, "scalar")]
     one = shape((2, tok, cols), BF16)

time: 75.6 us -> 76.8 us (1.016)
  waiting for transfers between devices: 24 us -> 26.9 us
  starting transfers between devices: 25.2 us -> 23.1 us
    ppermute x15, waiting for transfers between devices: 22.7 us -> 25.6 us  [to_shard(): return lax.ppermute(x, ('tm', 'tile'), pairs)]
    ppermute x15, starting transfers between devices: 22.9 us -> 21.2 us  [to_shard(): return lax.ppermute(x, ('tm', 'tile'), pairs)]
  transfers between devices with their start and end apart: 23 -> 23, of which waited for: 11 -> 9; matrix products, arithmetic and copies ran while one was open for 1% -> 1% of each run, Pallas kernels for 20% -> 20%
where the time goes in v4:
time: 76.8 us; the launch traced here: 76.6 us
  waiting for transfers between devices  26.9 us (35%)
  Pallas kernels  24 us (31%)
  starting transfers between devices  23.1 us (30%)
  local copies, waits for them, and re-layouts  1.6 us (2%)
  between operations  0.87 us (1%)
    ppermute x15, waiting for transfers between devices, to_shard(): return lax.ppermute(x, ('tm', 'tile'), pairs)  25.6 us
    ppermute x15, starting transfers between devices, to_shard(): return lax.ppermute(x, ('tm', 'tile'), pairs)  21.2 us
    pallas_call x6, Pallas kernels, call(): pl.pallas_call(functools.partial(kernel, self), grid=(self.own_heads // s...  17.8 us
    pallas_call x2, Pallas kernels, unpack(): pl.pallas_call(kernel, out_shape=[jax.ShapeDtypeStruct((tok, cols * shard...  3 us
    pallas_call x1, Pallas kernels, pack(): pl.pallas_call(functools.partial(pack_kernel, z), out_shape=[shape((4, z....  2.1 us
    ppermute x8, starting transfers between devices, to_replica(): return lax.ppermute(x, 'tm', pairs)  1.86 us
  transfers between devices with their start and end apart: 23, of which 9 were waited for; matrix products, arithmetic and copies ran while one was open for 1% of the time, Pallas kernels for 20%

profile of v4, /device:TPU:0, one launch (start us, length us, event | category | flops | bytes accessed | tf_op | source)
XLA Modules:
  0.0 76.6 jit_solution(13405537739614408016)
XLA Ops:
  0.7 2.1 %pack.1 = (bf16[4,128,384]{2,1,0:T(8,128)(2,1)S(1)}, bf16[4,128,384]{2,1,0:T(8,128)(2,1)S(1)}, bf16[4,128,384]{2,1,0:T(8,128)(2,1)S(1)}, bf16[4,128,384]{2,1,0:T...) custom-call(s32[3]{0:T(128)S(1)} %pad_add_fusion.pos_ref, ...), custom_call_target="tpu_custom_call" | custom-call | tf_op jit(solution)/shard_map/pack/pallas_call | solution.py:67
  2.8 3.0 %collective-permute-start = (bf16[4,128,384]{2,1,0:T(8,128)(2,1)S(1)}, bf16[4,128,384]{2,1,0:T(8,128)(2,1)S(1)}, u32[]{:S(2)}, u32[]{:S(2)}) collective-permute-start(bf16[4,128,384]{2,1,0:T(8,128)(2,1)S(1)} %get-tuple-element.50), channel_id=1, source_target_pairs={{0,8},{1,9},{2,10},{3,11},{4,12},{5,13},{6,14},{7,15},{8,0},{9,1},... | collective-permute-start | bytes 1179656 | tf_op jit(solution)/shard_map/ppermute | solution.py:574
  5.8 1.5 %collective-permute-start.1 = (bf16[4,128,384]{2,1,0:T(8,128)(2,1)S(1)}, bf16[4,128,384]{2,1,0:T(8,128)(2,1)S(1)}, u32[]{:S(2)}, u32[]{:S(2)}) collective-permute-start(bf16[4,128,384]{2,1,0:T(8,128)(2,1)S(1)} %get-tuple-element.52), channel_id=1, source_target_pairs={{0,16},{1,17},{2,18},{3,19},{4,20},{5,21},{6,22},{7,23},{8,24},{9,... | collective-permute-start | bytes 1179656 | tf_op jit(solution)/shard_map/ppermute | solution.py:574
  7.4 2.7 %collective-permute-start.5 = (bf16[2,128,384]{2,1,0:T(8,128)(2,1)S(1)}, bf16[2,128,384]{2,1,0:T(8,128)(2,1)S(1)}, u32[]{:S(2)}, u32[]{:S(2)}) collective-permute-start(bf16[2,128,384]{2,1,0:T(8,128)(2,1)S(1)} %get-tuple-element.54), channel_id=1, source_target_pairs={{0,7},{1,4},{2,5},{3,6},{4,3},{5,0},{6,1},{7,2},{8,15},{9,12},{10,... | collective-permute-start | bytes 589832 | tf_op jit(solution)/shard_map/ppermute | solution.py:574
  10.0 1.6 %collective-permute-start.6 = (bf16[2,128,384]{2,1,0:T(8,128)(2,1)S(1)}, bf16[2,128,384]{2,1,0:T(8,128)(2,1)S(1)}, u32[]{:S(2)}, u32[]{:S(2)}) collective-permute-start(bf16[2,128,384]{2,1,0:T(8,128)(2,1)S(1)} %get-tuple-element.55), channel_id=1, source_target_pairs={{0,7},{1,4},{2,5},{3,6},{4,3},{5,0},{6,1},{7,2},{8,15},{9,12},{10,... | collective-permute-start | bytes 589832 | tf_op jit(solution)/shard_map/ppermute | solution.py:574
  12.4 3.4 %collective-permute-done.after_ref.refs_0_.refs_1_ = bf16[4,128,384]{2,1,0:T(8,128)(2,1)S(1)} collective-permute-done((bf16[4,128,384]{2,1,0:T(8,128)(2,1)S(1)}, bf16[4,128,384]{2,1,0:T(8,128)(2,1)S(1)}, u32[]{:S(2)}, u32[]{:S(2)}) %collective-permute-start) | collective-permute-done | bytes 393248 | tf_op jit(solution)/shard_map/ppermute | solution.py:574
  17.3 7.5 %collective-permute-done.1.refs_1_.refs_2_ = bf16[4,128,384]{2,1,0:T(8,128)(2,1)S(1)} collective-permute-done((bf16[4,128,384]{2,1,0:T(8,128)(2,1)S(1)}, bf16[4,128,384]{2,1,0:T(8,128)(2,1)S(1)}, u32[]{:S(2)}, u32[]{:S(2)}) %collective-permute-start.1) | collective-permute-done | bytes 393248 | tf_op jit(solution)/shard_map/ppermute | solution.py:574
  25.0 3.7 %collective-permute-start.8 = (bf16[2,2,128,384]{3,2,1,0:T(8,128)(2,1)S(1)}, bf16[2,2,128,384]{3,2,1,0:T(8,128)(2,1)S(1)}, u32[]{:S(2)}, u32[]{:S(2)}) collective-permute-start(bf16[2,2,128,384]{3,2,1,0:T(8,128)(2,1)S(1)} %stack.23), channel_id=1, source_target_pairs={{0,7},{1,4},{2,5},{3,6},{4,3},{5,0},{6,1},{7,2},{8,15},{9,12},{10,... | collective-permute-start | bytes 1179656 | tf_op jit(solution)/shard_map/ppermute | solution.py:574
  29.5 1.5 %collective-permute-start.9 = (bf16[2,128,384]{2,1,0:T(8,128)(2,1)S(1)}, bf16[2,128,384]{2,1,0:T(8,128)(2,1)S(1)}, u32[]{:S(2)}, u32[]{:S(2)}) collective-permute-start(bf16[2,128,384]{2,1,0:T(8,128)(2,1)S(1)} %collective-permute-done.6.refs_2_), channel_id=1, source_target_pairs={{0,24},{1,25},{2,26},{3,27},{4,28},{5,29},{6,30},{7,31},{8,16},{9,... | collective-permute-start | bytes 589832 | tf_op jit(solution)/shard_map/ppermute | solution.py:574
  31.0 4.8 %own.1 = (bf16[3,128,512]{2,1,0:T(8,128)(2,1)S(1)}, bf16[3,128,512]{2,1,0:T(8,128)(2,1)S(1)}, bf16[3,8,256,256]{3,2,1,0:T(8,128)(2,1)S(1)}, f32[3,8,512,128]{3,2...) custom-call(s32[51]{0:T(128)S(1)} %concatenate.4.meta_ref, ...), custom_call_target="tpu_custom_call" | custom-call | tf_op jit(solution)/shard_map/own/pallas_call | solution.py:204
  35.7 1.5 %collective-permute-done.9.refs_0_ = bf16[2,128,384]{2,1,0:T(8,128)(2,1)S(1)} collective-permute-done((bf16[2,128,384]{2,1,0:T(8,128)(2,1)S(1)}, bf16[2,128,384]{2,1,0:T(8,128)(2,1)S(1)}, u32[]{:S(2)}, u32[]{:S(2)}) %collective-permute-start.9) | collective-permute-done | bytes 196640 | tf_op jit(solution)/shard_map/ppermute | solution.py:574
  37.6 2.6 %ahead.1 = (f32[3,8,8,128]{3,2,1,0:T(8,128)S(1)}, bf16[3,128,512]{2,1,0:T(8,128)(2,1)S(1)}, bf16[3,128,512]{2,1,0:T(8,128)(2,1)S(1)}, f32[3,8,512,128]{3,2,1,0:T(8,128)S(1)}, f32[3,8,512,128]{3,2,1,0:T(8,128)S(1)}) custom-call(s32[51]{0:T(128)S(1)} %concatenate.4.meta_ref, f32[8,12,128]{2,1,0:T(8,128)S(1)} %bias.1.refs_2_, ...), custom_call_target="tpu_custom_call" | custom-call | tf_op jit(solution)/shard_map/ahead/pallas_call | solution.py:204
  41.6 2.6 %back.1 = (f32[3,8,8,128]{3,2,1,0:T(8,128)S(1)}, f32[3,8,128,128]{3,2,1,0:T(8,128)S(1)}, f32[3,8,128,128]{3,2,1,0:T(8,128)S(1)}, bf16[2,128,384]{2,1,0:T(8,128)(2,1)S(1)}, bf16[3,2,128,384]{3,2,1,0:T(8,128)(2,1)S(1)}) custom-call(s32[51]{0:T(128)S(1)} %concatenate.4.meta_ref, bf16[3,8,256,256]{3,2,1,0:T(8,128)(2,1)S(1)} %get-tuple-element.60.both, ...), custom_call_target="tpu_custom_call" | custom-call | tf_op jit(solution)/shard_map/back/pallas_call | solution.py:204
  44.2 2.3 %rows_others.1 = (bf16[2,128,384]{2,1,0:T(8,128)(2,1)S(1)}, bf16[2,128,384]{2,1,0:T(8,128)(2,1)S(1)}, bf16[2,128,384]{2,1,0:T(8,128)(2,1)S(1)}, bf16[2,128,384]{2,1,0:T(8,128)(2,1)S(1)}) custom-call(s32[51]{0:T(128)S(1)} %concatenate.4.meta_ref, bf16[3,128,512]{2,1,0:T(8,128)(2,1)S(1)} %get-tuple-element.56.kt, ...), custom_call_target="tpu_custom_call" | custom-call | tf_op jit(solution)/shard_map/rows_others/pallas_call | solution.py:204
  47.6 2.3 %rows.1 = (bf16[2,128,384]{2,1,0:T(8,128)(2,1)S(1)}, bf16[2,128,384]{2,1,0:T(8,128)(2,1)S(1)}, bf16[2,128,384]{2,1,0:T(8,128)(2,1)S(1)}, bf16[2,128,384]{2,1,0:T(8,128)(2,1)S(1)}) custom-call(s32[51]{0:T(128)S(1)} %concatenate.4.meta_ref, bf16[3,128,512]{2,1,0:T(8,128)(2,1)S(1)} %get-tuple-element.56.kt, bf16[3,128,512]{2,1,0:T(8,128)(2,1)S(1)} %get-tuple-element.57.vt, ...), custom_call_target="tpu_custom_call" | custom-call | tf_op jit(solution)/shard_map/rows/pallas_call | solution.py:204
  50.2 2.0 %collective-permute-start.16 = (bf16[2,128,384]{2,1,0:T(8,128)(2,1)S(1)}, bf16[2,128,384]{2,1,0:T(8,128)(2,1)S(1)}, u32[]{:S(2)}, u32[]{:S(2)}) collective-permute-start(bf16[2,128,384]{2,1,0:T(8,128)(2,1)S(1)} %get-tuple-element.81), channel_id=1, source_target_pairs={{0,16},{1,17},{2,18},{3,19},{4,20},{5,21},{6,22},{7,23},{8,24},{9,... | collective-permute-start | bytes 589832 | tf_op jit(solution)/shard_map/ppermute | solution.py:574
  52.2 3.4 %sums.1 = (bf16[2,128,384]{2,1,0:T(8,128)(2,1)S(1)}, bf16[2,128,384]{2,1,0:T(8,128)(2,1)S(1)}, bf16[2,128,384]{2,1,0:T(8,128)(2,1)S(1)}, bf16[2,128,384]{2,1,0:T(8,128)(2,1)S(1)}) custom-call(s32[51]{0:T(128)S(1)} %concatenate.4.meta_ref, bf16[3,8,256,256]{3,2,1,0:T(8,128)(2,1)S(1)} %get-tuple-element.60.both, ...), custom_call_target="tpu_custom_call" | custom-call | tf_op jit(solution)/shard_map/sums/pallas_call | solution.py:204
  57.0 5.1 %collective-permute-done.18.refs_0_ = bf16[3,2,128,384]{3,2,1,0:T(8,128)(2,1)S(1)} collective-permute-done((bf16[3,2,128,384]{3,2,1,0:T(8,128)(2,1)S(1)}, bf16[3,2,128,384]{3,2,1,0:T(8,128)(2,1)S(1)}, u32[]{:S(2)}, u32[]{:S(2)}) %collective-permute-start.18) | collective-permute-done | bytes 589856 | tf_op jit(solution)/shard_map/ppermute | solution.py:574
  62.4 2.0 %collective-permute-start.21 = (bf16[2,128,384]{2,1,0:T(8,128)(2,1)S(1)}, bf16[2,128,384]{2,1,0:T(8,128)(2,1)S(1)}, u32[]{:S(2)}, u32[]{:S(2)}) collective-permute-start(bf16[2,128,384]{2,1,0:T(8,128)(2,1)S(1)} %get-tuple-element.92), channel_id=1, source_target_pairs={{0,16},{1,17},{2,18},{3,19},{4,20},{5,21},{6,22},{7,23},{8,24},{9,... | collective-permute-start | bytes 589832 | tf_op jit(solution)/shard_map/ppermute | solution.py:574
  65.9 1.5 %unpack.2 = (bf16[128,1536]{1,0:T(8,128)(2,1)}, bf16[128,1536]{1,0:T(8,128)(2,1)}) custom-call(s32[3]{0:T(128)S(1)} %pad_add_fusion.pos_ref, bf16[2,128,384]{2,1,0:T(8,128)(2,1)S(1)} %get-tuple-element.79.refs_0_, bf16[2,128,384]{2,1,0:T(8,128)(2,1)S(1)} %collective-permute-done.15.refs_1_, bf16[2,128,384]{2,1,0:T(8,128)(2,1)S(1)} %collective-permute-done.16.refs_2_, ...), custom_call_target="tpu_custom_call" | custom-call | tf_op jit(solution)/shard_map/unpack/pallas_call | solution.py:540
  67.4 3.1 %collective-permute-done.19.refs_1_ = bf16[2,128,384]{2,1,0:T(8,128)(2,1)S(1)} collective-permute-done((bf16[2,128,384]{2,1,0:T(8,128)(2,1)S(1)}, bf16[2,128,384]{2,1,0:T(8,128)(2,1)S(1)}, u32[]{:S(2)}, u32[]{:S(2)}) %collective-permute-start.19) | collective-permute-done | bytes 196640 | tf_op jit(solution)/shard_map/ppermute | solution.py:574
  70.5 3.0 %collective-permute-done.21.refs_3_ = bf16[2,128,384]{2,1,0:T(8,128)(2,1)S(1)} collective-permute-done((bf16[2,128,384]{2,1,0:T(8,128)(2,1)S(1)}, bf16[2,128,384]{2,1,0:T(8,128)(2,1)S(1)}, u32[]{:S(2)}, u32[]{:S(2)}) %collective-permute-start.21) | collective-permute-done | bytes 196640 | tf_op jit(solution)/shard_map/ppermute | solution.py:574
  73.5 1.6 %collective-permute-done.22.refs_4_ = bf16[2,128,384]{2,1,0:T(8,128)(2,1)S(1)} collective-permute-done((bf16[2,128,384]{2,1,0:T(8,128)(2,1)S(1)}, bf16[2,128,384]{2,1,0:T(8,128)(2,1)S(1)}, u32[]{:S(2)}, u32[]{:S(2)}) %collective-permute-start.22) | collective-permute-done | bytes 196640 | tf_op jit(solution)/shard_map/ppermute | solution.py:574
  75.1 1.5 %unpack.3 = (bf16[128,1536]{1,0:T(8,128)(2,1)}, bf16[128,1536]{1,0:T(8,128)(2,1)}) custom-call(s32[3]{0:T(128)S(1)} %pad_add_fusion.pos_ref, bf16[2,128,384]{2,1,0:T(8,128)(2,1)S(1)} %get-tuple-element.85.refs_0_, bf16[2,128,384]{2,1,0:T(8,128)(2,1)S(1)} %collective-permute-done.19.refs_1_, bf16[2,128,384]{2,1,0:T(8,128)(2,1)S(1)} %collective-permute-done.20.refs_2_, ...), custom_call_target="tpu_custom_call" | custom-call | tf_op jit(solution)/shard_map/unpack/pallas_call | solution.py:540
  (45 shorter events, 9.5 us)
Async XLA Ops:
  2.8 12.9 %collective-permute-start = (bf16[4,128,384]{2,1,0:T(8,128)(2,1)S(1)}, bf16[4,128,384]{2,1,0:T(8,128)(2,1)S(1)}, u32[]{:S(2)}, u32[]{:S(2)}) collective-permute-start(bf16[4,128,384]{2,1,0:T(8,128)(2,1)S(1)} %get-tuple-element.50), channel_id=1, source_target_pairs={{0,8},{1,9},{2,10},{3,11},{4,12},{5,13},{6,14},{7,15},{8,0},{9,1},... | collective-permute-start | bytes 1179656 | tf_op jit(solution)/shard_map/ppermute | solution.py:574
  5.8 19.0 %collective-permute-start.1 = (bf16[4,128,384]{2,1,0:T(8,128)(2,1)S(1)}, bf16[4,128,384]{2,1,0:T(8,128)(2,1)S(1)}, u32[]{:S(2)}, u32[]{:S(2)}) collective-permute-start(bf16[4,128,384]{2,1,0:T(8,128)(2,1)S(1)} %get-tuple-element.52), channel_id=1, source_target_pairs={{0,16},{1,17},{2,18},{3,19},{4,20},{5,21},{6,22},{7,23},{8,24},{9,... | collective-permute-start | bytes 1179656 | tf_op jit(solution)/shard_map/ppermute | solution.py:574
  7.4 21.5 %collective-permute-start.2 = (bf16[4,128,384]{2,1,0:T(8,128)(2,1)S(1)}, bf16[4,128,384]{2,1,0:T(8,128)(2,1)S(1)}, u32[]{:S(2)}, u32[]{:S(2)}) collective-permute-start(bf16[4,128,384]{2,1,0:T(8,128)(2,1)S(1)} %get-tuple-element.53), channel_id=1, source_target_pairs={{0,24},{1,25},{2,26},{3,27},{4,28},{5,29},{6,30},{7,31},{8,16},{9,... | collective-permute-start | bytes 1179656 | tf_op jit(solution)/shard_map/ppermute | solution.py:574
  7.4 21.4 %collective-permute-start.5 = (bf16[2,128,384]{2,1,0:T(8,128)(2,1)S(1)}, bf16[2,128,384]{2,1,0:T(8,128)(2,1)S(1)}, u32[]{:S(2)}, u32[]{:S(2)}) collective-permute-start(bf16[2,128,384]{2,1,0:T(8,128)(2,1)S(1)} %get-tuple-element.54), channel_id=1, source_target_pairs={{0,7},{1,4},{2,5},{3,6},{4,3},{5,0},{6,1},{7,2},{8,15},{9,12},{10,... | collective-permute-start | bytes 589832 | tf_op jit(solution)/shard_map/ppermute | solution.py:574
  10.0 18.8 %collective-permute-start.6 = (bf16[2,128,384]{2,1,0:T(8,128)(2,1)S(1)}, bf16[2,128,384]{2,1,0:T(8,128)(2,1)S(1)}, u32[]{:S(2)}, u32[]{:S(2)}) collective-permute-start(bf16[2,128,384]{2,1,0:T(8,128)(2,1)S(1)} %get-tuple-element.55), channel_id=1, source_target_pairs={{0,7},{1,4},{2,5},{3,6},{4,3},{5,0},{6,1},{7,2},{8,15},{9,12},{10,... | collective-permute-start | bytes 589832 | tf_op jit(solution)/shard_map/ppermute | solution.py:574
  15.8 0.8 %copy-start = (f32[1000,12]{0,1:T(8,128)S(1)}, f32[1000,12]{0,1:T(8,128)}, u32[]{:S(2)}) copy-start(f32[1000,12]{0,1:T(8,128)} %param.15) | copy-start | bytes 144004
  24.9 6.1 %collective-permute-start.4 = (bf16[2,2,128,384]{3,2,1,0:T(8,128)(2,1)S(1)}, bf16[2,2,128,384]{3,2,1,0:T(8,128)(2,1)S(1)}, u32[]{:S(2)}, u32[]{:S(2)}) collective-permute-start(bf16[2,2,128,384]{3,2,1,0:T(8,128)(2,1)S(1)} %stack.21), channel_id=1, source_target_pairs={{0,4},{4,0},{8,12},{12,8},{16,20},{20,16},{24,28},{28,24},{1,5},{5... | collective-permute-start | bytes 1179656 | tf_op jit(solution)/shard_map/ppermute | solution.py:578
  25.0 12.6 %collective-permute-start.8 = (bf16[2,2,128,384]{3,2,1,0:T(8,128)(2,1)S(1)}, bf16[2,2,128,384]{3,2,1,0:T(8,128)(2,1)S(1)}, u32[]{:S(2)}, u32[]{:S(2)}) collective-permute-start(bf16[2,2,128,384]{3,2,1,0:T(8,128)(2,1)S(1)} %stack.23), channel_id=1, source_target_pairs={{0,7},{1,4},{2,5},{3,6},{4,3},{5,0},{6,1},{7,2},{8,15},{9,12},{10,... | collective-permute-start | bytes 1179656 | tf_op jit(solution)/shard_map/ppermute | solution.py:574
  28.8 2.2 %collective-permute-start.3 = (bf16[2,128,384]{2,1,0:T(8,128)(2,1)S(1)}, bf16[2,128,384]{2,1,0:T(8,128)(2,1)S(1)}, u32[]{:S(2)}, u32[]{:S(2)}) collective-permute-start(bf16[2,128,384]{2,1,0:T(8,128)(2,1)S(1)} %stack.20), channel_id=1, source_target_pairs={{0,4},{4,0},{8,12},{12,8},{16,20},{20,16},{24,28},{28,24},{1,5},{5... | collective-permute-start | bytes 589832 | tf_op jit(solution)/shard_map/ppermute | solution.py:578
  28.9 2.0 %collective-permute-start.7 = (bf16[2,128,384]{2,1,0:T(8,128)(2,1)S(1)}, bf16[2,128,384]{2,1,0:T(8,128)(2,1)S(1)}, u32[]{:S(2)}, u32[]{:S(2)}) collective-permute-start(bf16[2,128,384]{2,1,0:T(8,128)(2,1)S(1)} %stack.22), channel_id=1, source_target_pairs={{0,4},{4,0},{8,12},{12,8},{16,20},{20,16},{24,28},{28,24},{1,5},{5... | collective-permute-start | bytes 589832 | tf_op jit(solution)/shard_map/ppermute | solution.py:578
  29.5 7.8 %collective-permute-start.9 = (bf16[2,128,384]{2,1,0:T(8,128)(2,1)S(1)}, bf16[2,128,384]{2,1,0:T(8,128)(2,1)S(1)}, u32[]{:S(2)}, u32[]{:S(2)}) collective-permute-start(bf16[2,128,384]{2,1,0:T(8,128)(2,1)S(1)} %collective-permute-done.6.refs_2_), channel_id=1, source_target_pairs={{0,24},{1,25},{2,26},{3,27},{4,28},{5,29},{6,30},{7,31},{8,16},{9,... | collective-permute-start | bytes 589832 | tf_op jit(solution)/shard_map/ppermute | solution.py:574
  40.2 1.4 %collective-permute-start.10 = (f32[3,8,8,128]{3,2,1,0:T(8,128)S(1)}, f32[3,8,8,128]{3,2,1,0:T(8,128)S(1)}, u32[]{:S(2)}, u32[]{:S(2)}) collective-permute-start(f32[3,8,8,128]{3,2,1,0:T(8,128)S(1)} %get-tuple-element.62.stats), channel_id=1, source_target_pairs={{0,4},{4,0},{8,12},{12,8},{16,20},{20,16},{24,28},{28,24},{1,5},{5... | collective-permute-start | bytes 294920 | tf_op jit(solution)/shard_map/ppermute | solution.py:578
  44.1 18.0 %collective-permute-start.18 = (bf16[3,2,128,384]{3,2,1,0:T(8,128)(2,1)S(1)}, bf16[3,2,128,384]{3,2,1,0:T(8,128)(2,1)S(1)}, u32[]{:S(2)}, u32[]{:S(2)}) collective-permute-start(bf16[3,2,128,384]{3,2,1,0:T(8,128)(2,1)S(1)} %get-tuple-element.86), channel_id=1, source_target_pairs={{0,5},{1,6},{2,7},{3,4},{4,1},{5,2},{6,3},{7,0},{8,13},{9,14},{10,... | collective-permute-start | bytes 1769480 | tf_op jit(solution)/shard_map/ppermute | solution.py:574
  46.5 3.4 %collective-permute-start.11 = (bf16[2,128,384]{2,1,0:T(8,128)(2,1)S(1)}, bf16[2,128,384]{2,1,0:T(8,128)(2,1)S(1)}, u32[]{:S(2)}, u32[]{:S(2)}) collective-permute-start(bf16[2,128,384]{2,1,0:T(8,128)(2,1)S(1)} %get-tuple-element.72), channel_id=1, source_target_pairs={{0,4},{4,0},{8,12},{12,8},{16,20},{20,16},{24,28},{28,24},{1,5},{5... | collective-permute-start | bytes 589832 | tf_op jit(solution)/shard_map/ppermute | solution.py:578
  46.6 3.3 %collective-permute-start.12 = (bf16[2,128,384]{2,1,0:T(8,128)(2,1)S(1)}, bf16[2,128,384]{2,1,0:T(8,128)(2,1)S(1)}, u32[]{:S(2)}, u32[]{:S(2)}) collective-permute-start(bf16[2,128,384]{2,1,0:T(8,128)(2,1)S(1)} %get-tuple-element.74), channel_id=1, source_target_pairs={{0,4},{4,0},{8,12},{12,8},{16,20},{20,16},{24,28},{28,24},{1,5},{5... | collective-permute-start | bytes 589832 | tf_op jit(solution)/shard_map/ppermute | solution.py:578
  47.1 2.8 %collective-permute-start.13 = (bf16[2,128,384]{2,1,0:T(8,128)(2,1)S(1)}, bf16[2,128,384]{2,1,0:T(8,128)(2,1)S(1)}, u32[]{:S(2)}, u32[]{:S(2)}) collective-permute-start(bf16[2,128,384]{2,1,0:T(8,128)(2,1)S(1)} %get-tuple-element.76), channel_id=1, source_target_pairs={{0,4},{4,0},{8,12},{12,8},{16,20},{20,16},{24,28},{28,24},{1,5},{5... | collective-permute-start | bytes 589832 | tf_op jit(solution)/shard_map/ppermute | solution.py:578
  47.1 2.7 %collective-permute-start.14 = (bf16[2,128,384]{2,1,0:T(8,128)(2,1)S(1)}, bf16[2,128,384]{2,1,0:T(8,128)(2,1)S(1)}, u32[]{:S(2)}, u32[]{:S(2)}) collective-permute-start(bf16[2,128,384]{2,1,0:T(8,128)(2,1)S(1)} %get-tuple-element.78), channel_id=1, source_target_pairs={{0,4},{4,0},{8,12},{12,8},{16,20},{20,16},{24,28},{28,24},{1,5},{5... | collective-permute-start | bytes 589832 | tf_op jit(solution)/shard_map/ppermute | solution.py:578
  50.1 12.4 %collective-permute-start.15 = (bf16[2,128,384]{2,1,0:T(8,128)(2,1)S(1)}, bf16[2,128,384]{2,1,0:T(8,128)(2,1)S(1)}, u32[]{:S(2)}, u32[]{:S(2)}) collective-permute-start(bf16[2,128,384]{2,1,0:T(8,128)(2,1)S(1)} %get-tuple-element.80), channel_id=1, source_target_pairs={{0,8},{1,9},{2,10},{3,11},{4,12},{5,13},{6,14},{7,15},{8,0},{9,1},... | collective-permute-start | bytes 589832 | tf_op jit(solution)/shard_map/ppermute | solution.py:574
  50.2 14.3 %collective-permute-start.16 = (bf16[2,128,384]{2,1,0:T(8,128)(2,1)S(1)}, bf16[2,128,384]{2,1,0:T(8,128)(2,1)S(1)}, u32[]{:S(2)}, u32[]{:S(2)}) collective-permute-start(bf16[2,128,384]{2,1,0:T(8,128)(2,1)S(1)} %get-tuple-element.81), channel_id=1, source_target_pairs={{0,16},{1,17},{2,18},{3,19},{4,20},{5,21},{6,22},{7,23},{8,24},{9,... | collective-permute-start | bytes 589832 | tf_op jit(solution)/shard_map/ppermute | solution.py:574
  55.6 10.3 %collective-permute-start.17 = (bf16[2,128,384]{2,1,0:T(8,128)(2,1)S(1)}, bf16[2,128,384]{2,1,0:T(8,128)(2,1)S(1)}, u32[]{:S(2)}, u32[]{:S(2)}) collective-permute-start(bf16[2,128,384]{2,1,0:T(8,128)(2,1)S(1)} %get-tuple-element.82), channel_id=1, source_target_pairs={{0,24},{1,25},{2,26},{3,27},{4,28},{5,29},{6,30},{7,31},{8,16},{9,... | collective-permute-start | bytes 589832 | tf_op jit(solution)/shard_map/ppermute | solution.py:574
  62.3 8.2 %collective-permute-start.19 = (bf16[2,128,384]{2,1,0:T(8,128)(2,1)S(1)}, bf16[2,128,384]{2,1,0:T(8,128)(2,1)S(1)}, u32[]{:S(2)}, u32[]{:S(2)}) collective-permute-start(bf16[2,128,384]{2,1,0:T(8,128)(2,1)S(1)} %get-tuple-element.90), channel_id=1, source_target_pairs={{0,5},{1,6},{2,7},{3,4},{4,1},{5,2},{6,3},{7,0},{8,13},{9,14},{10,... | collective-permute-start | bytes 589832 | tf_op jit(solution)/shard_map/ppermute | solution.py:574
  62.4 8.1 %collective-permute-start.20 = (bf16[2,128,384]{2,1,0:T(8,128)(2,1)S(1)}, bf16[2,128,384]{2,1,0:T(8,128)(2,1)S(1)}, u32[]{:S(2)}, u32[]{:S(2)}) collective-permute-start(bf16[2,128,384]{2,1,0:T(8,128)(2,1)S(1)} %get-tuple-element.91), channel_id=1, source_target_pairs={{0,8},{1,9},{2,10},{3,11},{4,12},{5,13},{6,14},{7,15},{8,0},{9,1},... | collective-permute-start | bytes 589832 | tf_op jit(solution)/shard_map/ppermute | solution.py:574
  62.4 11.0 %collective-permute-start.21 = (bf16[2,128,384]{2,1,0:T(8,128)(2,1)S(1)}, bf16[2,128,384]{2,1,0:T(8,128)(2,1)S(1)}, u32[]{:S(2)}, u32[]{:S(2)}) collective-permute-start(bf16[2,128,384]{2,1,0:T(8,128)(2,1)S(1)} %get-tuple-element.92), channel_id=1, source_target_pairs={{0,16},{1,17},{2,18},{3,19},{4,20},{5,21},{6,22},{7,23},{8,24},{9,... | collective-permute-start | bytes 589832 | tf_op jit(solution)/shard_map/ppermute | solution.py:574
  64.5 10.6 %collective-permute-start.22 = (bf16[2,128,384]{2,1,0:T(8,128)(2,1)S(1)}, bf16[2,128,384]{2,1,0:T(8,128)(2,1)S(1)}, u32[]{:S(2)}, u32[]{:S(2)}) collective-permute-start(bf16[2,128,384]{2,1,0:T(8,128)(2,1)S(1)} %get-tuple-element.93), channel_id=1, source_target_pairs={{0,24},{1,25},{2,26},{3,27},{4,28},{5,29},{6,30},{7,31},{8,16},{9,... | collective-permute-start | bytes 589832 | tf_op jit(solution)/shard_map/ppermute | solution.py:574
